TPU v7x, 128 devices: a whole 4x4x4 slice. The times are simulated.
128 devices in a mesh: ctx: 16 (over x, y), fsdp: 8 (over z, core).
Axes of the slice: x: 4, y: 4, z: 4, core: 2. Of those that a mesh axis runs over, the one named last changes fastest.
Arguments:
- inputs: bfloat16 [16, 1024, 1024], P('fsdp', 'ctx'), may hold values from -6 to 6
- gain_attn: bfloat16 [1024], P('fsdp'), may hold values from 0.5 to 1.5
- w_query: bfloat16 [1024, 1024], P('fsdp'), may hold values from -0.1875 to 0.1875
- w_key: bfloat16 [1024, 1024], P('fsdp'), may hold values from -0.1875 to 0.1875
- w_value: bfloat16 [1024, 1024], P('fsdp'), may hold values from -0.1875 to 0.1875
- w_out: bfloat16 [1024, 1024], P('fsdp'), may hold values from -1.5 to 1.5
- persist_key: bfloat16 [16, 1024], P(None, 'fsdp'), may hold values from -6 to 6
- persist_value: bfloat16 [16, 1024], P(None, 'fsdp'), may hold values from -6 to 6
- gain_ffn: bfloat16 [1024], P('fsdp'), may hold values from 0.5 to 1.5
- w_gate: bfloat16 [1024, 2816], P('fsdp'), may hold values from -0.1875 to 0.1875
- w_up: bfloat16 [1024, 2816], P('fsdp'), may hold values from -0.1875 to 0.1875
- w_down: bfloat16 [2816, 1024], P('fsdp'), may hold values from -0.109375 to 0.109375
- decay_table: bfloat16 [16, 8], P('fsdp'), may hold values from -1 to 7
- momentum_table: bfloat16 [16, 8], P('fsdp'), may hold values from -2 to 3
- lengths: int32 [16], P('fsdp'), may hold values from 256 to 1024, as said below
- decay_index: int32 [16, 16], P('fsdp', 'ctx'), may hold values from 0 to 15
- momentum_index: int32 [16, 16], P('fsdp', 'ctx'), may hold values from 0 to 15
- cotangent: bfloat16 [16, 1024, 1024], P('fsdp', 'ctx'), may hold values from -6 to 6
Outputs:
- output: bfloat16 [16, 1024, 1024], P('fsdp', 'ctx')
- input_grad: float32 [16, 1024, 1024], P('fsdp', 'ctx')
- grad_gain_attn: float32 [1024], P('fsdp')
- grad_query: float32 [1024, 1024], P('fsdp')
- grad_key: float32 [1024, 1024], P('fsdp')
- grad_value: float32 [1024, 1024], P('fsdp')
- grad_out: float32 [1024, 1024], P('fsdp')
- grad_persist_key: float32 [16, 1024], P(None, 'fsdp')
- grad_persist_value: float32 [16, 1024], P(None, 'fsdp')
- grad_gain_ffn: float32 [1024], P('fsdp')
- grad_gate: float32 [1024, 2816], P('fsdp')
- grad_up: float32 [1024, 2816], P('fsdp')
- grad_down: float32 [2816, 1024], P('fsdp')
- grad_decay_table: float32 [16, 8], P('fsdp')
- grad_momentum_table: float32 [16, 8], P('fsdp')
Inputs may be any that keep to these rules, and one draw needn't show every extreme that they name: `lengths`: among the 2 sequences of each index of fsdp, one has exactly 1024 live positions.
All inputs are finite; a program needn't handle non-finite values.
Results may differ from a plain program's by a relative error of at most 0.025.
Values may be sent and summed in bfloat16 or wider, within the bound.
A program may use at most 192 MiB of HBM per device.

v0:
```python
import jax
import jax.numpy as jnp
from jax import lax
from jax.sharding import PartitionSpec as P

H = 8
DH = 128
PERS = 16
SEG = 1024
BLOCK = 64
LEVELS = 16


step_rate = 0.1
highest = lax.Precision.HIGHEST


def from_behind(value, axis, steps):
    count = lax.axis_size(axis)
    first, last = (max(0, -steps), min(count, count - steps))
    return lax.ppermute(value, axis, [(source, source + steps) for source in range(first, last)])


def scaled_rows(values, gain_row):
    return values * lax.rsqrt(jnp.mean(values * values, axis=-1, keepdims=True) + 1e-06) * gain_row


def unit_heads(values):
    return (
        values
        * lax.rsqrt(jnp.mean(values * values, axis=-1, keepdims=True) + 1e-06)
        * values.shape[-1] ** (-0.5)
    )


def batched(pattern, left_side, right_side):
    return jnp.einsum(pattern, left_side, right_side, precision=highest)


def affine(linear, offset, state_in):
    return batched("shij,shjk->shik", linear, state_in) + offset


def forward_step(memory, velocity, outer_keys, outer_values, retention, momentum):
    surprise = batched("shkj,shjl->shkl", outer_keys, memory)
    if outer_values is not None:
        surprise = surprise - outer_values
    velocity = momentum * velocity - step_rate * surprise
    return (retention * memory + velocity, velocity)


def backward_step(adj_memory, adj_velocity, outer_keys, retention, momentum):
    total_adj = adj_memory + adj_velocity
    return (
        retention * adj_memory - step_rate * batched("shkj,shjl->shkl", outer_keys, total_adj),
        momentum * total_adj,
    )


def per_block(rates, block_index):
    return rates[:, block_index][:, :, None, None]


def shards(
    inputs,
    gain_attn,
    w_query,
    w_key,
    w_value,
    w_out,
    persist_key,
    persist_value,
    gain_ffn,
    w_gate,
    w_up,
    w_down,
    decay_table,
    momentum_table,
    lengths,
    decay_index,
    momentum_index,
    cotangent,
):
    (
        full_gain_attn,
        full_query,
        full_key,
        full_value,
        full_out,
        full_pkey,
        full_pvalue,
        full_gain_ffn,
        full_gate,
        full_up,
        full_down,
        full_decay,
        full_momentum,
    ) = (
        lax.all_gather(gain_attn, "fsdp", axis=0, tiled=True),
        lax.all_gather(w_query, "fsdp", axis=0, tiled=True),
        lax.all_gather(w_key, "fsdp", axis=0, tiled=True),
        lax.all_gather(w_value, "fsdp", axis=0, tiled=True),
        lax.all_gather(w_out, "fsdp", axis=0, tiled=True),
        lax.all_gather(persist_key, "fsdp", axis=1, tiled=True),
        lax.all_gather(persist_value, "fsdp", axis=1, tiled=True),
        lax.all_gather(gain_ffn, "fsdp", axis=0, tiled=True),
        lax.all_gather(w_gate, "fsdp", axis=0, tiled=True),
        lax.all_gather(w_up, "fsdp", axis=0, tiled=True),
        lax.all_gather(w_down, "fsdp", axis=0, tiled=True),
        lax.all_gather(decay_table, "fsdp", axis=0, tiled=True),
        lax.all_gather(momentum_table, "fsdp", axis=0, tiled=True),
    )
    seq_count, positions, model_width = inputs.shape
    ctx_count = lax.axis_size("ctx")
    fsdp_count = lax.axis_size("fsdp")
    score_scale = DH ** (-0.5)
    query_pos = lax.axis_index("ctx") * positions + jnp.arange(positions)
    live_rows = (query_pos[None, :] < lengths[:, None]).astype(jnp.float32)
    inputs_f32 = inputs.astype(jnp.float32)
    gain_one = full_gain_attn.astype(jnp.float32)
    normed = scaled_rows(inputs_f32, gain_one).astype(jnp.bfloat16)
    queries = jnp.dot(normed, full_query, preferred_element_type=jnp.float32).astype(jnp.bfloat16)
    key_rows = jnp.dot(normed, full_key, preferred_element_type=jnp.float32).astype(jnp.bfloat16)
    values = jnp.dot(normed, full_value, preferred_element_type=jnp.float32).astype(jnp.bfloat16)
    ctx_keys, ctx_values = (
        lax.all_gather(key_rows, "ctx", axis=1, tiled=True),
        lax.all_gather(values, "ctx", axis=1, tiled=True),
    )
    key_count = ctx_keys.shape[1]
    query_heads = queries.reshape(seq_count, positions, H, DH)
    key_heads = ctx_keys.reshape(seq_count, key_count, H, DH)
    value_heads = ctx_values.reshape(seq_count, key_count, H, DH)
    pkey_heads = full_pkey.reshape(PERS, H, DH)
    pvalue_heads = full_pvalue.reshape(PERS, H, DH)
    ctx_scores = (
        jnp.einsum("sqhd,skhd->shqk", query_heads, key_heads, preferred_element_type=jnp.float32)
        * score_scale
    )
    own_scores = (
        jnp.einsum("sqhd,khd->shqk", query_heads, pkey_heads, preferred_element_type=jnp.float32)
        * score_scale
    )
    key_pos = jnp.arange(key_count)
    allowed = (key_pos[None, :] <= query_pos[:, None]) & (
        key_pos[None, :] // SEG == query_pos[:, None] // SEG
    )
    allowed = allowed[None, None] & (key_pos[None, None, None, :] < lengths[:, None, None, None])
    ctx_scores = jnp.where(allowed, ctx_scores, -1e30)
    row_max = jnp.maximum(
        jnp.max(ctx_scores, axis=-1, keepdims=True), jnp.max(own_scores, axis=-1, keepdims=True)
    )
    ctx_exp = jnp.exp(ctx_scores - row_max)
    own_exp = jnp.exp(own_scores - row_max)
    denominator = jnp.sum(ctx_exp, axis=-1, keepdims=True) + jnp.sum(
        own_exp, axis=-1, keepdims=True
    )
    ctx_probs = ctx_exp / denominator
    own_probs = own_exp / denominator
    ctx_low = ctx_probs.astype(jnp.bfloat16)
    own_low = own_probs.astype(jnp.bfloat16)
    attended = jnp.einsum(
        "shqk,skhd->sqhd", ctx_low, value_heads, preferred_element_type=jnp.float32
    ) + jnp.einsum("shqk,khd->sqhd", own_low, pvalue_heads, preferred_element_type=jnp.float32)
    block_count = positions // BLOCK
    query_units, query_pull = jax.vjp(unit_heads, query_heads.astype(jnp.float32))
    key_units, key_pull = jax.vjp(
        unit_heads, key_rows.reshape(seq_count, positions, H, DH).astype(jnp.float32)
    )
    key_live = key_units * live_rows[:, :, None, None]
    value_f32 = values.reshape(seq_count, positions, H, DH).astype(jnp.float32)

    def blocks(array):
        return array.reshape(seq_count, block_count, BLOCK, H, DH)

    query_blocks = blocks(query_units)
    key_blocks = blocks(key_live)
    value_blocks = blocks(value_f32)
    outer_keys = batched("scthk,scthl->schkl", key_blocks, key_blocks)
    outer_values = batched("scthk,scthl->schkl", key_blocks, value_blocks)
    levels = jnp.arange(LEVELS)
    decay_pick = (decay_index[:, :, None] == levels).astype(jnp.float32)
    momentum_pick = (momentum_index[:, :, None] == levels).astype(jnp.float32)
    retention = jax.nn.sigmoid(batched("scl,lh->sch", decay_pick, full_decay.astype(jnp.float32)))
    momentum = jax.nn.sigmoid(
        batched("scl,lh->sch", momentum_pick, full_momentum.astype(jnp.float32))
    )
    square = jnp.zeros((seq_count, H, DH, DH), jnp.float32)
    eye_half = jnp.eye(DH, dtype=jnp.float32)
    zero_half = jnp.zeros((DH, DH), jnp.float32)
    upper_eye = jnp.broadcast_to(
        jnp.concatenate([eye_half, zero_half], 1), (seq_count, H, DH, 2 * DH)
    )
    lower_eye = jnp.broadcast_to(
        jnp.concatenate([zero_half, eye_half], 1), (seq_count, H, DH, 2 * DH)
    )
    lin_memory, lin_velocity = (upper_eye, lower_eye)
    off_memory, off_velocity = (square, square)
    block_index = 0
    lin_memory, lin_velocity = forward_step(
        lin_memory,
        lin_velocity,
        outer_keys[:, block_index],
        None,
        per_block(retention, block_index),
        per_block(momentum, block_index),
    )
    off_memory, off_velocity = forward_step(
        off_memory,
        off_velocity,
        outer_keys[:, block_index],
        outer_values[:, block_index],
        per_block(retention, block_index),
        per_block(momentum, block_index),
    )
    local_map = jnp.concatenate([lin_memory, lin_velocity], 2)
    local_offset = jnp.concatenate([off_memory, off_velocity], 2)
    empty_state = jnp.zeros_like(local_offset)

    def relay_state(step_index, incoming):
        return from_behind(
            affine(local_map, local_offset, incoming).astype(jnp.bfloat16), "ctx", 1
        ).astype(jnp.float32)

    entering = lax.fori_loop(0, ctx_count - 1, relay_state, empty_state)
    memory = entering[:, :, :DH]
    velocity = entering[:, :, DH:]
    block_index = 0
    before = [(memory, velocity)]
    read_list = [batched("sthk,shkl->sthl", query_blocks[:, block_index], memory)]
    memory, velocity = forward_step(
        memory,
        velocity,
        outer_keys[:, block_index],
        outer_values[:, block_index],
        per_block(retention, block_index),
        per_block(momentum, block_index),
    )
    read_rows = jnp.stack(read_list, 1).reshape(seq_count, positions, H, DH)
    mixed = (attended + read_rows).reshape(seq_count, positions, model_width).astype(jnp.bfloat16)
    branch = jnp.dot(mixed, full_out, preferred_element_type=jnp.float32)
    resid = inputs_f32 + branch
    gain_two = full_gain_ffn.astype(jnp.float32)
    normed_ffn = scaled_rows(resid, gain_two).astype(jnp.bfloat16)
    gate_proj = jnp.dot(normed_ffn, full_gate, preferred_element_type=jnp.float32)
    up_proj = jnp.dot(normed_ffn, full_up, preferred_element_type=jnp.float32)
    gate_sigmoid = jax.nn.sigmoid(gate_proj)
    hidden = (gate_proj * gate_sigmoid * up_proj).astype(jnp.bfloat16)
    output = (resid + jnp.dot(hidden, full_down, preferred_element_type=jnp.float32)).astype(
        jnp.bfloat16
    )
    out_grad = cotangent.astype(jnp.float32) * live_rows[:, :, None]
    out_low = out_grad.astype(jnp.bfloat16)
    grad_down = jnp.einsum("stf,std->fd", hidden, out_low, preferred_element_type=jnp.float32)
    d_hidden = jnp.einsum("std,fd->stf", out_low, full_down, preferred_element_type=jnp.float32)
    d_gate = (d_hidden * up_proj * gate_sigmoid * (1.0 + gate_proj * (1.0 - gate_sigmoid))).astype(
        jnp.bfloat16
    )
    d_up = (d_hidden * gate_proj * gate_sigmoid).astype(jnp.bfloat16)
    grad_gate = jnp.einsum("std,stf->df", normed_ffn, d_gate, preferred_element_type=jnp.float32)
    grad_up = jnp.einsum("std,stf->df", normed_ffn, d_up, preferred_element_type=jnp.float32)
    d_normed_ffn = jnp.einsum(
        "stf,df->std", d_gate, full_gate, preferred_element_type=jnp.float32
    ) + jnp.einsum("stf,df->std", d_up, full_up, preferred_element_type=jnp.float32)
    _, ffn_pull = jax.vjp(scaled_rows, resid, gain_two)
    d_resid_part, grad_gain_ffn = ffn_pull(d_normed_ffn)
    d_resid = out_grad + d_resid_part
    d_branch = d_resid.astype(jnp.bfloat16)
    grad_out = jnp.einsum("sti,sto->io", mixed, d_branch, preferred_element_type=jnp.float32)
    d_mixed = jnp.einsum("sto,io->sti", d_branch, full_out, preferred_element_type=jnp.float32)
    d_attended = d_mixed.astype(jnp.bfloat16).reshape(seq_count, positions, H, DH)
    d_reads = d_mixed.reshape(seq_count, positions, H, DH)
    ctx_dprobs = jnp.einsum(
        "sqhd,skhd->shqk", d_attended, value_heads, preferred_element_type=jnp.float32
    )
    own_dprobs = jnp.einsum(
        "sqhd,khd->shqk", d_attended, pvalue_heads, preferred_element_type=jnp.float32
    )
    row_delta = jnp.sum(ctx_probs * ctx_dprobs, axis=-1, keepdims=True) + jnp.sum(
        own_probs * own_dprobs, axis=-1, keepdims=True
    )
    ctx_dscores = (ctx_probs * (ctx_dprobs - row_delta)).astype(jnp.bfloat16)
    own_dscores = (own_probs * (own_dprobs - row_delta)).astype(jnp.bfloat16)
    d_query_att = (
        jnp.einsum("shqk,skhd->sqhd", ctx_dscores, key_heads, preferred_element_type=jnp.float32)
        + jnp.einsum("shqk,khd->sqhd", own_dscores, pkey_heads, preferred_element_type=jnp.float32)
    ) * score_scale
    grad_pkey = (
        jnp.einsum("shqk,sqhd->khd", own_dscores, query_heads, preferred_element_type=jnp.float32)
        * score_scale
    )
    grad_pvalue = jnp.einsum(
        "shqk,sqhd->khd", own_low, d_attended, preferred_element_type=jnp.float32
    )
    key_part = (
        jnp.einsum("shqk,sqhd->kshd", ctx_dscores, query_heads, preferred_element_type=jnp.float32)
        * score_scale
    )
    value_part = jnp.einsum(
        "shqk,sqhd->kshd", ctx_low, d_attended, preferred_element_type=jnp.float32
    )
    kv_terms = lax.psum_scatter(
        jnp.stack([key_part, value_part], 2)
        .reshape(positions * lax.axis_size("ctx"), seq_count, 2, model_width)
        .astype(jnp.bfloat16),
        "ctx",
        scatter_dimension=0,
        tiled=True,
    ).astype(jnp.float32)
    d_key_att = jnp.swapaxes(kv_terms[:, :, 0], 0, 1).reshape(seq_count, positions, H, DH)
    d_value_att = jnp.swapaxes(kv_terms[:, :, 1], 0, 1).reshape(seq_count, positions, H, DH)
    read_blocks = blocks(d_reads)
    read_terms = [batched("sthk,sthl->shkl", query_blocks[:, 0], read_blocks[:, 0])]
    back_memory, back_velocity = (upper_eye, lower_eye)
    rest_memory, rest_velocity = (square, square)
    for block_index in reversed(range(block_count)):
        back_memory, back_velocity = backward_step(
            back_memory,
            back_velocity,
            outer_keys[:, block_index],
            per_block(retention, block_index),
            per_block(momentum, block_index),
        )
        rest_memory, rest_velocity = backward_step(
            rest_memory,
            rest_velocity,
            outer_keys[:, block_index],
            per_block(retention, block_index),
            per_block(momentum, block_index),
        )
        rest_memory = rest_memory + read_terms[block_index]
    back_map = jnp.concatenate([back_memory, back_velocity], 2)
    back_offset = jnp.concatenate([rest_memory, rest_velocity], 2)

    def relay_adjoint(step_index, incoming):
        return from_behind(
            affine(back_map, back_offset, incoming).astype(jnp.bfloat16), "ctx", -1
        ).astype(jnp.float32)

    leaving = lax.fori_loop(0, ctx_count - 1, relay_adjoint, empty_state)
    adj_memory = leaving[:, :, :DH]
    adj_velocity = leaving[:, :, DH:]
    retention_grads = [None] * block_count
    momentum_grads = [None] * block_count
    query_unit_grads = [None] * block_count
    key_unit_grads = [None] * block_count
    value_mem_grads = [None] * block_count
    for block_index in reversed(range(block_count)):
        memory, velocity = before[block_index]
        total_adj = adj_memory + adj_velocity
        d_surprise = -step_rate * total_adj
        d_outer_keys = batched("shkl,shjl->shkj", d_surprise, memory)
        d_outer_values = -d_surprise
        retention_grads[block_index] = jnp.sum(adj_memory * memory, axis=(2, 3))
        momentum_grads[block_index] = jnp.sum(total_adj * velocity, axis=(2, 3))
        query_unit_grads[block_index] = batched(
            "sthl,shkl->sthk", read_blocks[:, block_index], memory
        )
        symmetric = d_outer_keys + jnp.swapaxes(d_outer_keys, 2, 3)
        key_unit_grads[block_index] = batched(
            "sthl,shjl->sthj", key_blocks[:, block_index], symmetric
        ) + batched("sthl,shkl->sthk", value_blocks[:, block_index], d_outer_values)
        value_mem_grads[block_index] = batched(
            "sthk,shkl->sthl", key_blocks[:, block_index], d_outer_values
        )
        adj_memory, adj_velocity = backward_step(
            adj_memory,
            adj_velocity,
            outer_keys[:, block_index],
            per_block(retention, block_index),
            per_block(momentum, block_index),
        )
        adj_memory = adj_memory + read_terms[block_index]
    retention_logit = jnp.stack(retention_grads, 1) * retention * (1.0 - retention)
    momentum_logit = jnp.stack(momentum_grads, 1) * momentum * (1.0 - momentum)
    grad_decay = batched("scl,sch->lh", decay_pick, retention_logit)
    grad_momentum = batched("scl,sch->lh", momentum_pick, momentum_logit)
    d_query_mem = query_pull(jnp.stack(query_unit_grads, 1).reshape(seq_count, positions, H, DH))[0]
    d_key_mem = key_pull(
        jnp.stack(key_unit_grads, 1).reshape(seq_count, positions, H, DH)
        * live_rows[:, :, None, None]
    )[0]
    d_value_mem = jnp.stack(value_mem_grads, 1).reshape(seq_count, positions, H, DH)
    d_queries = (
        (d_query_att + d_query_mem).reshape(seq_count, positions, model_width).astype(jnp.bfloat16)
    )
    d_keys = (d_key_att + d_key_mem).reshape(seq_count, positions, model_width).astype(jnp.bfloat16)
    d_values = (
        (d_value_att + d_value_mem).reshape(seq_count, positions, model_width).astype(jnp.bfloat16)
    )
    grad_query = jnp.einsum("sti,sto->io", normed, d_queries, preferred_element_type=jnp.float32)
    grad_key = jnp.einsum("sti,sto->io", normed, d_keys, preferred_element_type=jnp.float32)
    grad_value = jnp.einsum("sti,sto->io", normed, d_values, preferred_element_type=jnp.float32)
    d_normed = (
        jnp.einsum("sto,io->sti", d_queries, full_query, preferred_element_type=jnp.float32)
        + jnp.einsum("sto,io->sti", d_keys, full_key, preferred_element_type=jnp.float32)
        + jnp.einsum("sto,io->sti", d_values, full_value, preferred_element_type=jnp.float32)
    )
    _, attn_pull = jax.vjp(scaled_rows, inputs_f32, gain_one)
    d_input_part, grad_gain_attn = attn_pull(d_normed)
    input_grad = d_resid + d_input_part
    grad_parts = [
        grad_gain_attn,
        grad_query,
        grad_key,
        grad_value,
        grad_out,
        grad_pkey.reshape(PERS, model_width).T,
        grad_pvalue.reshape(PERS, model_width).T,
        grad_gain_ffn,
        grad_gate,
        grad_up,
        grad_down,
        grad_decay.reshape(LEVELS * H),
        grad_momentum.reshape(LEVELS * H),
    ]
    scattered = (
        lax.psum_scatter(
            grad_parts[0].astype(jnp.bfloat16), "fsdp", scatter_dimension=0, tiled=True
        ).astype(jnp.float32),
        lax.psum_scatter(
            grad_parts[1].astype(jnp.bfloat16), "fsdp", scatter_dimension=0, tiled=True
        ).astype(jnp.float32),
        lax.psum_scatter(
            grad_parts[2].astype(jnp.bfloat16), "fsdp", scatter_dimension=0, tiled=True
        ).astype(jnp.float32),
        lax.psum_scatter(
            grad_parts[3].astype(jnp.bfloat16), "fsdp", scatter_dimension=0, tiled=True
        ).astype(jnp.float32),
        lax.psum_scatter(
            grad_parts[4].astype(jnp.bfloat16), "fsdp", scatter_dimension=0, tiled=True
        ).astype(jnp.float32),
        lax.psum_scatter(
            grad_parts[5].astype(jnp.bfloat16), "fsdp", scatter_dimension=0, tiled=True
        ).astype(jnp.float32),
        lax.psum_scatter(
            grad_parts[6].astype(jnp.bfloat16), "fsdp", scatter_dimension=0, tiled=True
        ).astype(jnp.float32),
        lax.psum_scatter(
            grad_parts[7].astype(jnp.bfloat16), "fsdp", scatter_dimension=0, tiled=True
        ).astype(jnp.float32),
        lax.psum_scatter(
            grad_parts[8].astype(jnp.bfloat16), "fsdp", scatter_dimension=0, tiled=True
        ).astype(jnp.float32),
        lax.psum_scatter(
            grad_parts[9].astype(jnp.bfloat16), "fsdp", scatter_dimension=0, tiled=True
        ).astype(jnp.float32),
        lax.psum_scatter(
            grad_parts[10].astype(jnp.bfloat16), "fsdp", scatter_dimension=0, tiled=True
        ).astype(jnp.float32),
        lax.psum_scatter(
            grad_parts[11].astype(jnp.bfloat16), "fsdp", scatter_dimension=0, tiled=True
        ).astype(jnp.float32),
        lax.psum_scatter(
            grad_parts[12].astype(jnp.bfloat16), "fsdp", scatter_dimension=0, tiled=True
        ).astype(jnp.float32),
    )
    shares = (
        lax.psum(scattered[0].astype(jnp.bfloat16), "ctx").astype(jnp.float32),
        lax.psum(scattered[1].astype(jnp.bfloat16), "ctx").astype(jnp.float32),
        lax.psum(scattered[2].astype(jnp.bfloat16), "ctx").astype(jnp.float32),
        lax.psum(scattered[3].astype(jnp.bfloat16), "ctx").astype(jnp.float32),
        lax.psum(scattered[4].astype(jnp.bfloat16), "ctx").astype(jnp.float32),
        lax.psum(scattered[5].astype(jnp.bfloat16), "ctx").astype(jnp.float32),
        lax.psum(scattered[6].astype(jnp.bfloat16), "ctx").astype(jnp.float32),
        lax.psum(scattered[7].astype(jnp.bfloat16), "ctx").astype(jnp.float32),
        lax.psum(scattered[8].astype(jnp.bfloat16), "ctx").astype(jnp.float32),
        lax.psum(scattered[9].astype(jnp.bfloat16), "ctx").astype(jnp.float32),
        lax.psum(scattered[10].astype(jnp.bfloat16), "ctx").astype(jnp.float32),
        lax.psum(scattered[11].astype(jnp.bfloat16), "ctx").astype(jnp.float32),
        lax.psum(scattered[12].astype(jnp.bfloat16), "ctx").astype(jnp.float32),
    )
    table_rows = LEVELS // fsdp_count
    return (
        output,
        input_grad,
        shares[0],
        shares[1],
        shares[2],
        shares[3],
        shares[4],
        shares[5].T,
        shares[6].T,
        shares[7],
        shares[8],
        shares[9],
        shares[10],
        shares[11].reshape(table_rows, H),
        shares[12].reshape(table_rows, H),
    )


def solution(mesh):
    in_specs = (
        P("fsdp", "ctx", None),
        P("fsdp"),
        P("fsdp", None),
        P("fsdp", None),
        P("fsdp", None),
        P("fsdp", None),
        P(None, "fsdp"),
        P(None, "fsdp"),
        P("fsdp"),
        P("fsdp", None),
        P("fsdp", None),
        P("fsdp", None),
        P("fsdp", None),
        P("fsdp", None),
        P("fsdp"),
        P("fsdp", "ctx"),
        P("fsdp", "ctx"),
        P("fsdp", "ctx", None),
    )
    out_specs = (
        P("fsdp", "ctx", None),
        P("fsdp", "ctx", None),
        P("fsdp"),
        P("fsdp", None),
        P("fsdp", None),
        P("fsdp", None),
        P("fsdp", None),
        P(None, "fsdp"),
        P(None, "fsdp"),
        P("fsdp"),
        P("fsdp", None),
        P("fsdp", None),
        P("fsdp", None),
        P("fsdp", None),
        P("fsdp", None),
    )
    return jax.shard_map(shards, mesh=mesh, in_specs=in_specs, out_specs=out_specs, check_vma=False)
```

profile of v0, /device:TPU:0, one launch (start us, length us, event | category | flops | bytes accessed | tf_op | source)
XLA Modules:
  0.0 1568.9 jit_solution(7426906956024974043)
XLA Ops:
  40.6 24.6 %all-gather.14.cloned.1.call-done = bf16[1024,1024]{1,0:T(8,128)(2,1)} async-done(((bf16[128,1024]{1,0:T(8,128)(2,1)}), bf16[1024,1024]{1,0:T(8,128)(2,1)}) %all-gather.14.cloned.1.call-update) | async-done | bytes 2097168 | tf_op jit(solution)/shard_map/all_gather | solution.py:102
  148.3 39.3 %all-gather.22.cloned.1.call-done = bf16[2,1024,1024]{2,1,0:T(8,128)(2,1)} async-done(((bf16[2,64,1024]{2,1,0:T(8,128)(2,1)}), bf16[2,1024,1024]{2,1,0:T(8,128)(2,1)}) %all-gather.22.cloned.1.call-update) | async-done | bytes 4194320 | tf_op jit(solution)/shard_map/all_gather | solution.py:126
  195.2 46.2 %all-gather.16.cloned.1.call-done = bf16[2,1024,1024]{2,1,0:T(8,128)(2,1)} async-done(((bf16[2,64,1024]{2,1,0:T(8,128)(2,1)}), bf16[2,1024,1024]{2,1,0:T(8,128)(2,1)}) %all-gather.16.cloned.1.call-update) | async-done | bytes 4194320 | tf_op jit(solution)/shard_map/all_gather | solution.py:127
  247.8 457.0 %while.22 = (s32[]{:T(128)}, f32[2,8,256,128]{3,2,1,0:T(8,128)S(1)}, f32[2,8,256,256]{3,2,1,0:T(8,128)}, f32[2,8,256,128]{3,2,1,0:T(8,128)}, s32[]{:T(128)}, /*index=5*/s32[]{:T(128)}) while((s32[]{:T(128)}, f32[2,8,256,128]{3,2,1,0:T(8,128)S(1)}, f32[2,8,256,256]{3,2,1,0:T(8,128)}, f32[2,8,256,128]{3,2,1,0:T(8,128)}, s32[]{:T(128)}, ...), condition=%wide.region_7.8_spmd.clone, body=%wide.region_6.7_spmd.clone.sunk | while | flops 1612709888 | bytes 16777336 | solution.py:224
  259.0 21.4 %collective-permute-done = bf16[2,8,256,128]{3,2,1,0:T(8,128)(2,1)} collective-permute-done((bf16[2,8,256,128]{3,2,1,0:T(8,128)(2,1)S(1)}, bf16[2,8,256,128]{3,2,1,0:T(8,128)(2,1)}, u32[]{:S(2)}, u32[]{:S(2)}) %collective-permute-start) | collective-permute-done | bytes 1048608 | tf_op jit(solution)/shard_map/while/body/eval_jaxpr/ppermute | solution.py:21
  294.2 20.5 %collective-permute-done = bf16[2,8,256,128]{3,2,1,0:T(8,128)(2,1)} collective-permute-done((bf16[2,8,256,128]{3,2,1,0:T(8,128)(2,1)S(1)}, bf16[2,8,256,128]{3,2,1,0:T(8,128)(2,1)}, u32[]{:S(2)}, u32[]{:S(2)}) %collective-permute-start) | collective-permute-done | bytes 1048608 | tf_op jit(solution)/shard_map/while/body/eval_jaxpr/ppermute | solution.py:21
  328.6 19.5 %collective-permute-done = bf16[2,8,256,128]{3,2,1,0:T(8,128)(2,1)} collective-permute-done((bf16[2,8,256,128]{3,2,1,0:T(8,128)(2,1)S(1)}, bf16[2,8,256,128]{3,2,1,0:T(8,128)(2,1)}, u32[]{:S(2)}, u32[]{:S(2)}) %collective-permute-start) | collective-permute-done | bytes 1048608 | tf_op jit(solution)/shard_map/while/body/eval_jaxpr/ppermute | solution.py:21
  361.8 18.6 %collective-permute-done = bf16[2,8,256,128]{3,2,1,0:T(8,128)(2,1)} collective-permute-done((bf16[2,8,256,128]{3,2,1,0:T(8,128)(2,1)S(1)}, bf16[2,8,256,128]{3,2,1,0:T(8,128)(2,1)}, u32[]{:S(2)}, u32[]{:S(2)}) %collective-permute-start) | collective-permute-done | bytes 1048608 | tf_op jit(solution)/shard_map/while/body/eval_jaxpr/ppermute | solution.py:21
  394.1 17.7 %collective-permute-done = bf16[2,8,256,128]{3,2,1,0:T(8,128)(2,1)} collective-permute-done((bf16[2,8,256,128]{3,2,1,0:T(8,128)(2,1)S(1)}, bf16[2,8,256,128]{3,2,1,0:T(8,128)(2,1)}, u32[]{:S(2)}, u32[]{:S(2)}) %collective-permute-start) | collective-permute-done | bytes 1048608 | tf_op jit(solution)/shard_map/while/body/eval_jaxpr/ppermute | solution.py:21
  427.1 17.0 %collective-permute-done = bf16[2,8,256,128]{3,2,1,0:T(8,128)(2,1)} collective-permute-done((bf16[2,8,256,128]{3,2,1,0:T(8,128)(2,1)S(1)}, bf16[2,8,256,128]{3,2,1,0:T(8,128)(2,1)}, u32[]{:S(2)}, u32[]{:S(2)}) %collective-permute-start) | collective-permute-done | bytes 1048608 | tf_op jit(solution)/shard_map/while/body/eval_jaxpr/ppermute | solution.py:21
  460.0 16.1 %collective-permute-done = bf16[2,8,256,128]{3,2,1,0:T(8,128)(2,1)} collective-permute-done((bf16[2,8,256,128]{3,2,1,0:T(8,128)(2,1)S(1)}, bf16[2,8,256,128]{3,2,1,0:T(8,128)(2,1)}, u32[]{:S(2)}, u32[]{:S(2)}) %collective-permute-start) | collective-permute-done | bytes 1048608 | tf_op jit(solution)/shard_map/while/body/eval_jaxpr/ppermute | solution.py:21
  802.3 498.8 %while.23 = (s32[]{:T(128)}, f32[2,8,256,128]{3,2,1,0:T(8,128)}, f32[2,8,256,256]{3,2,1,0:T(8,128)}, f32[2,8,256,128]{3,2,1,0:T(8,128)}, s32[]{:T(128)}, /*index=5*/s32[]{:T(128)}) while((s32[]{:T(128)}, f32[2,8,256,128]{3,2,1,0:T(8,128)}, f32[2,8,256,256]{3,2,1,0:T(8,128)}, f32[2,8,256,128]{3,2,1,0:T(8,128)}, s32[]{:T(128)}, ...), condition=%wide.region_16.17_spmd.clone, body=%wide.region_15.16_spmd.clone.sunk | while | flops 1612709888 | bytes 16777336 | solution.py:339
  810.5 36.3 %collective-permute-done.1 = bf16[2,8,256,128]{3,2,1,0:T(8,128)(2,1)} collective-permute-done((bf16[2,8,256,128]{3,2,1,0:T(8,128)(2,1)S(1)}, bf16[2,8,256,128]{3,2,1,0:T(8,128)(2,1)}, u32[]{:S(2)}, u32[]{:S(2)}) %collective-permute-start.1) | collective-permute-done | bytes 1048608 | tf_op jit(solution)/shard_map/while/body/eval_jaxpr/ppermute | solution.py:21
  858.3 29.0 %collective-permute-done.1 = bf16[2,8,256,128]{3,2,1,0:T(8,128)(2,1)} collective-permute-done((bf16[2,8,256,128]{3,2,1,0:T(8,128)(2,1)S(1)}, bf16[2,8,256,128]{3,2,1,0:T(8,128)(2,1)}, u32[]{:S(2)}, u32[]{:S(2)}) %collective-permute-start.1) | collective-permute-done | bytes 1048608 | tf_op jit(solution)/shard_map/while/body/eval_jaxpr/ppermute | solution.py:21
  898.7 23.1 %collective-permute-done.1 = bf16[2,8,256,128]{3,2,1,0:T(8,128)(2,1)} collective-permute-done((bf16[2,8,256,128]{3,2,1,0:T(8,128)(2,1)S(1)}, bf16[2,8,256,128]{3,2,1,0:T(8,128)(2,1)}, u32[]{:S(2)}, u32[]{:S(2)}) %collective-permute-start.1) | collective-permute-done | bytes 1048608 | tf_op jit(solution)/shard_map/while/body/eval_jaxpr/ppermute | solution.py:21
  933.3 21.9 %collective-permute-done.1 = bf16[2,8,256,128]{3,2,1,0:T(8,128)(2,1)} collective-permute-done((bf16[2,8,256,128]{3,2,1,0:T(8,128)(2,1)S(1)}, bf16[2,8,256,128]{3,2,1,0:T(8,128)(2,1)}, u32[]{:S(2)}, u32[]{:S(2)}) %collective-permute-start.1) | collective-permute-done | bytes 1048608 | tf_op jit(solution)/shard_map/while/body/eval_jaxpr/ppermute | solution.py:21
  967.2 25.9 %collective-permute-done.1 = bf16[2,8,256,128]{3,2,1,0:T(8,128)(2,1)} collective-permute-done((bf16[2,8,256,128]{3,2,1,0:T(8,128)(2,1)S(1)}, bf16[2,8,256,128]{3,2,1,0:T(8,128)(2,1)}, u32[]{:S(2)}, u32[]{:S(2)}) %collective-permute-start.1) | collective-permute-done | bytes 1048608 | tf_op jit(solution)/shard_map/while/body/eval_jaxpr/ppermute | solution.py:21
  1004.5 22.3 %collective-permute-done.1 = bf16[2,8,256,128]{3,2,1,0:T(8,128)(2,1)} collective-permute-done((bf16[2,8,256,128]{3,2,1,0:T(8,128)(2,1)S(1)}, bf16[2,8,256,128]{3,2,1,0:T(8,128)(2,1)}, u32[]{:S(2)}, u32[]{:S(2)}) %collective-permute-start.1) | collective-permute-done | bytes 1048608 | tf_op jit(solution)/shard_map/while/body/eval_jaxpr/ppermute | solution.py:21
  1038.3 22.0 %collective-permute-done.1 = bf16[2,8,256,128]{3,2,1,0:T(8,128)(2,1)} collective-permute-done((bf16[2,8,256,128]{3,2,1,0:T(8,128)(2,1)S(1)}, bf16[2,8,256,128]{3,2,1,0:T(8,128)(2,1)}, u32[]{:S(2)}, u32[]{:S(2)}) %collective-permute-start.1) | collective-permute-done | bytes 1048608 | tf_op jit(solution)/shard_map/while/body/eval_jaxpr/ppermute | solution.py:21
  1071.9 20.6 %collective-permute-done.1 = bf16[2,8,256,128]{3,2,1,0:T(8,128)(2,1)} collective-permute-done((bf16[2,8,256,128]{3,2,1,0:T(8,128)(2,1)S(1)}, bf16[2,8,256,128]{3,2,1,0:T(8,128)(2,1)}, u32[]{:S(2)}, u32[]{:S(2)}) %collective-permute-start.1) | collective-permute-done | bytes 1048608 | tf_op jit(solution)/shard_map/while/body/eval_jaxpr/ppermute | solution.py:21
  1104.0 20.1 %collective-permute-done.1 = bf16[2,8,256,128]{3,2,1,0:T(8,128)(2,1)} collective-permute-done((bf16[2,8,256,128]{3,2,1,0:T(8,128)(2,1)S(1)}, bf16[2,8,256,128]{3,2,1,0:T(8,128)(2,1)}, u32[]{:S(2)}, u32[]{:S(2)}) %collective-permute-start.1) | collective-permute-done | bytes 1048608 | tf_op jit(solution)/shard_map/while/body/eval_jaxpr/ppermute | solution.py:21
  1135.5 19.0 %collective-permute-done.1 = bf16[2,8,256,128]{3,2,1,0:T(8,128)(2,1)} collective-permute-done((bf16[2,8,256,128]{3,2,1,0:T(8,128)(2,1)S(1)}, bf16[2,8,256,128]{3,2,1,0:T(8,128)(2,1)}, u32[]{:S(2)}, u32[]{:S(2)}) %collective-permute-start.1) | collective-permute-done | bytes 1048608 | tf_op jit(solution)/shard_map/while/body/eval_jaxpr/ppermute | solution.py:21
  1165.9 18.1 %collective-permute-done.1 = bf16[2,8,256,128]{3,2,1,0:T(8,128)(2,1)} collective-permute-done((bf16[2,8,256,128]{3,2,1,0:T(8,128)(2,1)S(1)}, bf16[2,8,256,128]{3,2,1,0:T(8,128)(2,1)}, u32[]{:S(2)}, u32[]{:S(2)}) %collective-permute-start.1) | collective-permute-done | bytes 1048608 | tf_op jit(solution)/shard_map/while/body/eval_jaxpr/ppermute | solution.py:21
  1195.4 17.2 %collective-permute-done.1 = bf16[2,8,256,128]{3,2,1,0:T(8,128)(2,1)} collective-permute-done((bf16[2,8,256,128]{3,2,1,0:T(8,128)(2,1)S(1)}, bf16[2,8,256,128]{3,2,1,0:T(8,128)(2,1)}, u32[]{:S(2)}, u32[]{:S(2)}) %collective-permute-start.1) | collective-permute-done | bytes 1048608 | tf_op jit(solution)/shard_map/while/body/eval_jaxpr/ppermute | solution.py:21
  1224.0 16.8 %collective-permute-done.1 = bf16[2,8,256,128]{3,2,1,0:T(8,128)(2,1)} collective-permute-done((bf16[2,8,256,128]{3,2,1,0:T(8,128)(2,1)S(1)}, bf16[2,8,256,128]{3,2,1,0:T(8,128)(2,1)}, u32[]{:S(2)}, u32[]{:S(2)}) %collective-permute-start.1) | collective-permute-done | bytes 1048608 | tf_op jit(solution)/shard_map/while/body/eval_jaxpr/ppermute | solution.py:21
  1252.2 17.2 %collective-permute-done.1 = bf16[2,8,256,128]{3,2,1,0:T(8,128)(2,1)} collective-permute-done((bf16[2,8,256,128]{3,2,1,0:T(8,128)(2,1)S(1)}, bf16[2,8,256,128]{3,2,1,0:T(8,128)(2,1)}, u32[]{:S(2)}, u32[]{:S(2)}) %collective-permute-start.1) | collective-permute-done | bytes 1048608 | tf_op jit(solution)/shard_map/while/body/eval_jaxpr/ppermute | solution.py:21
  1280.8 17.6 %collective-permute-done.1 = bf16[2,8,256,128]{3,2,1,0:T(8,128)(2,1)} collective-permute-done((bf16[2,8,256,128]{3,2,1,0:T(8,128)(2,1)S(1)}, bf16[2,8,256,128]{3,2,1,0:T(8,128)(2,1)}, u32[]{:S(2)}, u32[]{:S(2)}) %collective-permute-start.1) | collective-permute-done | bytes 1048608 | tf_op jit(solution)/shard_map/while/body/eval_jaxpr/ppermute | solution.py:21
  1326.5 25.1 %reduce-scatter.21.cloned.1.call-done = bf16[128,1024]{1,0:T(8,128)(2,1)} async-done(((bf16[1024,1024]{1,0:T(8,128)(2,1)}), bf16[128,1024]{1,0:T(8,128)(2,1)}) %reduce-scatter.21.cloned.1.call-update) | async-done | bytes 262160 | tf_op jit(solution)/shard_map/reduce_scatter | solution.py:426
  1351.6 34.8 %reduce-scatter.19.cloned.1.call-done = bf16[128,1024]{1,0:T(8,128)(2,1)} async-done(((bf16[1024,1024]{1,0:T(8,128)(2,1)}), bf16[128,1024]{1,0:T(8,128)(2,1)}) %reduce-scatter.19.cloned.1.call-update) | async-done | bytes 262160 | tf_op jit(solution)/shard_map/reduce_scatter | solution.py:423
  1393.5 25.0 %reduce-scatter.31.cloned.1.call-done = bf16[128,16]{1,0:T(8,128)(2,1)} async-done(((bf16[1024,16]{1,0:T(8,128)(2,1)}), bf16[128,16]{1,0:T(8,128)(2,1)}) %reduce-scatter.31.cloned.1.call-update) | async-done | bytes 4112
  1419.3 31.6 %reduce-scatter.33.cloned.1.call-done = bf16[128,16]{1,0:T(8,128)(2,1)} async-done(((bf16[1024,16]{1,0:T(8,128)(2,1)}), bf16[128,16]{1,0:T(8,128)(2,1)}) %reduce-scatter.33.cloned.1.call-update) | async-done | bytes 4112
  1472.1 74.7 %all-reduce.6 = (bf16[128]{0:T(256)(128)(2,1)S(1)}, bf16[16,128]{1,0:T(8,128)(2,1)S(1)}, bf16[16,128]{1,0:T(8,128)(2,1)S(1)}, bf16[128]{0:T(256)(128)(2,1)S(1)},...) all-reduce(bf16[128]{0:T(256)(128)(2,1)S(1)} %dynamic-slice.1, ...), channel_id=1, replica_groups=mesh['ctx'=16,'fsdp'=8] {'ctx'}, use_global_device_ids=true, to_apply=%region_21.22 | all-reduce | flops 4384 | bytes 17536 | tf_op jit(solution)/shard_map/psum | solution.py:458
  (510 shorter events, 791.2 us)
Async XLA Ops:
  7.2 30.4 %all-gather.20.cloned.1.call-start = ((), (), s32[]{:S(2)}) async-start(), calls=%async_computation.13 | async-start | bytes 2359296 | tf_op jit(solution)/shard_map/all_gather | solution.py:101
  7.9 57.2 %all-gather.14.cloned.1.call-start = ((), (), s32[]{:S(2)}) async-start(), calls=%async_computation.10 | async-start | bytes 2359296 | tf_op jit(solution)/shard_map/all_gather | solution.py:102
  8.7 121.2 %all-gather.18.cloned.1.call-start = ((), (), s32[]{:S(2)}) async-start(), calls=%async_computation.12 | async-start | bytes 2359296 | tf_op jit(solution)/shard_map/all_gather | solution.py:100
  9.4 133.0 %all-gather.30.cloned.1.call-start = ((), (), s32[]{:S(2)}) async-start(), calls=%async_computation.18 | async-start | bytes 6488064 | tf_op jit(solution)/shard_map/all_gather | solution.py:109
  10.0 177.5 %all-gather.22.cloned.1.call-start = ((), (), s32[]{:S(2)}) async-start(), calls=%async_computation.14 | async-start | bytes 4456448 | tf_op jit(solution)/shard_map/all_gather | solution.py:126
  40.5 200.9 %all-gather.16.cloned.1.call-start = ((), (), s32[]{:S(2)}) async-start(), calls=%async_computation.11 | async-start | bytes 4456448 | tf_op jit(solution)/shard_map/all_gather | solution.py:127
  68.0 639.1 %all-gather.24.cloned.1.call-start = ((), (), s32[]{:S(2)}) async-start(), calls=%async_computation.15 | async-start | bytes 2359296 | tf_op jit(solution)/shard_map/all_gather | solution.py:103
  68.7 640.8 %all-gather.28.cloned.1.call-start = ((), (), s32[]{:S(2)}) async-start(), calls=%async_computation.17 | async-start | bytes 6488064 | tf_op jit(solution)/shard_map/all_gather | solution.py:108
  69.5 644.8 %all-gather.26.cloned.1.call-start = ((), (), s32[]{:S(2)}) async-start(), calls=%async_computation.16 | async-start | bytes 6488064 | tf_op jit(solution)/shard_map/all_gather | solution.py:107
  70.2 1233.3 %reduce-scatter.15.cloned.1.call-start = ((), (), s32[]{:S(2)}) async-start(), calls=%async_computation.19 | async-start | bytes 8912896 | tf_op jit(solution)/shard_map/reduce_scatter | solution.py:301
  254.6 25.7 %collective-permute-start = (bf16[2,8,256,128]{3,2,1,0:T(8,128)(2,1)S(1)}, bf16[2,8,256,128]{3,2,1,0:T(8,128)(2,1)}, u32[]{:S(2)}, u32[]{:S(2)}) collective-permute-start(bf16[2,8,256,128]{3,2,1,0:T(8,128)(2,1)S(1)} %add_convert_fusion.4), channel_id=1, source_target_pairs={{0,8},{8,16},{16,24},{24,32},{32,40},{40,48},{48,56},{56,64},{64,7... | collective-permute-start | bytes 3145736 | tf_op jit(solution)/shard_map/while/body/eval_jaxpr/ppermute | solution.py:21
  288.6 26.0 %collective-permute-start = (bf16[2,8,256,128]{3,2,1,0:T(8,128)(2,1)S(1)}, bf16[2,8,256,128]{3,2,1,0:T(8,128)(2,1)}, u32[]{:S(2)}, u32[]{:S(2)}) collective-permute-start(bf16[2,8,256,128]{3,2,1,0:T(8,128)(2,1)S(1)} %add_convert_fusion.4), channel_id=1, source_target_pairs={{0,8},{8,16},{16,24},{24,32},{32,40},{40,48},{48,56},{56,64},{64,7... | collective-permute-start | bytes 3145736 | tf_op jit(solution)/shard_map/while/body/eval_jaxpr/ppermute | solution.py:21
  322.9 25.1 %collective-permute-start = (bf16[2,8,256,128]{3,2,1,0:T(8,128)(2,1)S(1)}, bf16[2,8,256,128]{3,2,1,0:T(8,128)(2,1)}, u32[]{:S(2)}, u32[]{:S(2)}) collective-permute-start(bf16[2,8,256,128]{3,2,1,0:T(8,128)(2,1)S(1)} %add_convert_fusion.4), channel_id=1, source_target_pairs={{0,8},{8,16},{16,24},{24,32},{32,40},{40,48},{48,56},{56,64},{64,7... | collective-permute-start | bytes 3145736 | tf_op jit(solution)/shard_map/while/body/eval_jaxpr/ppermute | solution.py:21
  356.3 24.1 %collective-permute-start = (bf16[2,8,256,128]{3,2,1,0:T(8,128)(2,1)S(1)}, bf16[2,8,256,128]{3,2,1,0:T(8,128)(2,1)}, u32[]{:S(2)}, u32[]{:S(2)}) collective-permute-start(bf16[2,8,256,128]{3,2,1,0:T(8,128)(2,1)S(1)} %add_convert_fusion.4), channel_id=1, source_target_pairs={{0,8},{8,16},{16,24},{24,32},{32,40},{40,48},{48,56},{56,64},{64,7... | collective-permute-start | bytes 3145736 | tf_op jit(solution)/shard_map/while/body/eval_jaxpr/ppermute | solution.py:21
  420.0 24.1 %collective-permute-start = (bf16[2,8,256,128]{3,2,1,0:T(8,128)(2,1)S(1)}, bf16[2,8,256,128]{3,2,1,0:T(8,128)(2,1)}, u32[]{:S(2)}, u32[]{:S(2)}) collective-permute-start(bf16[2,8,256,128]{3,2,1,0:T(8,128)(2,1)S(1)} %add_convert_fusion.4), channel_id=1, source_target_pairs={{0,8},{8,16},{16,24},{24,32},{32,40},{40,48},{48,56},{56,64},{64,7... | collective-permute-start | bytes 3145736 | tf_op jit(solution)/shard_map/while/body/eval_jaxpr/ppermute | solution.py:21
  452.4 23.7 %collective-permute-start = (bf16[2,8,256,128]{3,2,1,0:T(8,128)(2,1)S(1)}, bf16[2,8,256,128]{3,2,1,0:T(8,128)(2,1)}, u32[]{:S(2)}, u32[]{:S(2)}) collective-permute-start(bf16[2,8,256,128]{3,2,1,0:T(8,128)(2,1)S(1)} %add_convert_fusion.4), channel_id=1, source_target_pairs={{0,8},{8,16},{16,24},{24,32},{32,40},{40,48},{48,56},{56,64},{64,7... | collective-permute-start | bytes 3145736 | tf_op jit(solution)/shard_map/while/body/eval_jaxpr/ppermute | solution.py:21
  761.0 565.4 %reduce-scatter.17.cloned.1.call-start = ((), (), s32[]{:S(2)}) async-start(), calls=%async_computation.20 | async-start | bytes 2359296 | tf_op jit(solution)/shard_map/reduce_scatter | solution.py:420
  771.8 554.6 %reduce-scatter.23.cloned.1.call-start = ((), (), s32[]{:S(2)}) async-start(), calls=%async_computation.23 | async-start | bytes 2359296 | tf_op jit(solution)/shard_map/reduce_scatter | solution.py:429
  774.9 551.5 %reduce-scatter.25.cloned.1.call-start = ((), (), s32[]{:S(2)}) async-start(), calls=%async_computation.24 | async-start | bytes 6488064 | tf_op jit(solution)/shard_map/reduce_scatter | solution.py:441
  780.3 546.2 %reduce-scatter.27.cloned.1.call-start = ((), (), s32[]{:S(2)}) async-start(), calls=%async_computation.25 | async-start | bytes 6488064 | tf_op jit(solution)/shard_map/reduce_scatter | solution.py:444
  785.6 540.8 %reduce-scatter.29.cloned.1.call-start = ((), (), s32[]{:S(2)}) async-start(), calls=%async_computation.26 | async-start | bytes 6488064 | tf_op jit(solution)/shard_map/reduce_scatter | solution.py:447
  791.9 559.6 %reduce-scatter.21.cloned.1.call-start = ((), (), s32[]{:S(2)}) async-start(), calls=%async_computation.22 | async-start | bytes 2359296 | tf_op jit(solution)/shard_map/reduce_scatter | solution.py:426
  809.2 37.6 %collective-permute-start.1 = (bf16[2,8,256,128]{3,2,1,0:T(8,128)(2,1)S(1)}, bf16[2,8,256,128]{3,2,1,0:T(8,128)(2,1)}, u32[]{:S(2)}, u32[]{:S(2)}) collective-permute-start(bf16[2,8,256,128]{3,2,1,0:T(8,128)(2,1)S(1)} %add_convert_fusion.5), channel_id=1, source_target_pairs={{8,0},{16,8},{24,16},{32,24},{40,32},{48,40},{56,48},{64,56},{72,6... | collective-permute-start | bytes 3145736 | tf_op jit(solution)/shard_map/while/body/eval_jaxpr/ppermute | solution.py:21
  857.0 30.3 %collective-permute-start.1 = (bf16[2,8,256,128]{3,2,1,0:T(8,128)(2,1)S(1)}, bf16[2,8,256,128]{3,2,1,0:T(8,128)(2,1)}, u32[]{:S(2)}, u32[]{:S(2)}) collective-permute-start(bf16[2,8,256,128]{3,2,1,0:T(8,128)(2,1)S(1)} %add_convert_fusion.5), channel_id=1, source_target_pairs={{8,0},{16,8},{24,16},{32,24},{40,32},{48,40},{56,48},{64,56},{72,6... | collective-permute-start | bytes 3145736 | tf_op jit(solution)/shard_map/while/body/eval_jaxpr/ppermute | solution.py:21
  897.4 24.4 %collective-permute-start.1 = (bf16[2,8,256,128]{3,2,1,0:T(8,128)(2,1)S(1)}, bf16[2,8,256,128]{3,2,1,0:T(8,128)(2,1)}, u32[]{:S(2)}, u32[]{:S(2)}) collective-permute-start(bf16[2,8,256,128]{3,2,1,0:T(8,128)(2,1)S(1)} %add_convert_fusion.5), channel_id=1, source_target_pairs={{8,0},{16,8},{24,16},{32,24},{40,32},{48,40},{56,48},{64,56},{72,6... | collective-permute-start | bytes 3145736 | tf_op jit(solution)/shard_map/while/body/eval_jaxpr/ppermute | solution.py:21
  965.9 27.2 %collective-permute-start.1 = (bf16[2,8,256,128]{3,2,1,0:T(8,128)(2,1)S(1)}, bf16[2,8,256,128]{3,2,1,0:T(8,128)(2,1)}, u32[]{:S(2)}, u32[]{:S(2)}) collective-permute-start(bf16[2,8,256,128]{3,2,1,0:T(8,128)(2,1)S(1)} %add_convert_fusion.5), channel_id=1, source_target_pairs={{8,0},{16,8},{24,16},{32,24},{40,32},{48,40},{56,48},{64,56},{72,6... | collective-permute-start | bytes 3145736 | tf_op jit(solution)/shard_map/while/body/eval_jaxpr/ppermute | solution.py:21
  1003.2 23.6 %collective-permute-start.1 = (bf16[2,8,256,128]{3,2,1,0:T(8,128)(2,1)S(1)}, bf16[2,8,256,128]{3,2,1,0:T(8,128)(2,1)}, u32[]{:S(2)}, u32[]{:S(2)}) collective-permute-start(bf16[2,8,256,128]{3,2,1,0:T(8,128)(2,1)S(1)} %add_convert_fusion.5), channel_id=1, source_target_pairs={{8,0},{16,8},{24,16},{32,24},{40,32},{48,40},{56,48},{64,56},{72,6... | collective-permute-start | bytes 3145736 | tf_op jit(solution)/shard_map/while/body/eval_jaxpr/ppermute | solution.py:21
  1037.0 23.3 %collective-permute-start.1 = (bf16[2,8,256,128]{3,2,1,0:T(8,128)(2,1)S(1)}, bf16[2,8,256,128]{3,2,1,0:T(8,128)(2,1)}, u32[]{:S(2)}, u32[]{:S(2)}) collective-permute-start(bf16[2,8,256,128]{3,2,1,0:T(8,128)(2,1)S(1)} %add_convert_fusion.5), channel_id=1, source_target_pairs={{8,0},{16,8},{24,16},{32,24},{40,32},{48,40},{56,48},{64,56},{72,6... | collective-permute-start | bytes 3145736 | tf_op jit(solution)/shard_map/while/body/eval_jaxpr/ppermute | solution.py:21
  1310.6 75.8 %reduce-scatter.19.cloned.1.call-start = ((), (), s32[]{:S(2)}) async-start(), calls=%async_computation.21 | async-start | bytes 2359296 | tf_op jit(solution)/shard_map/reduce_scatter | solution.py:423
  1323.9 94.6 %reduce-scatter.31.cloned.1.call-start = ((), (), s32[]{:S(2)}) async-start(), calls=%async_computation.27 | async-start | bytes 294912
  1325.1 125.9 %reduce-scatter.33.cloned.1.call-start = ((), (), s32[]{:S(2)}) async-start(), calls=%async_computation.28 | async-start | bytes 294912
  1326.3 225.9 %all-reduce.11.cloned.1.call-start = ((), (), s32[]{:S(2)}) async-start(), calls=%async_computation.29 | async-start | bytes 6422528 | tf_op jit(solution)/shard_map/psum | solution.py:459
  (125 other events, 2904.4 us)
Sparse Core Ops, SparseCore 0:
  9.7 27.8 all-gather.19
  39.3 25.7 all-gather.13
  66.9 25.7 all-gather.17
  94.2 39.4 all-gather.29
  136.3 51.1 all-gather.21
  190.2 51.1 all-gather.15
  243.1 25.0 all-gather.23
  270.0 39.2 all-gather.27
  311.0 38.8 all-gather.25
  761.1 116.8 reduce-scatter.14
  880.4 34.0 reduce-scatter.16
  916.8 32.5 reduce-scatter.22
  951.8 40.1 reduce-scatter.24
  994.3 41.1 reduce-scatter.26
  1037.7 41.2 reduce-scatter.28
  1310.7 40.8 reduce-scatter.20
  1353.8 32.5 reduce-scatter.18
  1389.2 29.3 reduce-scatter.30
  1421.6 29.3 reduce-scatter.32
  1455.1 95.8 all-reduce.10
where the time goes:
time: 1580 us; the launch traced here: 1570 us
  waiting for transfers between devices  804 us (51%)
  matrix products  338 us (21%)
  blocking collectives  149 us (9%)
  starting transfers between devices  123 us (8%)
  other arithmetic  105 us (7%)
  local copies, waits for them, and re-layouts  31.4 us (2%)
  between operations  17.6 us (1%)
    ppermute x30, waiting for transfers between devices, from_behind(): lax.ppermute(value, axis, [(source, source + steps) for source in range(f...  558 us
    dot_general x46, matrix products, batched(): return jnp.einsum(pattern, left_side, right_side, precision=highest)  245 us
    ppermute x30, starting transfers between devices, from_behind(): lax.ppermute(value, axis, [(source, source + steps) for source in range(f...  122 us
    psum x1, blocking collectives, shards(): lax.psum(scattered[0].astype(jnp.bfloat16), 'ctx').astype(jnp.float32)  74.7 us
    unnamed x22, waiting for transfers between devices  61.5 us
    all_gather x1, waiting for transfers between devices, shards(): lax.all_gather(values, 'ctx', axis=1, tiled=True)  46.2 us
    convert_element_type x15, other arithmetic, relay_adjoint(): return from_behind(affine(back_map, back_offset, incoming).astype(jnp.bfl...  41.1 us
    all_gather x1, waiting for transfers between devices, shards(): lax.all_gather(key_rows, 'ctx', axis=1, tiled=True)  39.3 us
  transfers between devices with their start and end apart: 50, of which 38 were waited for; matrix products, arithmetic and copies ran while one was open for 26% of the time, Pallas kernels for 0%

commit v1 on v0

v1 whole, which is shorter than its diff:
```python
import functools

import jax
import jax.numpy as jnp
from jax import lax
from jax.experimental import pallas as pl
from jax.experimental.pallas import tpu as pltpu
from jax.sharding import PartitionSpec as P

MESH = pl.DeviceIdType.MESH
HIGHEST = lax.Precision.HIGHEST
bf16, f32 = jnp.bfloat16, jnp.float32
EPS = 1e-06
RATE = 0.1
SCALE = 128**-0.5
VMEM_LIMIT = 60 << 20


def coords():
    c, f = lax.axis_index("ctx"), lax.axis_index("fsdp")
    return c, lax.div(f, 2), lax.rem(f, 2)


def pair_of(c):
    return lax.div(c, 8), lax.rem(lax.div(c, 2), 4), lax.rem(c, 2)


def at_ctx(c, dx, dy):
    x, y = lax.div(c, 4), lax.rem(c, 4)
    return lax.rem(x + dx, 4) * 4 + lax.rem(y + dy, 4)


CTX_STEPS = [(dx, dy) for dx in range(4) for dy in range(4) if dx or dy]
CTX_STEPS.sort(key=lambda s: -(min(s[0], 4 - s[0]) + min(s[1], 4 - s[1])))


def device(c, z, k):
    return (c, 2 * z + k)


def nn(a, b, precision=None):
    return jnp.dot(a, b, preferred_element_type=f32, precision=precision)


def nt(a, b, precision=None):
    return lax.dot_general(
        a, b, (((1,), (1,)), ((), ())), preferred_element_type=f32, precision=precision
    )


def tn(a, b, precision=None):
    return lax.dot_general(
        a, b, (((0,), (0,)), ((), ())), preferred_element_type=f32, precision=precision
    )


def meet(peers):
    barrier = pltpu.get_barrier_semaphore()
    for peer in peers:
        pl.semaphore_signal(barrier, inc=1, device_id=peer, device_id_type=MESH)
    pl.semaphore_wait(barrier, len(peers))


def z_peers(c, z, k):
    return [device(c, lax.rem(z + d, 4), k) for d in range(1, 4)]


def remote(src, dst, ssem, rsem, peer):
    return pltpu.make_async_remote_copy(
        src_ref=src, dst_ref=dst, send_sem=ssem, recv_sem=rsem, device_id=peer, device_id_type=MESH
    )


def comm_call(body, name, cid, out_shapes, sems, *operands):
    return pl.pallas_call(
        body,
        out_shape=out_shapes,
        in_specs=[pl.BlockSpec(memory_space=pl.ANY)] * len(operands),
        out_specs=jax.tree.map(lambda _: pl.BlockSpec(memory_space=pl.ANY), out_shapes),
        scratch_shapes=[
            pltpu.SemaphoreType.DMA((sems,)),
            pltpu.SemaphoreType.DMA((sems,)),
            pltpu.SemaphoreType.DMA((sems,)),
        ],
        compiler_params=pltpu.CompilerParams(collective_id=cid, has_side_effects=True),
        name=name,
    )(*operands)


def like(*shapes, dtype=bf16):
    return [jax.ShapeDtypeStruct(s, dtype) for s in shapes]


def front_kernel(
    x, cot, meta, wq, wk, wv, wo, wg, wu, wd, pers,
    x_all, cot_all, meta_all, wq_all, wk_all, wv_all, wo_all, wg_all, wu_all, wd_all, pers_all,
    ssem, rsem, lsem,
):
    c, z, k = coords()
    f = 2 * z + k
    sibling = device(c, z, 1 - k)
    meet(z_peers(c, z, k) + [sibling])

    def quarter(ref):
        return lambda zz: ref.at[:, pl.ds(pl.multiple_of(zz * 256, 256), 256)]

    spread = [
        (lambda zz: meta, meta_all),
        (quarter(wq), wq_all), (quarter(wk), wk_all), (quarter(wv), wv_all),
        (lambda zz: wo, wo_all),
        (lambda zz: wg.at[zz], wg_all), (lambda zz: wu.at[zz], wu_all),
    ]
    gather = [(x, x_all), (cot, cot_all)]
    sends, local = [], []

    def start(copy):
        copy.start()
        sends.append(copy)

    base = 0
    for i, (src, dst) in enumerate(gather):
        mine = pltpu.make_async_copy(src, dst.at[z], lsem.at[i])
        mine.start()
        local.append(mine)
        for d in range(1, 4):
            n = base + d - 1
            start(remote(src, dst.at[z], ssem.at[n], rsem.at[n], device(c, lax.rem(z + d, 4), k)))
        base += 3
    first = base
    for i, (src, dst) in enumerate(spread):
        mine = pltpu.make_async_copy(src(z), dst.at[f], lsem.at[2 + i])
        mine.start()
        local.append(mine)
        for d in range(1, 4):
            n = base + d - 1
            zz = lax.rem(z + d, 4)
            start(remote(src(zz), dst.at[f], ssem.at[n], rsem.at[n], device(c, zz, k)))
        start(remote(src(z), dst.at[f], ssem.at[base + 3], rsem.at[base + 3], sibling))
        base += 7
    for i, (src, dst) in enumerate([(wd, wd_all), (pers, pers_all)]):
        mine = pltpu.make_async_copy(src, dst.at[k], lsem.at[9 + i])
        mine.start()
        local.append(mine)
        start(remote(src, dst.at[k], ssem.at[base], rsem.at[base], sibling))
        base += 1
    landed = []
    for i, (src, dst) in enumerate(spread):
        b = first + 7 * i
        for d in range(1, 4):
            n = b + 3 + d
            slot = dst.at[2 * lax.rem(z - d + 4, 4) + k]
            remote(slot, slot, ssem.at[b + d - 1], rsem.at[b + d - 1], sibling).wait_recv()
            start(remote(slot, slot, ssem.at[n], rsem.at[n], sibling))
            landed.append((slot, n))
        landed.append((dst.at[f], b + 3))
    for i, (src, dst) in enumerate(gather):
        for d in range(1, 4):
            landed.append((dst.at[z], 3 * i + d - 1))
    landed += [(wd_all.at[k], base - 2), (pers_all.at[k], base - 1)]
    for slot, n in landed:
        remote(slot, slot, ssem.at[n], rsem.at[n], sibling).wait_recv()
    for copy in sends:
        copy.wait_send()
    for copy in local:
        copy.wait()


def ctx_swap_kernel(n, *refs):
    srcs, dsts = refs[:n], refs[n : 2 * n]
    ssem, rsem, lsem = refs[2 * n :]
    c, z, k = coords()
    steps = [(at_ctx(c, dx, dy)) for dx, dy in CTX_STEPS]
    meet([device(cc, z, k) for cc in steps])
    sends, local = [], []
    for i, (src, dst) in enumerate(zip(srcs, dsts)):
        mine = pltpu.make_async_copy(src.at[c], dst.at[c], lsem.at[i])
        mine.start()
        local.append(mine)
    for j, cc in enumerate(steps):
        for i, (src, dst) in enumerate(zip(srcs, dsts)):
            s = j * n + i
            copy = remote(src.at[cc], dst.at[c], ssem.at[s], rsem.at[s], device(cc, z, k))
            copy.start()
            sends.append(copy)
    for copy in sends:
        copy.wait()
    for copy in local:
        copy.wait()


def ctx_swap(cid, name, *operands):
    n = len(operands)
    return comm_call(
        functools.partial(ctx_swap_kernel, n), name, cid, like(*[o.shape for o in operands]), 15 * n, *operands
    )


def z_swap_kernel(n, gather, *refs):
    srcs, dsts = refs[:n], refs[n : 2 * n]
    ssem, rsem, lsem = refs[2 * n :]
    c, z, k = coords()
    meet(z_peers(c, z, k))
    sends, local = [], []
    for i, (src, dst) in enumerate(zip(srcs, dsts)):
        mine = pltpu.make_async_copy(src if gather else src.at[z], dst.at[z], lsem.at[i])
        mine.start()
        local.append(mine)
        for d in range(1, 4):
            s = 3 * i + d - 1
            zz = lax.rem(z + d, 4)
            copy = remote(
                src if gather else src.at[zz], dst.at[z], ssem.at[s], rsem.at[s], device(c, zz, k)
            )
            copy.start()
            sends.append(copy)
    for copy in sends:
        copy.wait()
    for copy in local:
        copy.wait()


def z_swap(cid, name, *operands, gather=False):
    n = len(operands)
    return comm_call(
        functools.partial(z_swap_kernel, n, gather),
        name,
        cid,
        like(*[(4, *o.shape) if gather else o.shape for o in operands]),
        3 * n,
        *operands,
    )


def mixed_home_kernel(mixed, tok, quart, ssem, rsem, lsem):
    c, z, k = coords()
    hb, zs, sb = pair_of(c)
    head = 2 * z + hb
    spots = [c] + [at_ctx(c, dx, dy) for dx, dy in CTX_STEPS]
    senders = [device(hb2 * 8 + z * 2 + sb2, zz, k) for zz in range(4) for hb2 in range(2) for sb2 in range(2)]
    here = zs == z
    barrier = pltpu.get_barrier_semaphore()

    for zz in range(4):
        for hb2 in range(2):
            for sb2 in range(2):
                cc = hb2 * 8 + z * 2 + sb2

                @pl.when(jnp.logical_not((cc == c) & (zz == z)))
                def _():
                    pl.semaphore_signal(barrier, inc=1, device_id=device(cc, zz, k), device_id_type=MESH)

    for cc in spots[1:]:
        pl.semaphore_signal(barrier, inc=1, device_id=device(cc, z, k), device_id_type=MESH)
    pl.semaphore_wait(barrier, jnp.where(here, 30, 31))
    slot = head * 2 + sb

    def home(j):
        return remote(
            mixed.at[spots[j]], tok.at[slot], ssem.at[j], rsem.at[slot], device(spots[j], zs, k)
        )

    @pl.when(here)
    def _():
        pltpu.make_async_copy(mixed.at[c], tok.at[slot], rsem.at[slot]).start()

    @pl.when(jnp.logical_not(here))
    def _():
        home(0).start()

    mine = pltpu.make_async_copy(mixed.at[c], quart.at[c], lsem.at[0])
    mine.start()
    others = []
    for j in range(1, 16):
        home(j).start()
    for j in range(1, 16):
        copy = remote(
            mixed.at[spots[j]], quart.at[c], ssem.at[15 + j], rsem.at[15 + j], device(spots[j], z, k)
        )
        copy.start()
        others.append(copy)
    for n in range(16):
        remote(tok.at[n], tok.at[n], ssem.at[0], rsem.at[n], device(c, z, k)).wait_recv()
    for copy in others:
        copy.wait()

    @pl.when(jnp.logical_not(here))
    def _():
        home(0).wait_send()

    for j in range(1, 16):
        home(j).wait_send()
    mine.wait()


def mixed_home(cid, mixed):
    return comm_call(mixed_home_kernel, "mixed_home", cid, like((16, 64, 128), (16, 64, 128)), 32, mixed)


def grads_out_kernel(dmix, branch, blocks, branch_all, ssem, rsem, lsem):
    c, z, k = coords()
    hb, zs, sb = pair_of(c)
    here = zs == z
    barrier = pltpu.get_barrier_semaphore()
    spots = [c] + [at_ctx(c, dx, dy) for dx, dy in CTX_STEPS]
    for cc in spots[1:]:
        pl.semaphore_signal(barrier, inc=1, device_id=device(cc, zs, k), device_id_type=MESH)

    @pl.when(jnp.logical_not(here))
    def _():
        pl.semaphore_signal(barrier, inc=1, device_id=device(c, zs, k), device_id_type=MESH)

    for peer in z_peers(c, z, k):
        pl.semaphore_signal(barrier, inc=1, device_id=peer, device_id_type=MESH)
    pl.semaphore_wait(barrier, jnp.where(here, 18, 19))
    mine_is = [((hb2 * 8 + z * 2 + sb2) == c) for hb2 in range(2) for sb2 in range(2)]
    mine = pltpu.make_async_copy(branch, branch_all.at[z], lsem.at[0])
    mine.start()
    sends = []
    for d in range(4):
        zz = lax.rem(z + d, 4)
        for i in range(4):
            hb2, sb2 = i // 2, i % 2
            n = 4 * d + i
            src = dmix.at[(2 * zz + hb2) * 2 + sb2]
            copy = remote(
                src, blocks.at[c], ssem.at[n], rsem.at[c], device(hb2 * 8 + z * 2 + sb2, zz, k)
            )
            if d:
                copy.start()
                sends.append((None, copy))
            else:

                @pl.when(mine_is[i])
                def _():
                    pltpu.make_async_copy(src, blocks.at[c], rsem.at[c]).start()

                @pl.when(jnp.logical_not(mine_is[i]))
                def _():
                    copy.start()

                sends.append((mine_is[i], copy))
    for d in range(1, 4):
        copy = remote(
            branch, branch_all.at[z], ssem.at[15 + d], rsem.at[15 + d], device(c, lax.rem(z + d, 4), k)
        )
        copy.start()
        sends.append((None, copy))
    for n in range(16):
        remote(blocks.at[n], blocks.at[n], ssem.at[0], rsem.at[n], device(c, z, k)).wait_recv()
    for d in range(1, 4):
        remote(branch, branch_all.at[z], ssem.at[0], rsem.at[15 + d], device(c, z, k)).wait_recv()
    for local, copy in sends:
        if local is None:
            copy.wait_send()
        else:

            @pl.when(jnp.logical_not(local))
            def _():
                copy.wait_send()

    mine.wait()


def grads_out(cid, dmix, branch):
    return comm_call(
        grads_out_kernel, "grads_out", cid, like((16, 64, 128), (4, 128, 1024)), 32, dmix, branch
    )


def core_swap_kernel(n, *refs):
    srcs, dsts = refs[:n], refs[n : 2 * n]
    ssem, rsem, lsem = refs[2 * n :]
    c, z, k = coords()
    sibling = device(c, z, 1 - k)
    meet([sibling])
    sends = []
    for i, (src, dst) in enumerate(zip(srcs, dsts)):
        part = src.at[1 - k] if len(src.shape) == 3 else src.at[:, 1 - k]
        copy = remote(part, dst, ssem.at[i], rsem.at[i], sibling)
        copy.start()
        sends.append(copy)
    for copy in sends:
        copy.wait()


def core_swap(cid, name, *operands):
    n = len(operands)
    shapes = [o.shape[1:] if o.ndim == 3 else (o.shape[0], *o.shape[2:]) for o in operands]
    return comm_call(functools.partial(core_swap_kernel, n), name, cid, like(*shapes), n, *operands)


def reduce_kernel(gu, qkv, down, out, gu_in, qkv_in, down_in, out_in, ssem, rsem, lsem):
    c, z, k = coords()
    steps = [(at_ctx(c, dx, dy)) for dx, dy in CTX_STEPS]
    meet([device(cc, z, k) for cc in steps])

    def pieces(cc):
        rg, h = lax.div(cc, 2), lax.rem(cc, 2)
        rows = pl.ds(pl.multiple_of(rg * 16, 16), 16)
        return [
            (gu.at[h, :, rows, :], gu_in.at[c]),
            (qkv.at[:, rows, pl.ds(pl.multiple_of(h * 384, 384), 384)], qkv_in.at[c]),
            (
                down.at[pl.ds(pl.multiple_of(h * 176, 16), 176), pl.ds(pl.multiple_of(rg * 128, 128), 128)],
                down_in.at[c],
            ),
            (out.at[rows, pl.ds(pl.multiple_of(h * 512, 512), 512)], out_in.at[c]),
        ]

    sends, local = [], []
    for i, (src, dst) in enumerate(pieces(c)):
        mine = pltpu.make_async_copy(src, dst, lsem.at[i])
        mine.start()
        local.append(mine)
    for j, cc in enumerate(steps):
        for i, (src, dst) in enumerate(pieces(cc)):
            n = 4 * j + i
            copy = remote(src, dst, ssem.at[n], rsem.at[n], device(cc, z, k))
            copy.start()
            sends.append(copy)
    for copy in sends:
        copy.wait()
    for copy in local:
        copy.wait()


def reduce_ctx(cid, gu, qkv, down, out):
    return comm_call(
        reduce_kernel,
        "reduce_ctx",
        cid,
        like((16, 4, 16, 768), (16, 4, 16, 384), (16, 176, 128), (16, 16, 512)),
        60,
        gu, qkv, down, out,
    )


def ctx_gather_kernel(n, *refs):
    srcs, dsts = refs[:n], refs[n : 2 * n]
    ssem, rsem, lsem = refs[2 * n :]
    c, z, k = coords()
    steps = [(at_ctx(c, dx, dy)) for dx, dy in CTX_STEPS]
    meet([device(cc, z, k) for cc in steps])
    sends, local = [], []
    for i, (src, dst) in enumerate(zip(srcs, dsts)):
        mine = pltpu.make_async_copy(src, dst.at[c], lsem.at[i])
        mine.start()
        local.append(mine)
    for j, cc in enumerate(steps):
        for i, (src, dst) in enumerate(zip(srcs, dsts)):
            s = j * n + i
            copy = remote(src, dst.at[c], ssem.at[s], rsem.at[s], device(cc, z, k))
            copy.start()
            sends.append(copy)
    for copy in sends:
        copy.wait()
    for copy in local:
        copy.wait()


def ctx_gather(cid, name, *operands):
    n = len(operands)
    return comm_call(
        functools.partial(ctx_gather_kernel, n),
        name,
        cid,
        like(*[(16, *o.shape) for o in operands]),
        15 * n,
        *operands,
    )


def unit_rows(rows):
    r = lax.rsqrt(jnp.mean(rows * rows, axis=-1, keepdims=True) + EPS)
    return rows * r * SCALE, r


def unit_back(rows, r, grad):
    return SCALE * (r * grad - rows * (r * r * r) * jnp.mean(rows * grad, axis=-1, keepdims=True))


def plan_rows(c, z, k, meta, qkv):
    hb, zs, sb = pair_of(c)
    head = 2 * z + hb
    length = meta[2 * zs + k, pl.ds(2 + sb, 1), :][:, :1]
    decay = meta[0, pl.ds(8 + head, 1), :]
    moment = meta[0, pl.ds(16 + head, 1), :]
    for f in range(1, 8):
        decay += meta[f, pl.ds(8 + head, 1), :]
        moment += meta[f, pl.ds(16 + head, 1), :]
    plan = qkv[:, 192:208, :].astype(f32)
    lanes = lax.broadcasted_iota(jnp.int32, (16, 128), 1).astype(f32)
    decay_pick = jnp.where(plan[:, 0, :] == lanes, 1.0, 0.0)
    moment_pick = jnp.where(plan[:, 1, :] == lanes, 1.0, 0.0)
    retention = jax.nn.sigmoid(jnp.sum(decay_pick * decay, axis=1, keepdims=True))
    momentum = jax.nn.sigmoid(jnp.sum(moment_pick * moment, axis=1, keepdims=True))
    return length, decay_pick, moment_pick, retention, momentum


def live_rows(length):
    places = lax.broadcasted_iota(jnp.int32, (1024, 1), 0).astype(f32)
    return jnp.where(places < length, 1.0, 0.0)


def pair_forward_kernel(
    qkv, pers, meta, mixed, probs, own, m0, s0, outer, q_u, k_u, vals, both, rate_f, rate_m, reads
):
    c, z, k = coords()
    hb = pair_of(c)[0]
    length, _, _, retention, momentum = plan_rows(c, z, k, meta, qkv)
    rate_f[...] = jnp.broadcast_to(retention, (16, 128))
    rate_m[...] = jnp.broadcast_to(momentum, (16, 128))
    q = qkv[:, 0:64, :].reshape(1024, 128)
    kk = qkv[:, 64:128, :].reshape(1024, 128)
    v = qkv[:, 128:192, :].reshape(1024, 128)
    live = live_rows(length)
    q_u[...] = unit_rows(q.astype(f32))[0]
    k_u[...] = unit_rows(kk.astype(f32))[0] * live
    vals[...] = v.astype(f32)
    for b in range(16):
        rows = slice(64 * b, 64 * b + 64)
        ku = k_u[rows, :]
        both[b] = tn(ku, jnp.concatenate([ku, vals[rows, :]], axis=1), HIGHEST)
        outer[b] = both[b, :, :128]
    memory = jnp.zeros((128, 128), f32)
    velocity = jnp.zeros((128, 128), f32)
    for b in range(16):
        m0[b] = memory
        s0[b] = velocity
        rows = slice(64 * b, 64 * b + 64)
        stacked = jnp.concatenate([q_u[rows, :], both[b, :, :128]], axis=0)
        got = nn(stacked, memory, HIGHEST)
        reads[rows, :] = got[:64]
        surprise = got[64:] - both[b, :, 128:]
        velocity = rate_m[b : b + 1, :] * velocity - RATE * surprise
        memory = rate_f[b : b + 1, :] * memory + velocity
    pk = pers[hb, 0]
    pv = pers[hb, 1]
    for i in range(4):
        span = 256 * (i + 1)
        qs = slice(256 * i, span)
        scores = nt(kk[:span], q[qs]) * SCALE
        own_scores = nt(pk, q[qs]) * SCALE
        key_at = lax.broadcasted_iota(jnp.int32, (span, 256), 0)
        query_at = lax.broadcasted_iota(jnp.int32, (span, 256), 1) + 256 * i
        allowed = (key_at <= query_at) & (key_at.astype(f32) < length)
        scores = jnp.where(allowed, scores, -1e30)
        top = jnp.maximum(
            jnp.max(scores, axis=0, keepdims=True), jnp.max(own_scores, axis=0, keepdims=True)
        )
        e = jnp.exp(scores - top)
        own_e = jnp.exp(own_scores - top)
        total = jnp.sum(e, axis=0, keepdims=True) + jnp.sum(own_e, axis=0, keepdims=True)
        p = (e / total).astype(bf16)
        own_p = (own_e / total).astype(bf16)
        probs[:span, qs] = p
        own[:, qs] = own_p
        att = tn(v[:span], p) + tn(pv, own_p)
        mixed[4 * i : 4 * i + 4] = (att.T + reads[qs, :]).astype(bf16).reshape(4, 64, 128)


def vmem_call(body, name, out_shapes, scratch, *operands):
    return pl.pallas_call(
        body,
        out_shape=out_shapes,
        in_specs=[pl.BlockSpec(memory_space=pltpu.VMEM)] * len(operands),
        out_specs=jax.tree.map(lambda _: pl.BlockSpec(memory_space=pltpu.VMEM), out_shapes),
        scratch_shapes=scratch,
        compiler_params=pltpu.CompilerParams(vmem_limit_bytes=VMEM_LIMIT),
        name=name,
    )(*operands)


def pair_forward(qkv, pers, meta):
    return vmem_call(
        pair_forward_kernel,
        "pair_forward",
        like((16, 64, 128), (1024, 1024), (16, 1024))
        + like((16, 128, 128), (16, 128, 128), (16, 128, 128), dtype=f32),
        [
            pltpu.VMEM((1024, 128), f32),
            pltpu.VMEM((1024, 128), f32),
            pltpu.VMEM((1024, 128), f32),
            pltpu.VMEM((16, 128, 256), f32),
            pltpu.VMEM((16, 128), f32),
            pltpu.VMEM((16, 128), f32),
            pltpu.VMEM((1024, 128), f32),
        ],
        qkv, pers, meta,
    )


def pair_backward_kernel(
    qkv, dmix, pers, meta, probs, own, m0, s0, outer,
    dqkv, d_own, d_plan,
    dq_s, dk_s, dv_s, adj, rate_f, rate_m,
):
    c, z, k = coords()
    hb = pair_of(c)[0]
    length, decay_pick, moment_pick, retention, momentum = plan_rows(c, z, k, meta, qkv)
    rate_f[...] = jnp.broadcast_to(retention, (16, 128))
    rate_m[...] = jnp.broadcast_to(momentum, (16, 128))
    q = qkv[:, 0:64, :].reshape(1024, 128)
    kk = qkv[:, 64:128, :].reshape(1024, 128)
    v = qkv[:, 128:192, :].reshape(1024, 128)
    dm = dmix[...].reshape(1024, 128)
    pk = pers[hb, 0]
    pv = pers[hb, 1]
    live = live_rows(length)
    qf, kf, vf, dmf = (a.astype(f32) for a in (q, kk, v, dm))
    q_u, q_r = unit_rows(qf)
    k_u, k_r = unit_rows(kf)
    k_l = k_u * live

    dk_s[...] = jnp.zeros_like(dk_s)
    dv_s[...] = jnp.zeros_like(dv_s)
    d_pk = jnp.zeros((16, 128), f32)
    d_pv = jnp.zeros((16, 128), f32)
    for i in range(4):
        span = 256 * (i + 1)
        qs = slice(256 * i, span)
        p = probs[:span, qs]
        own_p = own[:, qs]
        dp = nt(v[:span], dm[qs])
        own_dp = nt(pv, dm[qs])
        pf, own_pf = p.astype(f32), own_p.astype(f32)
        delta = jnp.sum(pf * dp, axis=0, keepdims=True) + jnp.sum(
            own_pf * own_dp, axis=0, keepdims=True
        )
        ds = (pf * (dp - delta)).astype(bf16)
        own_ds = (own_pf * (own_dp - delta)).astype(bf16)
        dq = tn(kk[:span], ds) + tn(pk, own_ds)
        dq_s[qs, :] = dq.T * SCALE
        dk_s[:span, :] += nn(ds, q[qs]) * SCALE
        dv_s[:span, :] += nn(p, dm[qs])
        d_pk += nn(own_ds, q[qs]) * SCALE
        d_pv += nn(own_p, dm[qs])
    d_own[0] = d_pk
    d_own[1] = d_pv

    adj_m = jnp.zeros((128, 128), f32)
    adj_v = jnp.zeros((128, 128), f32)
    d_decay = jnp.zeros((1, 128), f32)
    d_moment = jnp.zeros((1, 128), f32)
    for b in reversed(range(16)):
        rows = slice(64 * b, 64 * b + 64)
        total = adj_m + adj_v
        adj[b] = total
        g_f = jnp.sum(adj_m * m0[b])
        g_m = jnp.sum(total * s0[b])
        f_row, m_row = rate_f[b : b + 1, :], rate_m[b : b + 1, :]
        d_decay += decay_pick[b : b + 1, :] * (g_f * f_row * (1.0 - f_row))
        d_moment += moment_pick[b : b + 1, :] * (g_m * m_row * (1.0 - m_row))
        adj_m = (
            f_row * adj_m
            - RATE * nn(outer[b], total, HIGHEST)
            + tn(q_u[rows], dmf[rows], HIGHEST)
        )
        adj_v = m_row * total
    d_plan[...] = jnp.concatenate([d_decay, d_moment, jnp.zeros((6, 128), f32)], axis=0)
    for b in range(16):
        rows = slice(64 * b, 64 * b + 64)
        total = adj[b]
        d_outer = -RATE * nt(total, m0[b], HIGHEST)
        d_qu = nt(dmf[rows], m0[b], HIGHEST)
        d_kl = nn(k_l[rows], d_outer + d_outer.T, HIGHEST) + RATE * nt(vf[rows], total, HIGHEST)
        d_v = RATE * nn(k_l[rows], total, HIGHEST)
        dq = dq_s[rows, :] + unit_back(qf[rows], q_r[rows], d_qu)
        dk = dk_s[rows, :] + unit_back(kf[rows], k_r[rows], d_kl * live[rows])
        dv = dv_s[rows, :] + d_v
        dqkv[b, 0:64, :] = dq.astype(bf16)
        dqkv[b, 64:128, :] = dk.astype(bf16)
        dqkv[b, 128:192, :] = dv.astype(bf16)


def pair_backward(qkv, dmix, pers, meta, probs, own, m0, s0, outer):
    return vmem_call(
        pair_backward_kernel,
        "pair_backward",
        like((16, 192, 128)) + like((2, 16, 128), (8, 128), dtype=f32),
        [
            pltpu.VMEM((1024, 128), f32),
            pltpu.VMEM((1024, 128), f32),
            pltpu.VMEM((1024, 128), f32),
            pltpu.VMEM((16, 128, 128), f32),
            pltpu.VMEM((16, 128), f32),
            pltpu.VMEM((16, 128), f32),
        ],
        qkv, dmix, pers, meta, probs, own, m0, s0, outer,
    )


def scaled(values):
    return lax.rsqrt(jnp.mean(values * values, axis=-1, keepdims=True) + EPS)


def norm_back(values, gain, grad):
    r = scaled(values)
    inner = grad * gain
    back = r * inner - (r * r * r) * values * jnp.mean(values * inner, axis=-1, keepdims=True)
    return back, jnp.sum(grad * values * r, axis=0)


def shards(
    inputs, gain_attn, w_query, w_key, w_value, w_out, persist_key, persist_value, gain_ffn,
    w_gate, w_up, w_down, decay_table, momentum_table, lengths, decay_index, momentum_index,
    cotangent,
):
    c, z, k = coords()
    f = 2 * z + k
    hb, zs, sb = pair_of(c)
    x = inputs.reshape(128, 1024)
    lanes = jnp.arange(128)

    def wide(v):
        return jnp.broadcast_to(v.reshape(2, 1).astype(f32), (2, 128))

    def placed(table):
        t = table.astype(f32)
        return sum(t[r][:, None] * (lanes[None, :] == 2 * f + r) for r in range(2))

    meta = jnp.concatenate(
        [
            gain_attn[None].astype(f32), gain_ffn[None].astype(f32), wide(lengths),
            wide(decay_index), wide(momentum_index), placed(decay_table), placed(momentum_table),
        ],
        axis=0,
    )

    def quarters(w):
        return jnp.pad(w.reshape(128, 4, 704).swapaxes(0, 1), ((0, 0), (0, 0), (0, 64)))

    (
        x_all, cot_all, meta_all, wq, wk, wv, wo, wg, wu, wd, pers,
    ) = comm_call(
        front_kernel,
        "front",
        1,
        like((4, 128, 1024), (4, 128, 1024))
        + like((8, 24, 128), dtype=f32)
        + like(*[(8, 128, 256)] * 3, (8, 128, 1024), *[(8, 128, 768)] * 2, (2, 352, 1024), (2, 2, 16, 128)),
        64,
        x, cotangent.reshape(128, 1024), meta, w_query, w_key, w_value, w_out,
        quarters(w_gate), quarters(w_up), w_down, jnp.stack([persist_key, persist_value]),
    )
    gain_one = meta_all[:, 0, :].reshape(1024)
    gain_two = meta_all[:, 1, :].reshape(1024)
    by_z = lax.dynamic_index_in_dim(meta_all.reshape(4, 2, 24, 128), k, 1, keepdims=False)
    places = c * 64 + jnp.arange(64)
    live = (places[None, None, :] < by_z[:, 2:4, :1]).astype(f32)

    xf = x_all.reshape(512, 1024).astype(f32)
    normed = (xf * scaled(xf) * gain_one).astype(bf16)
    w_qkv = jnp.concatenate([w.reshape(1024, 256) for w in (wq, wk, wv)], axis=1)
    qkv = nn(normed, w_qkv).astype(bf16)
    rows = qkv.reshape(4, 2, 64, 3, 2, 128).transpose(4, 0, 1, 3, 2, 5).reshape(16, 192, 128)
    plan = by_z[:, 4:8, :].reshape(4, 2, 2, 128).swapaxes(1, 2).astype(bf16)
    plan = jnp.pad(jnp.broadcast_to(plan[None], (2, 4, 2, 2, 128)).reshape(16, 2, 128), ((0, 0), (0, 14), (0, 0)))
    (pair,) = ctx_swap(2, "qkv_out", jnp.concatenate([rows, plan], axis=1))

    mixed, probs, own, m0, s0, outer = pair_forward(pair, pers, meta_all)
    mix_tok, mix_quart = mixed_home(3, mixed)
    mix_tok = mix_tok.reshape(8, 2, 64, 128).transpose(1, 2, 0, 3).reshape(128, 1024)
    mix_quart = mix_quart.reshape(2, 4, 2, 64, 128).transpose(1, 2, 3, 0, 4).reshape(512, 256)

    w_o = wo.reshape(1024, 1024)
    xt = x.astype(f32)
    resid = xt + nn(mix_tok, w_o)
    nf = (resid * scaled(resid) * gain_two).astype(bf16)
    (nf_all,) = z_swap(4, "ffn_gather", nf, gather=True)
    nf_all = nf_all.reshape(512, 1024)
    w_g, w_u = wg.reshape(1024, 768), wu.reshape(1024, 768)
    w_d = jnp.pad(wd.reshape(704, 1024), ((0, 64), (0, 0)))
    g, u = nn(nf_all, w_g), nn(nf_all, w_u)
    s = jax.nn.sigmoid(g)
    hidden = (g * s * u).astype(bf16)
    out_part = nn(hidden, w_d).astype(bf16)
    od = (cot_all.reshape(4, 2, 64, 1024).astype(f32) * live[..., None]).astype(bf16).reshape(512, 1024)
    dh = nt(od, w_d)
    d_g = (dh * u * s * (1.0 + g * (1.0 - s))).astype(bf16)
    d_u = (dh * g * s).astype(bf16)
    nf_part = (nt(d_g, w_g) + nt(d_u, w_u)).astype(bf16)
    out_in, nf_in = z_swap(5, "ffn_scatter", out_part.reshape(4, 128, 1024), nf_part.reshape(4, 128, 1024))
    output = (resid + jnp.sum(out_in.astype(f32), axis=0)).astype(bf16)
    d_nf = jnp.sum(nf_in.astype(f32), axis=0)
    out_grad = cotangent.reshape(128, 1024).astype(f32) * lax.dynamic_index_in_dim(
        live, z, 0, keepdims=False
    ).reshape(128, 1)
    back, g_gain_two = norm_back(resid, gain_two, d_nf)
    d_resid = out_grad + back
    d_branch = d_resid.astype(bf16)
    dmix = nt(d_branch, w_o).astype(bf16).reshape(2, 64, 8, 128).transpose(2, 0, 1, 3).reshape(16, 64, 128)
    dm_blocks, branch_all = grads_out(6, dmix, d_branch)
    dqkv, d_own, d_plan = pair_backward(pair, dm_blocks, pers, meta_all, probs, own, m0, s0, outer)
    (dq_home,) = ctx_swap(7, "dqkv_home", dqkv)
    dq_rows = dq_home.reshape(2, 4, 2, 3, 64, 128).transpose(1, 2, 4, 3, 0, 5).reshape(512, 768)
    dn_part = nt(dq_rows, w_qkv).astype(bf16)
    (dn_in,) = z_swap(8, "dnormed_scatter", dn_part.reshape(4, 128, 1024))
    back, g_gain_one = norm_back(xt, gain_one, jnp.sum(dn_in.astype(f32), axis=0))
    input_grad = d_resid + back

    g_qkv = tn(normed, dq_rows).astype(bf16).reshape(4, 2, 128, 768)
    g_gate = tn(nf_all, d_g).astype(bf16).reshape(4, 2, 128, 768)
    g_up = tn(nf_all, d_u).astype(bf16).reshape(4, 2, 128, 768)
    g_down = tn(hidden, od)[:704].astype(bf16).reshape(2, 352, 1024)
    g_out = tn(mix_quart, branch_all.reshape(512, 1024)).astype(bf16).reshape(2, 128, 1024)
    other = core_swap(9, "core_swap", g_gate, g_up, g_qkv, g_down, g_out)

    def both(mine, theirs, axis):
        own_half = lax.dynamic_index_in_dim(mine, k, axis, keepdims=False)
        return (own_half.astype(f32) + theirs.astype(f32)).astype(bf16)

    gate2, up2, qkv2 = (both(m, t, 1) for m, t in zip((g_gate, g_up, g_qkv), other[:3]))
    down2, out2 = both(g_down, other[3], 0), both(g_out, other[4], 0)
    gathered = reduce_ctx(10, jnp.stack([gate2, up2]), qkv2, down2, out2)
    gu_p, qkv_p, down_p, out_p = (jnp.sum(a.astype(f32), axis=0).astype(bf16) for a in gathered)
    gu_p, qkv_p = z_swap(11, "grad_z", gu_p, qkv_p)
    gu_f, qkv_f, down_f, out_f = ctx_gather(12, "grad_gather", gu_p, qkv_p, down_p, out_p)
    gu_f = gu_f.reshape(8, 2, 4, 16, 768)[..., :704].transpose(1, 0, 3, 2, 4).reshape(2, 128, 2816).astype(f32)
    qkv_f = qkv_f.reshape(8, 2, 4, 16, 384).transpose(0, 3, 2, 1, 4).reshape(128, 4, 3, 256)
    qkv_f = qkv_f.transpose(2, 0, 1, 3).reshape(3, 128, 1024).astype(f32)
    down_f = down_f.reshape(8, 2, 176, 128).transpose(1, 2, 0, 3).reshape(352, 1024).astype(f32)
    out_f = out_f.reshape(8, 2, 16, 512).transpose(0, 2, 1, 3).reshape(128, 1024).astype(f32)

    head = 2 * z + hb
    at_head = (jnp.arange(8) == head).astype(f32)
    small = jnp.concatenate(
        [
            g_gain_one, g_gain_two,
            (at_head[:, None, None, None] * d_own[None]).reshape(-1),
            (at_head[:, None, None] * d_plan[None, :2, :16]).reshape(-1),
        ]
    )
    small = lax.psum(small, ("ctx", "fsdp"))
    own_gain_one = lax.dynamic_slice(small, (f * 128,), (128,))
    own_gain_two = lax.dynamic_slice(small, (1024 + f * 128,), (128,))
    own_pers = lax.dynamic_slice(small, (2048 + f * 4096,), (4096,)).reshape(2, 16, 128)
    tables = small[2048 + 32768 :].reshape(8, 2, 16)
    own_tables = lax.dynamic_slice(tables, (0, 0, 2 * f), (8, 2, 2)).transpose(1, 2, 0)
    return (
        output.reshape(2, 64, 1024),
        input_grad.reshape(2, 64, 1024),
        own_gain_one,
        qkv_f[0], qkv_f[1], qkv_f[2],
        out_f,
        own_pers[0], own_pers[1],
        own_gain_two,
        gu_f[0], gu_f[1],
        down_f,
        own_tables[0], own_tables[1],
    )


def solution(mesh):
    rows, cols = P("fsdp", None), P(None, "fsdp")
    tokens = P("fsdp", "ctx", None)
    in_specs = (
        tokens, P("fsdp"), rows, rows, rows, rows, cols, cols, P("fsdp"), rows, rows, rows, rows, rows,
        P("fsdp"), P("fsdp", "ctx"), P("fsdp", "ctx"), tokens,
    )
    out_specs = (
        tokens, tokens, P("fsdp"), rows, rows, rows, rows, cols, cols, P("fsdp"), rows, rows, rows, rows, rows,
    )
    return jax.shard_map(shards, mesh=mesh, in_specs=in_specs, out_specs=out_specs, check_vma=False)
```

time: 1580 us -> 488 us (0.31)
  the two profiles are of different devices: /device:TPU:0 before, /device:TPU:1 now
where the time goes in v1:
time: 488 us; the launch traced here: 478 us
  Pallas kernels  337 us (69%)
  local copies, waits for them, and re-layouts  59.5 us (12%)
  other arithmetic  27.6 us (6%)
  matrix products  26.7 us (5%)
  between operations  15.3 us (3%)
  waiting for transfers between devices  12.7 us (3%)
    pallas_call x12, Pallas kernels, comm_call(): pl.pallas_call(body, out_shape=out_shapes, in_specs=[pl.BlockSpec(memory_...  309 us
    pallas_call x2, Pallas kernels, vmem_call(): pl.pallas_call(body, out_shape=out_shapes, in_specs=[pl.BlockSpec(memory_...  27.7 us
    unnamed x112, local copies, waits for them, and re-layouts  14.7 us
    psum x1, waiting for transfers between devices, shards(): small = lax.psum(small, ('ctx', 'fsdp'))  12.6 us
    dot_general x5, matrix products, tn(): lax.dot_general(a, b, (((0,), (0,)), ((), ())), preferred_element_type=f3...  10.4 us
  transfers between devices with their start and end apart: 1, of which 1 were waited for; matrix products, arithmetic and copies ran while one was open for 12% of the time, Pallas kernels for 23%

profile of v1, /device:TPU:1, one launch (start us, length us, event | category | flops | bytes accessed | tf_op | source)
XLA Modules:
  0.0 478.3 jit_solution(10315684841721744614)
XLA Ops:
  18.8 71.6 %front.1 = (bf16[4,128,1024]{2,1,0:T(8,128)(2,1)}, bf16[4,128,1024]{2,1,0:T(8,128)(2,1)}, f32[8,24,128]{2,1,0:T(8,128)}, bf16[8,128,256]{2,1,0:T(8,128)(2,1)}, b...) custom-call(bf16[128,1024]{1,0:T(8,128)(2,1)} %bitcast.196, ...), custom_call_target="tpu_custom_call" | custom-call | tf_op jit(solution)/shard_map/front/pallas_call | solution.py:75
  96.9 16.6 %qkv_out.1.qkv = bf16[16,208,128]{2,1,0:T(8,128)(2,1)} custom-call(bf16[16,208,128]{2,1,0:T(8,128)(2,1)} %fusion.12.refs_0_), custom_call_target="tpu_custom_call" | custom-call | tf_op jit(solution)/shard_map/qkv_out/pallas_call | solution.py:75
  113.5 10.7 %pair_forward.1 = (bf16[16,64,128]{2,1,0:T(8,128)(2,1)}, bf16[1024,1024]{1,0:T(8,128)(2,1)}, bf16[16,1024]{1,0:T(8,128)(2,1)}, f32[16,128,128]{2,1,0:T(8,128)}, ...) custom-call(bf16[16,208,128]{2,1,0:T(8,128)(2,1)} %qkv_out.1.qkv, bf16[2,2,16,128]{3,2,1,0:T(8,128)(2,1)} %get-tuple-element.61.pers, ...), custom_call_target="tpu_custom_call" | custom-call | tf_op jit(solution)/shard_map/pair_forward/pallas_call | solution.py:563
  124.2 12.0 %mixed_home.1 = (bf16[16,64,128]{2,1,0:T(8,128)(2,1)}, bf16[16,64,128]{2,1,0:T(8,128)(2,1)}) custom-call(bf16[16,64,128]{2,1,0:T(8,128)(2,1)} %get-tuple-element.62.mixed), custom_call_target="tpu_custom_call" | custom-call | tf_op jit(solution)/shard_map/mixed_home/pallas_call | solution.py:75
  139.5 13.8 %ffn_gather.1 = bf16[4,128,1024]{2,1,0:T(8,128)(2,1)} custom-call(bf16[128,1024]{1,0:T(8,128)(2,1)} %multiply_convert_fusion.4.refs_0_), custom_call_target="tpu_custom_call" | custom-call | tf_op jit(solution)/shard_map/ffn_gather/pallas_call | solution.py:75
  153.3 2.8 fusion.38
  160.3 2.0 convolution_convert_fusion.4
  163.7 2.0 add_convert_fusion
  165.7 27.3 %ffn_scatter.1 = (bf16[4,128,1024]{2,1,0:T(8,128)(2,1)}, bf16[4,128,1024]{2,1,0:T(8,128)(2,1)}) custom-call(bf16[4,128,1024]{2,1,0:T(8,128)(2,1)} %bitcast.232, bf16[4,128,1024]{2,1,0:T(8,128)(2,1)} %bitcast.233), custom_call_target="tpu_custom_call" | custom-call | tf_op jit(solution)/shard_map/ffn_scatter/pallas_call | solution.py:75
  198.3 28.1 %grads_out.1 = (bf16[16,64,128]{2,1,0:T(8,128)(2,1)}, bf16[4,128,1024]{2,1,0:T(8,128)(2,1)}) custom-call(bf16[16,64,128]{2,1,0:T(8,128)(2,1)} %bitcast.235, bf16[128,1024]{1,0:T(8,128)(2,1)} %copy-done.12), custom_call_target="tpu_custom_call" | custom-call | tf_op jit(solution)/shard_map/grads_out/pallas_call | solution.py:75
  226.4 17.0 %pair_backward.1 = (bf16[16,192,128]{2,1,0:T(8,128)(2,1)}, f32[2,16,128]{2,1,0:T(8,128)}, f32[8,128]{1,0:T(8,128)}) custom-call(bf16[16,208,128]{2,1,0:T(8,128)(2,1)} %qkv_out.1.qkv, bf16[16,64,128]{2,1,0:T(8,128)(2,1)} %get-tuple-element.71.dmix, bf16[2,2,16,128]{3,2,1,0:T(8,128)(2,1)} %get-tuple-element.61.pers, f32[8,24,128]{2,1,0:T(8,128)} %get-tuple-element.57.meta, ...), custom_call_target="tpu_custom_call" | custom-call | tf_op jit(solution)/shard_map/pair_backward/pallas_call | solution.py:563
  243.4 14.8 %dqkv_home.1 = bf16[16,192,128]{2,1,0:T(8,128)(2,1)} custom-call(bf16[16,192,128]{2,1,0:T(8,128)(2,1)} %get-tuple-element.77.refs_0_), custom_call_target="tpu_custom_call" | custom-call | tf_op jit(solution)/shard_map/dqkv_home/pallas_call | solution.py:75
  258.3 2.2 copy.93
  260.8 3.5 convolution_convert_fusion.3
  264.3 13.4 %dnormed_scatter.1 = bf16[4,128,1024]{2,1,0:T(8,128)(2,1)} custom-call(bf16[4,128,1024]{2,1,0:T(8,128)(2,1)} %bitcast.234), custom_call_target="tpu_custom_call" | custom-call | tf_op jit(solution)/shard_map/dnormed_scatter/pallas_call | solution.py:75
  281.1 2.6 fusion.40
  283.8 2.2 convolution_convert_fusion.1
  286.0 2.2 convolution_convert_fusion.2
  290.8 2.2 convolution_convert_fusion
  294.3 8.9 %core_swap.1 = (bf16[4,128,768]{2,1,0:T(8,128)(2,1)}, bf16[4,128,768]{2,1,0:T(8,128)(2,1)}, bf16[4,128,768]{2,1,0:T(8,128)(2,1)}, bf16[352,1024]{1,0:T(8,128)(2,1)}, bf16[128,1024]{1,0:T(8,128)(2,1)}) custom-call(bf16[4,2,128,768]{3,2,1,0:T(8,128)(2,1)} %bitcast.203, bf16[4,2,128,768]{3,2,1,0:T(8,128)(2,1)} %bitcast.201, bf16[4,2,128,768]{3,2,1,0:T(8,128)(2,1)} %bitcast.205, ...), custom_call_target="tpu_custom_call" | custom-call | tf_op jit(solution)/shard_map/core_swap/pallas_call | solution.py:75
  305.1 2.2 fusion.10.down
  311.8 52.9 %reduce_ctx.1 = (bf16[16,4,16,768]{3,2,1,0:T(8,128)(2,1)}, bf16[16,4,16,384]{3,2,1,0:T(8,128)(2,1)}, bf16[16,176,128]{2,1,0:T(8,128)(2,1)}, bf16[16,16,512]{2,1,0:T(8,128)(2,1)}) custom-call(bf16[2,4,128,768]{3,2,1,0:T(8,128)(2,1)} %pad_maximum_fusion.1.gu, bf16[4,128,768]{2,1,0:T(8,128)(2,1)} %fusion.4.qkv, bf16[352,1024]{1,0:T(8,128)(2,1)} %fusion.10.down, ...), custom_call_target="tpu_custom_call" | custom-call | tf_op jit(solution)/shard_map/reduce_ctx/pallas_call | solution.py:75
  364.7 2.4 reduce_sum.155.refs_0_
  370.1 5.2 %grad_z.1 = (bf16[4,16,768]{2,1,0:T(8,128)(2,1)}, bf16[4,16,384]{2,1,0:T(8,128)(2,1)}) custom-call(bf16[4,16,768]{2,1,0:T(8,128)(2,1)} %reduce_sum.155.refs_0_, bf16[4,16,384]{2,1,0:T(8,128)(2,1)} %reduce_sum.156.refs_1_), custom_call_target="tpu_custom_call" | custom-call | tf_op jit(solution)/shard_map/grad_z/pallas_call | solution.py:75
  375.3 44.3 %grad_gather.1 = (bf16[16,4,16,768]{3,2,1,0:T(8,128)(2,1)}, bf16[16,4,16,384]{3,2,1,0:T(8,128)(2,1)}, bf16[16,176,128]{2,1,0:T(8,128)(2,1)}, bf16[16,16,512]{2,1,0:T(8,128)(2,1)}) custom-call(bf16[4,16,768]{2,1,0:T(8,128)(2,1)} %get-tuple-element.89.refs_0_, bf16[4,16,384]{2,1,0:T(8,128)(2,1)} %get-tuple-element.90.refs_1_, ...), custom_call_target="tpu_custom_call" | custom-call | tf_op jit(solution)/shard_map/grad_gather/pallas_call | solution.py:75
  419.6 3.1 copy.91
  422.7 4.4 reshape.432
  427.2 8.5 %slice_reduce_fusion = (f32[128,4,256]{2,1,0:T(4,128)}, f32[128,4,256]{2,1,0:T(4,128)}, f32[128,4,256]{2,1,0:T(4,128)S(1)}) fusion(f32[3,128,4,256]{3,0,2,1:T(4,128)} %bitcast.198), kind=kLoop, calls=%fused_computation.60 | loop fusion | bytes 3145728 | tf_op jit(solution)/shard_map/slice | solution.py:844
  437.5 1.9 fusion.33
  448.2 2.2 squeeze.42
  451.4 2.2 squeeze.41
  453.6 12.6 %all-reduce.6.cloned.1.call-done = f32[35072]{0:T(1024)} async-done(((f32[35072]{0:T(1024)}), f32[35072]{0:T(1024)}) %all-reduce.6.cloned.1.call-update) | async-done | bytes 140304 | tf_op jit(solution)/shard_map/psum | solution.py:834
  (210 shorter events, 65.2 us)
Async XLA Ops:
  7.2 459.1 %all-reduce.6.cloned.1.call-start = ((), (), s32[]{:S(2)}) async-start(), calls=%async_computation | async-start | bytes 286720 | tf_op jit(solution)/shard_map/psum | solution.py:834
  10.5 2.9 copy-start.30
  14.1 2.0 copy-start.38
  14.1 1.9 copy-start.39
  14.1 2.0 copy-start.36
  14.1 2.0 copy-start.37
  90.3 2.4 copy-start
  96.9 40.5 %copy-start.2 = (bf16[8,128,1024]{2,1,0:T(8,128)(2,1)S(1)}, bf16[8,128,1024]{2,1,0:T(8,128)(2,1)}, u32[]{:S(2)}) copy-start(bf16[8,128,1024]{2,1,0:T(8,128)(2,1)} %get-tuple-element.64) | copy-start | bytes 6291460
  96.9 40.5 %copy-start.5 = (bf16[2,64,1024]{2,1,0:T(8,128)(2,1)S(1)}, bf16[2,64,1024]{2,1,0:T(8,128)(2,1)}, u32[]{:S(2)}) copy-start(bf16[2,64,1024]{2,1,0:T(8,128)(2,1)} %param.18) | copy-start | bytes 786436
  153.3 2.9 copy-start.18
  153.3 2.9 copy-start.41
  157.7 2.5 copy-start.21
  160.2 2.0 copy-start.51
  160.3 2.0 copy-start.49
  160.3 3.0 copy-start.47
  258.3 2.6 copy-start.44
  260.8 3.5 copy-start.27
  264.3 15.8 %copy-start.35 = (f32[2,16,128]{2,1,0:T(8,128)S(1)}, f32[2,16,128]{2,1,0:T(8,128)}, u32[]{:S(2)}) copy-start(f32[2,16,128]{2,1,0:T(8,128)} %get-tuple-element.78) | copy-start | bytes 49156
  281.1 2.6 copy-start.19
  281.1 2.6 copy-start.48
  283.8 2.2 copy-start.50
  290.8 2.3 copy-start.22
  294.3 8.9 %copy-start.11 = (bf16[256,1024]{1,0:T(8,128)(2,1)S(1)}, bf16[256,1024]{1,0:T(8,128)(2,1)}, u32[]{:S(2)}) copy-start(bf16[256,1024]{1,0:T(8,128)(2,1)} %convolution_convert_fusion.6) | copy-start | bytes 1572868
  294.3 10.8 %copy-start.1 = (bf16[704,1024]{1,0:T(8,128)(2,1)S(1)}, bf16[704,1024]{1,0:T(8,128)(2,1)}, u32[]{:S(2)}) copy-start(bf16[704,1024]{1,0:T(8,128)(2,1)} %slice.146) | copy-start | bytes 4325380
  303.2 4.1 copy-start.10
  303.2 4.1 copy-start.26
  364.6 4.0 copy-start.32
  364.6 4.7 copy-start.29
  427.2 8.5 %copy-start.31 = (bf16[16,176,128]{2,1,0:T(8,128)(2,1)S(1)}, bf16[16,176,128]{2,1,0:T(8,128)(2,1)}, u32[]{:S(2)}) copy-start(bf16[16,176,128]{2,1,0:T(8,128)(2,1)} %get-tuple-element.96) | copy-start | bytes 2162692
  437.5 2.0 copy-start.13
  440.5 2.2 copy-start.14
  448.2 2.2 copy-start.6
  (21 other events, 28.6 us)
Sparse Core Ops, SparseCore 0:
  281.2 185.0 all-reduce.5

commit v2 on v0

v2 whole, which is shorter than its diff:
```python
import functools

import jax
import jax.numpy as jnp
from jax import lax
from jax.experimental import pallas as pl
from jax.experimental.pallas import tpu as pltpu
from jax.sharding import PartitionSpec as P

MESH = pl.DeviceIdType.MESH
HIGHEST = lax.Precision.HIGHEST
bf16, f32 = jnp.bfloat16, jnp.float32
EPS = 1e-06
RATE = 0.1
SCALE = 128**-0.5
VMEM_LIMIT = 63 << 20
SEMS = (90, 97, 13)


def coords():
    c, f = lax.axis_index("ctx"), lax.axis_index("fsdp")
    return c, lax.div(f, 2), lax.rem(f, 2)


def pair_of(c):
    return lax.div(c, 8), lax.rem(lax.div(c, 2), 4), lax.rem(c, 2)


def at_ctx(c, dx, dy):
    x, y = lax.div(c, 4), lax.rem(c, 4)
    return lax.rem(x + dx, 4) * 4 + lax.rem(y + dy, 4)


CTX_STEPS = [(dx, dy) for dx in range(4) for dy in range(4) if dx or dy]
CTX_STEPS.sort(key=lambda s: -(min(s[0], 4 - s[0]) + min(s[1], 4 - s[1])))
Z_STEPS = (1, 3, 2)


def device(c, z, k):
    return (c, 2 * z + k)


def nn(a, b, precision=None):
    return jnp.dot(a, b, preferred_element_type=f32, precision=precision)


def nt(a, b, precision=None):
    return lax.dot_general(
        a, b, (((1,), (1,)), ((), ())), preferred_element_type=f32, precision=precision
    )


def tn(a, b, precision=None):
    return lax.dot_general(
        a, b, (((0,), (0,)), ((), ())), preferred_element_type=f32, precision=precision
    )


def ds(index, size):
    return pl.ds(pl.multiple_of(index * size, size), size)


def remote(src, dst, ssem, rsem, peer):
    return pltpu.make_async_remote_copy(
        src_ref=src, dst_ref=dst, send_sem=ssem, recv_sem=rsem, device_id=peer, device_id_type=MESH
    )


class Net:
    def __init__(self, ssem, rsem, lsem, here):
        self.ssem, self.rsem, self.lsem, self.here = ssem, rsem, lsem, here
        self.s = self.r = self.l = 0
        self.due = []

    def slots(self, n=1):
        self.r += n
        return self.r - n

    def send(self, moves, size, r, s=None):
        if s is None:
            s = self.group(size)
        for src, dst, peer, *own in moves:
            at = own[0] if own else r
            remote(src, dst, self.ssem.at[s], self.rsem.at[at], peer).start()
        return s

    def group(self, size):
        s = self.s
        self.s += 1
        self.due.append((size, s))
        return s

    def own(self, src, dst, r):
        pltpu.make_async_copy(src, dst, self.rsem.at[r]).start()

    def landed(self, size, r):
        remote(size, size, self.ssem.at[0], self.rsem.at[r], self.here).wait_recv()

    def local(self, src, dst):
        copy = pltpu.make_async_copy(src, dst, self.lsem.at[self.l])
        self.l += 1
        copy.start()
        return copy

    def drain(self, count=None):
        count = len(self.due) if count is None else count
        for size, s in self.due[:count]:
            remote(size, size, self.ssem.at[s], self.rsem.at[0], self.here).wait_send()
        self.due = self.due[count:]


def scaled(values):
    return lax.rsqrt(jnp.mean(values * values, axis=-1, keepdims=True) + EPS)


def norm_back(values, gain, grad):
    r = scaled(values)
    inner = grad * gain
    back = r * inner - (r * r * r) * values * jnp.mean(values * inner, axis=-1, keepdims=True)
    return back, jnp.sum(grad * values * r, axis=0, keepdims=True)


def unit_rows(rows):
    r = lax.rsqrt(jnp.mean(rows * rows, axis=-1, keepdims=True) + EPS)
    return rows * r * SCALE, r


def unit_back(rows, r, grad):
    return SCALE * (r * grad - rows * (r * r * r) * jnp.mean(rows * grad, axis=-1, keepdims=True))


class Shared:
    def __init__(self, net, first, zdim, part1, part2, src, r1, t1, r2, t2, zr, final):
        self.net, self.first, self.zdim = net, first, zdim
        self.part1, self.part2 = part1, part2
        self.src, self.r1, self.t1, self.r2, self.t2, self.zr, self.final = src, r1, t1, r2, t2, zr, final
        self.slot = net.slots(5)

    def place(self, c, z, k):
        x, y = lax.div(c, 4), lax.rem(c, 4)
        self.c, self.z, self.k = c, z, k
        self.i, self.j = (x, y) if self.first == "x" else (y, x)

    def peer(self, second, d):
        along_x = (self.first == "x") != second
        return device(at_ctx(self.c, d if along_x else 0, 0 if along_x else d), self.z, self.k)

    def step1(self):
        self.net.send(
            [
                (self.src.at[self.part1(lax.rem(self.i + d, 4))], self.r1.at[d - 1], self.peer(False, d))
                for d in (2, 1, 3)
            ],
            self.r1,
            self.slot,
        )

    def step2(self):
        self.net.landed(self.r1, self.slot)
        total = self.src[self.part1(self.i)].astype(f32)
        for d in range(3):
            total += self.r1[d].astype(f32)
        self.t1[...] = total.astype(bf16)
        self.net.send(
            [
                (self.t1.at[self.part2(lax.rem(self.j + d, 4))], self.r2.at[d - 1], self.peer(True, d))
                for d in (2, 1, 3)
            ],
            self.r2,
            self.slot + 1,
        )

    def step3(self):
        self.net.landed(self.r2, self.slot + 1)
        total = self.t1[self.part2(self.j)].astype(f32)
        for d in range(3):
            total += self.r2[d].astype(f32)
        self.t2[...] = total.astype(bf16)
        if self.zdim:
            self.zr[self.z] = self.t2[self.z]
            moves = []
            for d in (2, 1, 3):
                zz = lax.rem(self.z + d, 4)
                moves.append((self.t2.at[zz], self.zr.at[self.z], device(self.c, zz, self.k)))
            self.net.send(moves, self.zr.at[pl.ds(0, 3)], self.slot + 2)

    def block(self, i):
        return self.final.at[self.part1_final(i)]

    def piece(self, i, j):
        return self.final.at[self.piece_final(i, j)]

    def step4(self):
        if self.zdim:
            self.net.landed(self.zr.at[pl.ds(0, 3)], self.slot + 2)
        src = self.zr if self.zdim else self.t2
        spot = self.piece(self.i, self.j)
        self.mine = self.net.local(src, spot)
        self.net.send([(src, spot, self.peer(True, d)) for d in (2, 1, 3)], self.r2, self.slot + 3)

    def step5(self):
        self.mine.wait()
        self.net.landed(self.r2, self.slot + 3)
        spot = self.block(self.i)
        self.net.send([(spot, spot, self.peer(False, d)) for d in (2, 1, 3)], self.r1, self.slot + 4)

    def step6(self):
        self.net.landed(self.r1, self.slot + 4)


def shared_shapes(zdim, block, piece):
    lead = (4,) if zdim else ()
    return [
        pltpu.VMEM((3, *lead, *block), bf16),
        pltpu.VMEM((*lead, *block), bf16),
        pltpu.VMEM((3, *lead, *piece), bf16),
        pltpu.VMEM((*lead, *piece), bf16),
        pltpu.VMEM((*lead, *piece), bf16),
    ]


def wide_shared(net, first, column, width, src, scratch, final):
    half = width // 2
    shared = Shared(
        net,
        first,
        True,
        lambda i: (slice(None), ds(i, 32), pl.ds(column, width)),
        lambda j: (slice(None), ds(lax.div(j, 2), 16), ds(lax.rem(j, 2), half)),
        src,
        *scratch,
        final,
    )
    shared.part1_final = lambda i: (slice(None), ds(i, 32), slice(None))
    shared.piece_final = lambda i, j: (
        slice(None),
        ds(2 * i + lax.div(j, 2), 16),
        ds(lax.rem(j, 2), half),
    )
    return shared


def down_shared(net, first, row, rows, src, scratch, final):
    half = rows // 2
    shared = Shared(
        net,
        first,
        False,
        lambda i: (pl.ds(row, rows), ds(i, 256)),
        lambda j: (ds(lax.div(j, 2), half), ds(lax.rem(j, 2), 128)),
        src,
        *scratch,
        final,
    )
    shared.part1_final = shared.part1
    shared.piece_final = lambda i, j: (
        pl.ds(pl.multiple_of(row + lax.div(j, 2) * half, 16), half),
        ds(2 * i + lax.rem(j, 2), 128),
    )
    return shared


def out_shared(net, src, scratch, final):
    shared = Shared(
        net,
        "y",
        False,
        lambda i: (ds(i, 32), slice(None)),
        lambda j: (ds(lax.div(j, 2), 16), ds(lax.rem(j, 2), 512)),
        src,
        *scratch,
        final,
    )
    shared.part1_final = lambda i: (ds(i, 32), slice(None))
    shared.piece_final = lambda i, j: (ds(2 * i + lax.div(j, 2), 16), ds(lax.rem(j, 2), 512))
    return shared


class Weight:
    def __init__(self, net, buf, block, parts, c, z, k):
        self.net, self.buf, self.block = net, buf, block
        self.c, self.z, self.k = c, z, k
        x, y = lax.div(c, 4), lax.rem(c, 4)
        self.parts = [(first, *((x, y) if first == "x" else (y, x)), col, width) for first, col, width in parts]
        self.slot = net.slots(2 + 3 * len(parts))

    def peer(self, along_x, d):
        return device(at_ctx(self.c, d if along_x else 0, 0 if along_x else d), self.z, self.k)

    def piece(self, i, j, col, width):
        half = width // 2
        return ds(2 * i + lax.div(j, 2), 16), pl.ds(
            pl.multiple_of(col + lax.rem(j, 2) * half, 128), half
        )

    def step0(self):
        n, k = self.net, self.k
        sibling = device(self.c, self.z, 1 - k)
        self.mine = n.local(self.block(self.z), self.buf.at[0, k])
        for p, (first, i, j, col, width) in enumerate(self.parts):
            rows, cols = self.piece(i, j, col, width)
            n.send(
                [
                    (
                        self.block(lax.rem(self.z + d, 4)).at[rows, cols],
                        self.buf.at[4 - d, k, rows, cols],
                        device(self.c, lax.rem(self.z + d, 4), k),
                    )
                    for d in Z_STEPS
                ],
                self.buf.at[pl.ds(1, 3), k, rows, cols],
                self.slot + 2 + 3 * p,
            )
        n.send([(self.block(self.z), self.buf.at[0, k], sibling)], self.buf.at[0, k], self.slot)

    def step1(self):
        for p, (first, i, j, col, width) in enumerate(self.parts):
            rows, cols = self.piece(i, j, col, width)
            spot = self.buf.at[pl.ds(1, 3), self.k, rows, cols]
            self.net.landed(spot, self.slot + 2 + 3 * p)
            size = self.buf.at[pl.ds(1, 3), self.k, pl.ds(0, 48), pl.ds(col, width // 2)]
            self.net.send(
                [(spot, spot, self.peer(first != "x", d)) for d in (2, 1, 3)], size, self.slot + 3 + 3 * p
            )

    def step2(self):
        for p, (first, i, j, col, width) in enumerate(self.parts):
            size = self.buf.at[pl.ds(1, 3), self.k, pl.ds(0, 48), pl.ds(col, width // 2)]
            self.net.landed(size, self.slot + 3 + 3 * p)
            spot = self.buf.at[pl.ds(1, 3), self.k, ds(i, 32), pl.ds(col, width)]
            size = self.buf.at[pl.ds(1, 3), self.k, pl.ds(0, 96), pl.ds(col, width)]
            self.net.send(
                [(spot, spot, self.peer(first == "x", d)) for d in (2, 1, 3)], size, self.slot + 4 + 3 * p
            )

    def step3(self):
        for p, (first, i, j, col, width) in enumerate(self.parts):
            size = self.buf.at[pl.ds(1, 3), self.k, pl.ds(0, 96), pl.ds(col, width)]
            self.net.landed(size, self.slot + 4 + 3 * p)
        spot = self.buf.at[pl.ds(1, 3), self.k]
        self.net.send([(spot, spot, device(self.c, self.z, 1 - self.k))], spot, self.slot + 1)

    def step4(self):
        self.mine.wait()
        self.net.landed(self.buf.at[0, 0], self.slot)
        self.net.landed(self.buf.at[pl.ds(1, 3), 0], self.slot + 1)


SHARED = dict(
    gate=(True, (32, 768), (16, 384)),
    up=(True, (32, 768), (16, 384)),
    q=(True, (32, 256), (16, 128)),
    k=(True, (32, 256), (16, 128)),
    v=(True, (32, 256), (16, 128)),
    down_a=(False, (192, 256), (96, 128)),
    down_b=(False, (160, 256), (80, 128)),
    out=(False, (32, 1024), (16, 512)),
)

SCRATCH = dict(
    meta=((4, 2, 24, 128), f32),
    plan=((4, 4, 4, 8, 128), f32),
    pers=((2, 2, 16, 128), bf16),
    x_all=((4, 128, 1024), bf16),
    cot_all=((4, 128, 1024), bf16),
    w_own=((4, 128, 768), bf16),
    w_all=((4, 2, 128, 768), bf16),
    wo_all=((4, 2, 128, 1024), bf16),
    stage=((4, 128, 1536), bf16),
    wgu_all=((4, 2, 128, 1536), bf16),
    wide=((128, 1024), f32),
    wd_all=((768, 1024), bf16),
    n_all=((4, 128, 1024), bf16),
    qkv_s=((3, 512, 256), bf16),
    qkv=((16, 3, 64, 128), bf16),
    probs=((1024, 1024), bf16),
    own=((16, 1024), bf16),
    m0=((16, 128, 128), bf16),
    s0=((16, 128, 128), bf16),
    qa=((16, 192, 128), bf16),
    outer=((16, 128, 128), f32),
    k_l=((16, 64, 128), bf16),
    bias=((1024, 128), f32),
    gf_rows=((16, 128), f32),
    gm_rows=((16, 128), f32),
    rate_f=((16, 128), f32),
    rate_m=((16, 128), f32),
    read_adj=((16, 128, 128), f32),
    reads=((1024, 128), f32),
    mixed=((16, 64, 128), bf16),
    mt=((128, 1024), bf16),
    mq=((512, 256), bf16),
    resid=((128, 1024), f32),
    nf_all=((4, 128, 1024), bf16),
    hid_all=((4, 128, 768), bf16),
    dh=((4, 128, 768), f32),
    dgu_all=((4, 128, 1536), bf16),
    od_all=((4, 128, 1024), bf16),
    nf_own=((128, 1024), f32),
    nf_s=((4, 128, 1024), bf16),
    nf_r=((3, 128, 1024), bf16),
    out_s=((4, 128, 1024), bf16),
    out_r=((3, 128, 1024), bf16),
    d_resid=((128, 1024), f32),
    dbr_all=((4, 128, 1024), bf16),
    dmix=((128, 1024), bf16),
    dm=((16, 64, 128), bf16),
    dq_a=((1024, 128), f32),
    dk_a=((1024, 128), f32),
    dv_a=((1024, 128), f32),
    adj=((16, 128, 128), bf16),
    dqkv=((16, 3, 64, 128), bf16),
    dq_home=((3, 512, 256), bf16),
    dq_l=((512, 768), bf16),
    dn_s=((4, 128, 1024), bf16),
    dn_r=((3, 128, 1024), bf16),
    gu_r=((4, 128, 1536), bf16),
    nf_gain=((1, 1024), f32),
    gu_1=((4, 128, 1536), bf16),
    gd=((768, 1024), bf16),
    gd_r=((352, 1024), bf16),
    gd_1=((352, 1024), bf16),
    gq_s=((4, 128, 768), bf16),
    gq_r=((4, 128, 768), bf16),
    gq_1=((4, 128, 768), bf16),
    go_s=((128, 1024), bf16),
    go_r=((128, 1024), bf16),
    go_1=((128, 1024), bf16),
    gains=((16, 128), f32),
    tables=((16, 128), f32),
    d_own=((32, 128), f32),
    keep=((64, 128), f32),
    give=((64, 128), f32),
    sm_s=((64, 128), f32),
    sm_x=((4, 64, 128), f32),
    sm_y=((4, 64, 128), f32),
    sm_z=((4, 32, 128), f32),
)

INPUTS = [
    "x", "cot", "wq", "wk", "wv", "wo", "wg", "wu", "wd", "pk", "pv", "ga", "gf", "dec", "mom",
    "lens", "didx", "midx",
]
OUTPUTS = dict(
    output=((128, 1024), bf16),
    input_grad=((128, 1024), f32),
    f_gate=((4, 128, 768), bf16),
    f_up=((4, 128, 768), bf16),
    f_q=((4, 128, 256), bf16),
    f_k=((4, 128, 256), bf16),
    f_v=((4, 128, 256), bf16),
    f_down=((352, 1024), bf16),
    f_out=((128, 1024), bf16),
    small=((64, 128), f32),
)


class Refs:
    pass


def layer_kernel(*refs):
    names = INPUTS + list(OUTPUTS) + list(SCRATCH)
    a = Refs()
    for name, ref in zip(names, refs):
        setattr(a, name, ref)
    rest = refs[len(names) :]
    ssem, rsem, lsem, plane_sem, cube_sem, own_sem = rest[-6:]
    c, z, k = coords()
    f = 2 * z + k
    hb, zs, sb = pair_of(c)
    x_at, y_at = lax.div(c, 4), lax.rem(c, 4)
    here, sibling = device(c, z, k), device(c, z, 1 - k)
    same_plane = zs == z
    net = Net(ssem, rsem, lsem, here)
    shared = {}
    sources = dict(
        gate=("x", 0, 768, a.gu_1, a.f_gate),
        up=("y", 768, 768, a.gu_1, a.f_up),
        q=("x", 0, 256, a.gq_1, a.f_q),
        k=("x", 256, 256, a.gq_1, a.f_k),
        v=("y", 512, 256, a.gq_1, a.f_v),
    )
    for n, name in enumerate(SHARED):
        scratch = rest[5 * n : 5 * n + 5]
        if name in sources:
            first, column, width, src, final = sources[name]
            shared[name] = wide_shared(net, first, column, width, src, scratch, final)
        elif name == "down_a":
            shared[name] = down_shared(net, "x", 0, 192, a.gd_1, scratch, a.f_down)
        elif name == "down_b":
            shared[name] = down_shared(net, "y", 192, 160, a.gd_1, scratch, a.f_down)
        else:
            shared[name] = out_shared(net, a.go_1, scratch, a.f_out)
        shared[name].place(c, z, k)

    def z_at(d):
        return lax.rem(z + d + 4, 4)

    def z_peer(d):
        return device(c, z_at(d), k)

    barrier = pltpu.get_barrier_semaphore()

    def along(axis, d):
        return device(at_ctx(c, d if axis == "x" else 0, 0 if axis == "x" else d), z, k)

    for d in Z_STEPS:
        for peer in (z_peer(d), along("x", d), along("y", d)):
            pl.semaphore_signal(barrier, inc=1, device_id=peer, device_id_type=MESH)
    pl.semaphore_signal(barrier, inc=1, device_id=sibling, device_id_type=MESH)

    for n, w in enumerate((a.wq, a.wk, a.wv)):
        for m in range(4):
            pltpu.make_async_copy(
                w.at[:, pl.ds(256 * m, 256)], a.w_own.at[m, :, pl.ds(256 * n, 256)], own_sem
            ).start()

    lane8 = lax.broadcasted_iota(jnp.int32, (8, 128), 1)
    row8 = lax.broadcasted_iota(jnp.int32, (8, 128), 0)
    eye8 = lax.broadcasted_iota(jnp.int32, (8, 8), 0) == lax.broadcasted_iota(jnp.int32, (8, 8), 1)

    def by_head(table):
        placed = jnp.zeros((8, 128), f32)
        for r in range(2):
            row = jnp.broadcast_to(table[r : r + 1, :].astype(f32), (8, 8))
            column = jnp.sum(jnp.where(eye8, row, 0.0), axis=1, keepdims=True)
            placed += jnp.where(lane8 == 2 * f + r, column, 0.0)
        return placed

    head_rows = jnp.where(row8 == 0, a.ga[...].astype(f32), 0.0)
    head_rows = jnp.where(row8 == 1, a.gf[...].astype(f32), head_rows)
    for n in range(2):
        head_rows = jnp.where(row8 == 2 + n, a.lens[n].astype(f32), head_rows)
    a.meta[z, k, 0:8, :] = head_rows
    a.meta[z, k, 8:16, :] = by_head(a.dec[...])
    a.meta[z, k, 16:24, :] = by_head(a.mom[...])
    plan = jnp.zeros((8, 128), f32)
    for n in range(2):
        plan = jnp.where(row8 == n, a.didx[n].astype(f32), plan)
        plan = jnp.where(row8 == 2 + n, a.midx[n].astype(f32), plan)
    a.plan[z, x_at, y_at] = plan
    a.pers[k, 0] = a.pk[...]
    a.pers[k, 1] = a.pv[...]
    a.x_all[z] = a.x[...]

    pl.semaphore_wait(barrier, 10)
    for d in Z_STEPS:
        pl.semaphore_signal(plane_sem, inc=1, device_id=along("y", d), device_id_type=MESH)

    r_meta, r_meta_s, r_x = net.slots(), net.slots(), net.slots(3)
    r_plan, r_pers, r_wd, r_cot = net.slots(3), net.slots(), net.slots(), net.slots()
    w_qkv = Weight(net, a.w_all, lambda zz: a.w_own.at[zz], [("x", 0, 512), ("y", 512, 256)], c, z, k)
    w_o = Weight(net, a.wo_all, lambda zz: a.wo, [("x", 0, 512), ("y", 512, 512)], c, z, k)
    w_gu = Weight(net, a.wgu_all, lambda zz: a.stage.at[zz], [("x", 0, 768), ("y", 768, 768)], c, z, k)

    pltpu.make_async_copy(a.w_own, a.w_own, own_sem).wait()
    w_qkv.step0()
    net.send(
        [(a.x_all.at[z], a.x_all.at[z], z_peer(d), r_x + d - 1) for d in Z_STEPS], a.x_all.at[pl.ds(0, 3)], None
    )
    spot = a.meta.at[z, k]
    net.send([(spot, spot, z_peer(d)) for d in Z_STEPS], a.meta.at[pl.ds(0, 3), 0], r_meta)
    w_o.step0()
    spot = a.plan.at[z, x_at, y_at]
    net.send([(spot, spot, along("x", d)) for d in Z_STEPS], a.plan.at[0, 0, pl.ds(0, 3)], r_plan)
    net.send([(a.pers.at[k], a.pers.at[k], sibling)], a.pers.at[0], r_pers)
    wd_rows = pl.ds(pl.multiple_of(k * 352, 32), 352)
    own_wd = net.local(a.wd, a.wd_all.at[wd_rows, :])
    net.send([(a.wd, a.wd_all.at[wd_rows, :], sibling)], a.gd_r, r_wd)
    a.wd_all[704:768, :] = jnp.zeros((64, 1024), bf16)
    w_qkv.step1()
    net.landed(a.meta.at[pl.ds(0, 3), 0], r_meta)
    spot = a.meta.at[:, k]
    net.send([(spot, spot, sibling)], spot, r_meta_s)
    net.landed(a.plan.at[0, 0, pl.ds(0, 3)], r_plan)
    spot = a.plan.at[z, :, y_at]
    net.send([(spot, spot, along("y", d)) for d in Z_STEPS], a.plan.at[0, pl.ds(0, 3)], r_plan + 1)
    w_qkv.step2()
    w_o.step1()
    for n in range(4):
        for m, w in enumerate((a.wg, a.wu)):
            block = jnp.concatenate([w[:, 704 * n : 704 * n + 704], jnp.zeros((128, 64), bf16)], axis=1)
            a.stage[n, :, 768 * m : 768 * m + 768] = block
    w_gu.step0()
    own_cot = net.local(a.cot, a.cot_all.at[z])
    net.send([(a.cot, a.cot_all.at[z], z_peer(d)) for d in Z_STEPS], a.cot_all.at[pl.ds(0, 3)], r_cot)
    early = len(net.due)

    pl.semaphore_wait(plane_sem, 3)
    for d in Z_STEPS:
        pl.semaphore_signal(cube_sem, inc=1, device_id=z_peer(d), device_id_type=MESH)
    net.landed(a.plan.at[0, pl.ds(0, 3)], r_plan + 1)
    net.send([(a.plan.at[z], a.plan.at[z], z_peer(d)) for d in Z_STEPS], a.plan.at[pl.ds(0, 3)], r_plan + 2)
    net.landed(a.meta.at[:, k], r_meta_s)

    def gain_row(n):
        return jnp.concatenate([a.meta[i // 2, i % 2, n : n + 1, :] for i in range(8)], axis=1)

    gain_one, gain_two = gain_row(0), gain_row(1)
    w_qkv.step3()

    def ahead(e):
        return ds(z_at(e), 256)

    def whole(ref, e):
        return ref[e].reshape(256, ref.shape[-1])

    for d in (0, *Z_STEPS):
        zz = z_at(-d)
        if d:
            net.landed(a.x_all.at[0], r_x + d - 1)
        xf = a.x_all[zz].astype(f32)
        a.n_all[zz] = (xf * scaled(xf) * gain_one).astype(bf16)
    w_qkv.step4()
    for d in (0, *Z_STEPS):
        zz = z_at(-d)
        rows = sum(nn(a.n_all[zz, :, ahead(e)], whole(a.w_all, e)) for e in range(4)).astype(bf16)
        for n in range(3):
            a.qkv_s[n, ds(zz, 128), :] = rows[:, 256 * n : 256 * n + 256]

    r_qkv = net.slots()

    def pair_block(ref, cc):
        hb2, zs2, sb2 = pair_of(cc)
        return ref.at[:, ds(zs2 * 2 + sb2, 64), ds(hb2, 128)]

    net.own(pair_block(a.qkv_s, c), a.qkv.at[c], r_qkv)
    net.send(
        [
            (pair_block(a.qkv_s, at_ctx(c, dx, dy)), a.qkv.at[c], device(at_ctx(c, dx, dy), z, k))
            for dx, dy in CTX_STEPS
        ],
        a.qkv.at[pl.ds(0, 15)],
        r_qkv,
    )

    w_o.step2()
    w_gu.step1()

    net.landed(a.plan.at[pl.ds(0, 3)], r_plan + 2)
    net.landed(a.pers.at[0], r_pers)
    head = 2 * z + hb
    length = a.meta[zs, k, pl.ds(2 + sb, 1), :][:, :1]
    decay, moment = (sum(a.meta[i // 2, i % 2, pl.ds(at + head, 1), :] for i in range(8)) for at in (8, 16))
    lanes = lax.broadcasted_iota(jnp.int32, (16, 128), 1).astype(f32)
    decay_at = a.plan[zs, :, :, pl.ds(sb, 1), :].reshape(16, 128)
    moment_at = a.plan[zs, :, :, pl.ds(2 + sb, 1), :].reshape(16, 128)
    decay_pick = jnp.where(decay_at == lanes, 1.0, 0.0)
    moment_pick = jnp.where(moment_at == lanes, 1.0, 0.0)
    retention = jax.nn.sigmoid(jnp.sum(decay_pick * decay, axis=1, keepdims=True))
    momentum = jax.nn.sigmoid(jnp.sum(moment_pick * moment, axis=1, keepdims=True))
    a.rate_f[...] = jnp.broadcast_to(retention, (16, 128))
    a.rate_m[...] = jnp.broadcast_to(momentum, (16, 128))
    pk, pv = a.pers[hb, 0], a.pers[hb, 1]
    places = lax.broadcasted_iota(jnp.int32, (1024, 1), 0).astype(f32)
    live = jnp.where(places < length, 1.0, 0.0)
    a.bias[...] = jnp.broadcast_to(jnp.where(places < length, 0.0, -1e30), (1024, 128))
    early_late = lax.broadcasted_iota(jnp.int32, (256, 256), 0) <= lax.broadcasted_iota(jnp.int32, (256, 256), 1)

    net.landed(a.qkv, r_qkv)
    w_gu.step2()

    def rows_of(n):
        return a.qkv[:, n].reshape(1024, 128)

    q, kk, v = rows_of(0), rows_of(1), rows_of(2)
    a.qa[:, 0:64] = unit_rows(q.astype(f32))[0].astype(bf16).reshape(16, 64, 128)
    a.k_l[...] = (unit_rows(kk.astype(f32))[0] * live).astype(bf16).reshape(16, 64, 128)
    for b in range(16):
        got = tn(a.k_l[b], jnp.concatenate([a.k_l[b], a.qkv[b, 2]], axis=1))
        a.qa[b, 64:192] = got[:, :128].astype(bf16)
        a.outer[b] = got[:, 128:]
    w_o.step3()
    pl.semaphore_wait(cube_sem, 3)
    r_home, r_mq = net.slots(), net.slots()
    home_s = net.s
    net.s += 1
    home_spot = a.mt.at[ds(sb, 64), ds(head, 128)]
    quart_spot = a.mq.at[ds(zs * 2 + sb, 64), ds(hb, 128)]

    def go_home(cc):
        return remote(a.mixed.at[cc], home_spot, ssem.at[home_s], rsem.at[r_home], device(cc, zs, k))

    memory = jnp.zeros((128, 128), f32)
    velocity = jnp.zeros((128, 128), f32)
    for i in range(4):
        for b in range(4 * i, 4 * i + 4):
            low = memory.astype(bf16)
            a.m0[b] = low
            a.s0[b] = velocity.astype(bf16)
            got = nn(a.qa[b], low)
            a.reads[64 * b : 64 * b + 64, :] = got[:64]
            velocity = a.rate_m[b : b + 1, :] * velocity - RATE * (got[64:] - a.outer[b])
            memory = a.rate_f[b : b + 1, :] * memory + velocity
        span = 256 * (i + 1)
        qs = slice(256 * i, span)
        scores = nt(kk[:span], q[qs]) * SCALE + jnp.concatenate([a.bias[:span, :]] * 2, axis=1)
        last = jnp.where(early_late, scores[256 * i :], -1e30)
        scores = jnp.concatenate([scores[: 256 * i], last], axis=0) if i else last
        own_scores = nt(pk, q[qs]) * SCALE
        top = jnp.maximum(
            jnp.max(scores, axis=0, keepdims=True), jnp.max(own_scores, axis=0, keepdims=True)
        )
        e = jnp.exp(scores - top)
        own_e = jnp.exp(own_scores - top)
        total = jnp.sum(e, axis=0, keepdims=True) + jnp.sum(own_e, axis=0, keepdims=True)
        share = 1.0 / total
        p = (e * share).astype(bf16)
        own_p = (own_e * share).astype(bf16)
        a.probs[:span, qs] = p
        a.own[:, qs] = own_p
        att = tn(v[:span], p) + tn(pv, own_p)
        a.mixed[4 * i : 4 * i + 4] = (att.T + a.reads[qs, :]).astype(bf16).reshape(4, 64, 128)
        for row in (i - 1, i) if i % 2 else ():
            for dy in range(4):
                cc = 4 * row + lax.rem(y_at + dy, 4)
                if dy:
                    go_home(cc).start()
                else:
                    stays = same_plane & (x_at == row)

                    @pl.when(stays)
                    def _():
                        net.own(a.mixed.at[cc], home_spot, r_home)

                    @pl.when(jnp.logical_not(stays))
                    def _():
                        go_home(cc).start()

    net.own(a.mixed.at[c], quart_spot, r_mq)
    net.send(
        [
            (a.mixed.at[at_ctx(c, dx, dy)], quart_spot, device(at_ctx(c, dx, dy), z, k))
            for dx, dy in CTX_STEPS
        ],
        a.mixed.at[pl.ds(0, 15)],
        r_mq,
    )
    w_gu.step3()

    w_o.step4()
    net.landed(a.mt, r_home)
    r_nf = net.slots(3)
    xf = a.x[...].astype(f32)
    resid = xf + sum(nn(a.mt[:, ahead(e)], whole(a.wo_all, e)) for e in range(4))
    a.resid[...] = resid
    a.nf_all[z] = (resid * scaled(resid) * gain_two).astype(bf16)
    net.send(
        [(a.nf_all.at[z], a.nf_all.at[z], z_peer(d), r_nf + d - 1) for d in Z_STEPS],
        a.nf_all.at[pl.ds(0, 3)],
        None,
    )
    own_wd.wait()
    own_cot.wait()
    w_gu.step4()
    net.landed(a.gd_r, r_wd)

    def live_chunk(zz):
        at = (lax.broadcasted_iota(jnp.int32, (64, 1), 0) + c * 64).astype(f32)
        return jnp.concatenate(
            [jnp.where(at < a.meta[zz, k, 2 + n : 3 + n, :][:, :1], 1.0, 0.0) for n in range(2)], axis=0
        )

    net.landed(a.cot_all.at[pl.ds(0, 3)], r_cot)
    for zz in range(4):
        od = (a.cot_all[zz].astype(f32) * live_chunk(zz)).astype(bf16)
        a.od_all[zz] = od
    a.dh[...] = nt(a.od_all[...].reshape(512, 1024), a.wd_all[...]).reshape(4, 128, 768)
    r_nfp, r_out = net.slots(), net.slots()
    nfp_s = net.group(a.nf_s.at[pl.ds(0, 3)])
    for group in ((0,), (1, 3), (2,)):
        places = [z_at(-d) for d in group]
        for d in group:
            if d:
                net.landed(a.nf_all.at[0], r_nf + d - 1)

        def stacked(read):
            parts = [read(zz) for zz in places]
            return jnp.concatenate(parts, axis=0) if len(parts) > 1 else parts[0]

        gu = sum(nn(stacked(lambda zz: a.nf_all[zz, :, ahead(e)]), whole(a.wgu_all, e)) for e in range(4))
        dh = stacked(lambda zz: a.dh[zz])
        g, u = gu[:, :768], gu[:, 768:]
        s = jax.nn.sigmoid(g)
        gs = g * s
        hidden = (gs * u).astype(bf16)
        d_gu = jnp.concatenate(
            [(dh * u * (s + gs * (1.0 - s))).astype(bf16), (dh * gs).astype(bf16)], axis=1
        )
        for n, zz in enumerate(places):
            a.hid_all[zz] = hidden[128 * n : 128 * n + 128]
            a.dgu_all[zz] = d_gu[128 * n : 128 * n + 128]
        for e in range(4):
            part = nt(d_gu, whole(a.wgu_all, e))
            for n, d in enumerate(group):
                if d:
                    a.nf_s[places[n], :, ahead(e)] = part[128 * n : 128 * n + 128].astype(bf16)
                else:
                    a.nf_own[:, ahead(e)] = part
        for n, d in enumerate(group):
            if d:
                net.send([(a.nf_s.at[places[n]], a.nf_r.at[d - 1], z_peer(-d))], None, r_nfp, nfp_s)

    r_gu_c, r_gd_c = net.slots(), net.slots()
    net.drain(early)

    def all_rows(ref):
        return ref[...].reshape(512, ref.shape[-1])

    def gu_tile(n, half):
        return tn(a.nf_all[:, :, ds(2 * n + half, 128)].reshape(512, 128), all_rows(a.dgu_all))

    for n in range(4):
        a.stage[n] = gu_tile(n, 1 - k).astype(bf16)
    net.send([(a.stage, a.gu_r, sibling)], a.stage, r_gu_c)
    a.gd[...] = tn(all_rows(a.hid_all), all_rows(a.od_all)).astype(bf16)
    my_rows = pl.ds(pl.multiple_of(k * 352, 32), 352)
    their_rows = pl.ds(pl.multiple_of((1 - k) * 352, 32), 352)
    net.send([(a.gd.at[their_rows, :], a.gd_r, sibling)], a.gd_r, r_gd_c)

    d_nf = a.nf_own[...]
    net.landed(a.nf_r, r_nfp)
    for d in range(3):
        d_nf += a.nf_r[d].astype(f32)
    back, nf_gain = norm_back(a.resid[...], gain_two, d_nf)
    a.nf_gain[...] = nf_gain
    d_resid = a.od_all[z].astype(f32) + back
    a.d_resid[...] = d_resid
    a.dbr_all[z] = d_resid.astype(bf16)
    for e in range(4):
        a.dmix[:, ahead(e)] = nt(a.dbr_all[z], whole(a.wo_all, e)).astype(bf16)
    r_dm, r_dbr = net.slots(), net.slots()
    dm_s = net.s
    net.s += 1
    for d in (*Z_STEPS, 0):
        for n in range(4):
            owner = (n // 2) * 8 + z * 2 + n % 2
            src = a.dmix.at[ds(n % 2, 64), ds(2 * z_at(d) + n // 2, 128)]
            copy = remote(src, a.dm.at[c], ssem.at[dm_s], rsem.at[r_dm], device(owner, z_at(d), k))
            if d:
                copy.start()
            else:

                @pl.when(owner == c)
                def _():
                    net.own(src, a.dm.at[c], r_dm)

                @pl.when(owner != c)
                def _():
                    copy.start()

    for d in Z_STEPS:
        zz = z_at(-d)
        a.out_s[zz] = nn(a.hid_all[zz], a.wd_all[...]).astype(bf16)
    net.landed(a.gu_r, r_gu_c)
    for n in range(4):
        a.gu_1[n] = (gu_tile(n, k) + a.gu_r[n].astype(f32)).astype(bf16)
    net.landed(a.gd_r, r_gd_c)
    a.gd_1[...] = (a.gd[my_rows, :].astype(f32) + a.gd_r[...].astype(f32)).astype(bf16)
    net.landed(a.dm, r_dm)
    ffn = [shared[n] for n in ("gate", "up", "down_a", "down_b")]
    q_w, k_w, val, w_out = (shared[n] for n in ("q", "k", "v", "out"))
    for one in ffn:
        one.step1()
    net.send([(a.dbr_all.at[z], a.dbr_all.at[z], z_peer(d)) for d in Z_STEPS], a.dbr_all.at[pl.ds(0, 3)], r_dbr)

    dm = a.dm[...].reshape(1024, 128)
    a.dk_a[...] = jnp.zeros((1024, 128), f32)
    a.dv_a[...] = jnp.zeros((1024, 128), f32)
    for b in range(16):
        a.read_adj[b] = tn(a.qa[b, 0:64], a.dm[b])
    d_pk = jnp.zeros((16, 128), f32)
    d_pv = jnp.zeros((16, 128), f32)
    adj_m = jnp.zeros((128, 128), f32)
    adj_v = jnp.zeros((128, 128), f32)
    for i in range(4):
        for b in range(15 - 4 * i, 11 - 4 * i, -1):
            total = adj_m + adj_v
            low = total.astype(bf16)
            a.adj[b] = low
            a.gf_rows[b : b + 1, :] = jnp.sum(adj_m * a.m0[b].astype(f32), axis=0, keepdims=True)
            a.gm_rows[b : b + 1, :] = jnp.sum(total * a.s0[b].astype(f32), axis=0, keepdims=True)
            adj_m = a.rate_f[b : b + 1, :] * adj_m - RATE * nn(a.qa[b, 64:192], low) + a.read_adj[b]
            adj_v = a.rate_m[b : b + 1, :] * total
        span = 256 * (i + 1)
        qs = slice(256 * i, span)
        p = a.probs[:span, qs]
        own_p = a.own[:, qs]
        dp = nt(v[:span], dm[qs])
        own_dp = nt(pv, dm[qs])
        pf, own_pf = p.astype(f32), own_p.astype(f32)
        delta = jnp.sum(pf * dp, axis=0, keepdims=True) + jnp.sum(
            own_pf * own_dp, axis=0, keepdims=True
        )
        d_s = (pf * (dp - delta)).astype(bf16)
        own_ds = (own_pf * (own_dp - delta)).astype(bf16)
        dq = tn(kk[:span], d_s) + tn(pk, own_ds)
        a.dq_a[qs, :] = dq.T * SCALE
        a.dk_a[:span, :] += nn(d_s, q[qs]) * SCALE
        a.dv_a[:span, :] += nn(p, dm[qs])
        d_pk += nn(own_ds, q[qs]) * SCALE
        d_pv += nn(own_p, dm[qs])
    a.d_own[0:16, :] = d_pk
    a.d_own[16:32, :] = d_pv

    r_dq, r_dkv = net.slots(), net.slots()
    spots = [at_ctx(c, dx, dy) for dx, dy in CTX_STEPS] + [c]
    dq_s = net.group(a.dqkv.at[pl.ds(0, 15), 0])
    dkv_s = net.group(a.dqkv.at[pl.ds(0, 15), pl.ds(1, 2)])

    def at_home(first, count):
        return a.dq_home.at[pl.ds(first, count), ds(zs * 2 + sb, 64), ds(hb, 128)]

    def send_home(n, b, first, count, r, s):
        src, dst = a.dqkv.at[b, pl.ds(first, count)], at_home(first, count)
        if n == 15:
            net.own(src, dst, r)
        else:
            net.send([(src, dst, device(b, z, k))], None, r, s)

    for b in range(16):
        qf = a.qkv[b, 0].astype(f32)
        d_qu = nt(a.dm[b], a.m0[b])
        rows = slice(64 * b, 64 * b + 64)
        a.dqkv[b, 0] = (a.dq_a[rows, :] + unit_back(qf, unit_rows(qf)[1], d_qu)).astype(bf16)
    for n, b in enumerate(spots):
        send_home(n, b, 0, 1, r_dq, dq_s)
    for b in range(16):
        rows = slice(64 * b, 64 * b + 64)
        total, k_l = a.adj[b], a.k_l[b]
        d_outer = -RATE * nt(total, a.m0[b])
        kf = a.qkv[b, 1].astype(f32)
        sym = (d_outer + d_outer.T).astype(bf16)
        got = nn(k_l, jnp.concatenate([sym, total], axis=1))
        d_kl = got[:, :128] + RATE * nt(a.qkv[b, 2], total)
        a.dqkv[b, 1] = (a.dk_a[rows, :] + unit_back(kf, unit_rows(kf)[1], d_kl * live[rows])).astype(bf16)
        a.dqkv[b, 2] = (a.dv_a[rows, :] + RATE * got[:, 128:]).astype(bf16)
    for n, b in enumerate(spots):
        send_home(n, b, 1, 2, r_dkv, dkv_s)
    d_plan = []
    for rows, rate, pick in ((a.gf_rows, a.rate_f, decay_pick), (a.gm_rows, a.rate_m, moment_pick)):
        total = jnp.sum(rows[...], axis=1, keepdims=True) * rate[...] * (1.0 - rate[...])
        d_plan.append(jnp.sum(pick * total, axis=0, keepdims=True))
    d_decay, d_moment = d_plan

    r_gq, r_gkv, r_go, r_dn, r_sm = net.slots(), net.slots(), net.slots(), net.slots(), net.slots(4)

    def qkv_tile(n, half, first, count):
        return tn(
            a.n_all[:, :, ds(2 * n + half, 128)].reshape(512, 128), a.dq_l[:, 256 * first : 256 * (first + count)]
        )

    net.landed(a.dq_home.at[0], r_dq)
    a.dq_l[:, 0:256] = a.dq_home[0]
    for n in range(4):
        a.gq_s[n, :, 0:256] = qkv_tile(n, 1 - k, 0, 1).astype(bf16)
    spot = pl.ds(0, 256)
    net.send([(a.gq_s.at[:, :, spot], a.gq_r.at[:, :, spot], sibling)], a.gq_s.at[:, :, spot], r_gq)
    for one in ffn:
        one.step2()
    net.landed(a.gq_r.at[:, :, spot], r_gq)
    for n in range(4):
        a.gq_1[n, :, 0:256] = (qkv_tile(n, k, 0, 1) + a.gq_r[n, :, 0:256].astype(f32)).astype(bf16)

    q_w.step1()

    def out_tile(half):
        return tn(a.mq[:, ds(half, 128)], all_rows(a.dbr_all))

    net.landed(a.dbr_all.at[pl.ds(0, 3)], r_dbr)
    net.landed(a.mixed, r_mq)
    a.go_s[...] = out_tile(1 - k).astype(bf16)
    net.send([(a.go_s, a.go_r, sibling)], a.go_s, r_go)
    for one in ffn:
        one.step3()

    net.landed(a.dq_home.at[pl.ds(1, 2)], r_dkv)
    for n in (1, 2):
        a.dq_l[:, 256 * n : 256 * n + 256] = a.dq_home[n]
    for n in range(4):
        a.gq_s[n, :, 256:768] = qkv_tile(n, 1 - k, 1, 2).astype(bf16)
    spot = pl.ds(256, 512)
    net.send([(a.gq_s.at[:, :, spot], a.gq_r.at[:, :, spot], sibling)], a.gq_s.at[:, :, spot], r_gkv)
    gain_grad = jnp.zeros((1, 1024), f32)
    dn_s = net.group(a.dn_s.at[pl.ds(0, 3)])
    for d in (*Z_STEPS, 0):
        zz = z_at(-d)
        for e in range(4):
            a.wide[:, ahead(e)] = nt(a.dq_l[ds(zz, 128), :], whole(a.w_all, e))
        part = a.wide[...]
        if d:
            a.dn_s[zz] = part.astype(bf16)
            net.send([(a.dn_s.at[zz], a.dn_r.at[d - 1], z_peer(-d))], None, r_dn, dn_s)
        else:
            a.nf_own[...] = part
        rows_f = a.x_all[zz].astype(f32)
        gain_grad += jnp.sum(part * (rows_f * scaled(rows_f)), axis=0, keepdims=True)
    net.landed(a.gq_r.at[:, :, spot], r_gkv)
    for n in range(4):
        a.gq_1[n, :, 256:768] = (qkv_tile(n, k, 1, 2) + a.gq_r[n, :, 256:768].astype(f32)).astype(bf16)
    k_w.step1()
    val.step1()
    net.send(
        [(a.out_s.at[z_at(-d)], a.out_r.at[d - 1], z_peer(-d)) for d in Z_STEPS], a.out_s.at[pl.ds(0, 3)], r_out
    )
    for i in range(8):
        columns = slice(128 * i, 128 * i + 128)
        a.gains[i : i + 1, :] = gain_grad[:, columns]
        a.gains[8 + i : 9 + i, :] = a.nf_gain[:, columns]
    head_at = row8 == head
    a.keep[0:32, :] = jnp.where(hb == k, a.d_own[...], 0.0)
    a.give[0:32, :] = jnp.where(hb == k, 0.0, a.d_own[...])
    for ref in (a.keep, a.give):
        ref[32:48, :] = a.gains[...]
        ref[48:56, :] = jnp.where(head_at, d_decay, 0.0)
        ref[56:64, :] = jnp.where(head_at, d_moment, 0.0)
    net.send([(a.give, a.sm_s, sibling)], a.give, r_sm)
    net.landed(a.go_r, r_go)
    a.go_1[...] = (out_tile(k) + a.go_r[...].astype(f32)).astype(bf16)
    w_out.step1()
    q_w.step2()
    net.landed(a.sm_s, r_sm)
    a.sm_x[x_at] = a.keep[...] + a.sm_s[...]
    net.send(
        [(a.sm_x.at[x_at], a.sm_x.at[x_at], along("x", d)) for d in Z_STEPS], a.sm_x.at[pl.ds(0, 3)], r_sm + 1
    )

    k_w.step2()
    val.step2()
    for one in ffn:
        one.step4()
    net.landed(a.sm_x.at[pl.ds(0, 3)], r_sm + 1)
    a.sm_y[y_at] = a.sm_x[0] + a.sm_x[1] + a.sm_x[2] + a.sm_x[3]
    net.send(
        [(a.sm_y.at[y_at], a.sm_y.at[y_at], along("y", d)) for d in Z_STEPS], a.sm_y.at[pl.ds(0, 3)], r_sm + 2
    )
    w_out.step2()
    for one in (q_w, k_w, val):
        one.step3()
    for one in ffn:
        one.step5()
    net.landed(a.sm_y.at[pl.ds(0, 3)], r_sm + 2)
    plane = a.sm_y[0] + a.sm_y[1] + a.sm_y[2] + a.sm_y[3]
    a.small[0:32, :] = plane[0:32]
    a.sm_z[z] = plane[32:64]
    net.send([(a.sm_z.at[z], a.sm_z.at[z], z_peer(d)) for d in Z_STEPS], a.sm_z.at[pl.ds(0, 3)], r_sm + 3)
    w_out.step3()
    for one in (q_w, k_w, val, w_out):
        one.step4()
    d_n = a.nf_own[...]
    net.landed(a.dn_r, r_dn)
    for d in range(3):
        d_n += a.dn_r[d].astype(f32)
    back, _ = norm_back(a.x[...].astype(f32), gain_one, d_n)
    a.input_grad[...] = a.d_resid[...] + back
    for one in (q_w, k_w, val, w_out):
        one.step5()
    out_sum = a.resid[...] + nn(a.hid_all[z], a.wd_all[...])
    net.landed(a.out_r, r_out)
    for d in range(3):
        out_sum += a.out_r[d].astype(f32)
    a.output[...] = out_sum.astype(bf16)
    net.landed(a.sm_z.at[pl.ds(0, 3)], r_sm + 3)
    a.small[32:64, :] = a.sm_z[0] + a.sm_z[1] + a.sm_z[2] + a.sm_z[3]
    for one in (*ffn, w_out, q_w, k_w, val):
        one.step6()
    net.drain()
    assert (net.s, net.r, net.l) == SEMS, (net.s, net.r, net.l)

    for slot, ref in ((home_s, a.mixed), (dm_s, a.dm)):

        @pl.when(same_plane)
        def _():
            size = ref.at[pl.ds(0, 15)]
            remote(size, size, ssem.at[slot], rsem.at[0], here).wait_send()

        @pl.when(jnp.logical_not(same_plane))
        def _():
            remote(ref, ref, ssem.at[slot], rsem.at[0], here).wait_send()


def finish_kernel(*refs):
    ins, outs = refs[:10], refs[10:25]
    buf_in, buf_out, sem_in, sem_out = refs[25:35], refs[35:48], refs[48], refs[49]
    c, z, k = coords()
    f = 2 * z + k
    loads = [pltpu.make_async_copy(ins[n], buf_in[n], sem_in.at[n]) for n in range(10)]
    for copy in (*loads[2:], *loads[:2]):
        copy.start()
    gate, up, q, kk, v, down, w_out, small = buf_in[2:]
    gain1, gq, gk, gv, go, pk, pv, gain2, gg, gu, gd, dec, mom = buf_out
    sent = []

    def store(*indices):
        for n in indices:
            copy = pltpu.make_async_copy(buf_out[n], outs[2 + n], sem_out.at[2 + n])
            copy.start()
            sent.append(copy)

    for at, (src, dst, n) in enumerate(((gate, gg, 8), (up, gu, 9))):
        loads[2 + at].wait()
        for m in range(4):
            dst[:, 704 * m : 704 * m + 704] = src[m, :, 0:704].astype(f32)
        store(n)
    for at, (src, dst, n) in enumerate(((q, gq, 1), (kk, gk, 2), (v, gv, 3))):
        loads[4 + at].wait()
        for m in range(4):
            dst[:, 256 * m : 256 * m + 256] = src[m].astype(f32)
        store(n)
    for at, (src, dst, n) in enumerate(((down, gd, 10), (w_out, go, 4))):
        loads[7 + at].wait()
        dst[...] = src[...].astype(f32)
        store(n)
    loads[9].wait()
    pk[...] = small[0:16, :]
    pv[...] = small[16:32, :]
    gain1[...] = small[pl.ds(32 + f, 1), :]
    gain2[...] = small[pl.ds(40 + f, 1), :]
    eye = lax.broadcasted_iota(jnp.int32, (8, 8), 0) == lax.broadcasted_iota(jnp.int32, (8, 8), 1)
    lane = lax.broadcasted_iota(jnp.int32, (8, 128), 1)
    for ref, at in ((dec, 48), (mom, 56)):
        for r in range(2):
            column = jnp.sum(jnp.where(lane == 2 * f + r, small[at : at + 8, :], 0.0), axis=1, keepdims=True)
            ref[r : r + 1, :] = jnp.sum(jnp.where(eye, column, 0.0), axis=0, keepdims=True)
    store(0, 5, 6, 7, 11, 12)
    for n in range(2):
        loads[n].wait()
        copy = pltpu.make_async_copy(buf_in[n], outs[n], sem_out.at[n])
        copy.start()
        sent.append(copy)
    for copy in sent:
        copy.wait()


def shards(
    inputs, gain_attn, w_query, w_key, w_value, w_out, persist_key, persist_value, gain_ffn,
    w_gate, w_up, w_down, decay_table, momentum_table, lengths, decay_index, momentum_index,
    cotangent,
):
    operands = dict(
        x=inputs.reshape(128, 1024), cot=cotangent.reshape(128, 1024),
        wq=w_query, wk=w_key, wv=w_value, wo=w_out, wg=w_gate, wu=w_up, wd=w_down,
        pk=persist_key, pv=persist_value, ga=gain_attn.reshape(1, 128), gf=gain_ffn.reshape(1, 128),
        dec=decay_table, mom=momentum_table, lens=lengths, didx=decay_index.reshape(2), midx=momentum_index.reshape(2),
    )
    far = {"cot", "wq", "wk", "wv", "wo", "wd"}
    scalars = {"lens", "didx", "midx"}

    def space(name):
        return pl.ANY if name in far else pltpu.SMEM if name in scalars else pltpu.VMEM

    near = {"output", "input_grad", "small"}
    scratch = [pltpu.VMEM(shape, dtype) for shape, dtype in SCRATCH.values()]
    for zdim, block, piece in SHARED.values():
        scratch += shared_shapes(zdim, block, piece)
    scratch += [pltpu.SemaphoreType.DMA((n,)) for n in SEMS]
    scratch += [pltpu.SemaphoreType.REGULAR, pltpu.SemaphoreType.REGULAR, pltpu.SemaphoreType.DMA]
    results = pl.pallas_call(
        layer_kernel,
        out_shape=[jax.ShapeDtypeStruct(s, t) for s, t in OUTPUTS.values()],
        in_specs=[pl.BlockSpec(memory_space=space(n)) for n in INPUTS],
        out_specs=[pl.BlockSpec(memory_space=pltpu.VMEM if n in near else pl.ANY) for n in OUTPUTS],
        scratch_shapes=scratch,
        compiler_params=pltpu.CompilerParams(
            collective_id=1, has_side_effects=True, vmem_limit_bytes=VMEM_LIMIT
        ),
        name="layer",
    )(*[operands[n] for n in INPUTS])
    shapes = [
        (1, 128), (128, 1024), (128, 1024), (128, 1024), (128, 1024), (16, 128), (16, 128), (1, 128),
        (128, 2816), (128, 2816), (352, 1024), (2, 8), (2, 8),
    ]
    far_away = pl.BlockSpec(memory_space=pl.ANY)
    output, input_grad, *grads = pl.pallas_call(
        finish_kernel,
        out_shape=[jax.ShapeDtypeStruct(*OUTPUTS[n]) for n in ("output", "input_grad")]
        + [jax.ShapeDtypeStruct(s, f32) for s in shapes],
        in_specs=[far_away] * 10,
        out_specs=[far_away] * 15,
        scratch_shapes=[pltpu.VMEM(*v) for v in OUTPUTS.values()]
        + [pltpu.VMEM(s, f32) for s in shapes]
        + [pltpu.SemaphoreType.DMA((10,)), pltpu.SemaphoreType.DMA((15,))],
        compiler_params=pltpu.CompilerParams(vmem_limit_bytes=VMEM_LIMIT),
        name="finish",
    )(*results)
    gain1, gq, gk, gv, go, pk, pv, gain2, gg, gu, gd, dec, mom = grads
    return (
        output.reshape(2, 64, 1024), input_grad.reshape(2, 64, 1024), gain1.reshape(128),
        gq, gk, gv, go, pk, pv, gain2.reshape(128), gg, gu, gd, dec, mom,
    )


def solution(mesh):
    rows, cols = P("fsdp", None), P(None, "fsdp")
    tokens = P("fsdp", "ctx", None)
    in_specs = (
        tokens, P("fsdp"), rows, rows, rows, rows, cols, cols, P("fsdp"), rows, rows, rows, rows, rows,
        P("fsdp"), P("fsdp", "ctx"), P("fsdp", "ctx"), tokens,
    )
    out_specs = (
        tokens, tokens, P("fsdp"), rows, rows, rows, rows, cols, cols, P("fsdp"), rows, rows, rows, rows, rows,
    )
    return jax.shard_map(shards, mesh=mesh, in_specs=in_specs, out_specs=out_specs, check_vma=False)
```

time: 1580 us -> 178 us (0.11)
  waiting for transfers between devices: 804 us -> 0 us
  matrix products: 338 us -> 0 us
  Pallas kernels: 0 us -> 175 us
  blocking collectives: 149 us -> 0 us
  starting transfers between devices: 123 us -> 0 us
  other arithmetic: 105 us -> 0 us
  local copies, waits for them, and re-layouts: 31.4 us -> 0 us
  between operations: 17.6 us -> 0.86 us
    ppermute x30 -> x0, waiting for transfers between devices: 558 us -> none  [from_behind(): lax.ppermute(value, axis, [(source, source + steps) for source in range(f...]
    dot_general x79 -> x0, matrix products: 338 us -> none  [the longest x46 245 us: batched(): return jnp.einsum(pattern, left_side, right_side, precision=highest)]
    pallas_call x0 -> x2, Pallas kernels: none -> 175 us  [the longest x1 171 us: shards(): pl.pallas_call(layer_kernel, out_shape=[jax.ShapeDtypeStruct(s, t) for s,...]
    all_gather x9 -> x0, waiting for transfers between devices: 124 us -> none  [the longest x1 46.2 us: shards(): lax.all_gather(values, 'ctx', axis=1, tiled=True)]
    ppermute x30 -> x0, starting transfers between devices: 122 us -> none  [from_behind(): lax.ppermute(value, axis, [(source, source + steps) for source in range(f...]
    convert_element_type x47 -> x0, other arithmetic: 76.8 us -> none  [the longest x15 41.1 us: relay_adjoint(): return from_behind(affine(back_map, back_offset, incoming).astype(jnp.bfl...]
    psum x1 -> x0, blocking collectives: 74.7 us -> none  [shards(): lax.psum(scattered[0].astype(jnp.bfloat16), 'ctx').astype(jnp.float32)]
    unnamed x22 -> x0, waiting for transfers between devices: 61.5 us -> none
  transfers between devices with their start and end apart: 50 -> 0, of which waited for: 38 -> 0; matrix products, arithmetic and copies ran while one was open for 26% -> 0% of each run, Pallas kernels for 0% -> 0%
where the time goes in v2:
time: 178 us; the launch traced here: 176 us
  Pallas kernels  175 us (98%)
    pallas_call x1, Pallas kernels, shards(): pl.pallas_call(layer_kernel, out_shape=[jax.ShapeDtypeStruct(s, t) for s,...  171 us
    pallas_call x1, Pallas kernels, shards(): pl.pallas_call(finish_kernel, out_shape=[jax.ShapeDtypeStruct(*OUTPUTS[n]...  4.5 us

profile of v2, /device:TPU:0, one launch (start us, length us, event | category | flops | bytes accessed | tf_op | source)
XLA Modules:
  0.0 176.2 jit_solution(583173335830173716)
XLA Ops:
  0.7 170.8 %layer.1 = (bf16[128,1024]{1,0:T(8,128)(2,1)}, f32[128,1024]{1,0:T(8,128)}, bf16[4,128,768]{2,1,0:T(8,128)(2,1)}, bf16[4,128,768]{2,1,0:T(8,128)(2,1)}, bf16[4,1...) custom-call(bf16[128,1024]{1,0:T(8,128)(2,1)} %bitcast.10, ...), custom_call_target="tpu_custom_call" | custom-call | tf_op jit(solution)/shard_map/layer/pallas_call | solution.py:1159
  171.5 4.5 %finish.1 = (bf16[128,1024]{1,0:T(8,128)(2,1)}, f32[128,1024]{1,0:T(8,128)}, f32[1,128]{1,0:T(1,128)}, f32[128,1024]{1,0:T(8,128)}, f32[128,1024]{1,0:T(8,128)},...) custom-call(bf16[128,1024]{1,0:T(8,128)(2,1)} %get-tuple-element.40., ...), custom_call_target="tpu_custom_call" | custom-call | tf_op jit(solution)/shard_map/finish/pallas_call | solution.py:1175

commit v3 on v2

--- a/solution.py
+++ b/solution.py
@@ -14,7 +14,7 @@
 RATE = 0.1
 SCALE = 128**-0.5
 VMEM_LIMIT = 63 << 20
-SEMS = (90, 97, 13)
+SEMS = (84, 91, 20)
 
 
 def coords():
@@ -22,8 +22,8 @@
     return c, lax.div(f, 2), lax.rem(f, 2)
 
 
-def pair_of(c):
-    return lax.div(c, 8), lax.rem(lax.div(c, 2), 4), lax.rem(c, 2)
+def pair_of(c, z):
+    return lax.div(c, 8), lax.rem(lax.div(c, 2) + 8 - z, 4), lax.rem(c, 2)
 
 
 def at_ctx(c, dx, dy):
@@ -277,73 +277,60 @@
 
 
 class Weight:
-    def __init__(self, net, buf, block, parts, c, z, k):
-        self.net, self.buf, self.block = net, buf, block
+    def __init__(self, net, buf, sources, c, z, k):
+        self.net, self.buf, self.sources = net, buf, sources
         self.c, self.z, self.k = c, z, k
-        x, y = lax.div(c, 4), lax.rem(c, 4)
-        self.parts = [(first, *((x, y) if first == "x" else (y, x)), col, width) for first, col, width in parts]
-        self.slot = net.slots(2 + 3 * len(parts))
-
-    def peer(self, along_x, d):
-        return device(at_ctx(self.c, d if along_x else 0, 0 if along_x else d), self.z, self.k)
-
-    def piece(self, i, j, col, width):
-        half = width // 2
-        return ds(2 * i + lax.div(j, 2), 16), pl.ds(
-            pl.multiple_of(col + lax.rem(j, 2) * half, 128), half
-        )
+        self.half = buf.shape[-1] // 2
+        self.slot = net.slots(6)
+
+    def axes(self):
+        for n, at in enumerate((lax.div(self.c, 4), lax.rem(self.c, 4))):
+            yield n, ds(at, 32), pl.ds(n * self.half, self.half)
+
+    def size(self, rows):
+        return self.buf.at[pl.ds(1, 3), 0, pl.ds(0, rows), pl.ds(0, self.half)]
 
     def step0(self):
-        n, k = self.net, self.k
+        net, k = self.net, self.k
         sibling = device(self.c, self.z, 1 - k)
-        self.mine = n.local(self.block(self.z), self.buf.at[0, k])
-        for p, (first, i, j, col, width) in enumerate(self.parts):
-            rows, cols = self.piece(i, j, col, width)
-            n.send(
-                [
-                    (
-                        self.block(lax.rem(self.z + d, 4)).at[rows, cols],
-                        self.buf.at[4 - d, k, rows, cols],
-                        device(self.c, lax.rem(self.z + d, 4), k),
-                    )
-                    for d in Z_STEPS
-                ],
-                self.buf.at[pl.ds(1, 3), k, rows, cols],
-                self.slot + 2 + 3 * p,
-            )
-        n.send([(self.block(self.z), self.buf.at[0, k], sibling)], self.buf.at[0, k], self.slot)
+        for n, rows, _ in self.axes():
+            moves = []
+            for d in Z_STEPS:
+                zz = lax.rem(self.z + d, 4)
+                for src, start, column, width in self.sources(zz):
+                    if column // self.half == n:
+                        spot = self.buf.at[4 - d, k, rows, pl.ds(column, width)]
+                        moves.append((src.at[rows, pl.ds(start, width)], spot, device(self.c, zz, k)))
+            net.send(moves, self.size(32), self.slot + n)
+        self.mine = []
+        moves = []
+        for src, start, column, width in self.sources(self.z):
+            block, spot = src.at[:, pl.ds(start, width)], self.buf.at[0, k, :, pl.ds(column, width)]
+            self.mine.append(net.local(block, spot))
+            moves.append((block, spot, sibling))
+        net.send(moves, self.buf.at[0, k], self.slot + 4)
 
     def step1(self):
-        for p, (first, i, j, col, width) in enumerate(self.parts):
-            rows, cols = self.piece(i, j, col, width)
-            spot = self.buf.at[pl.ds(1, 3), self.k, rows, cols]
-            self.net.landed(spot, self.slot + 2 + 3 * p)
-            size = self.buf.at[pl.ds(1, 3), self.k, pl.ds(0, 48), pl.ds(col, width // 2)]
-            self.net.send(
-                [(spot, spot, self.peer(first != "x", d)) for d in (2, 1, 3)], size, self.slot + 3 + 3 * p
-            )
+        for n, rows, columns in self.axes():
+            self.net.landed(self.size(32), self.slot + n)
+            spot = self.buf.at[pl.ds(1, 3), self.k, rows, columns]
+            moves = []
+            for d in (2, 1, 3):
+                peer = device(at_ctx(self.c, 0 if n else d, d if n else 0), self.z, self.k)
+                moves.append((spot, spot, peer))
+            self.net.send(moves, self.size(96), self.slot + 2 + n)
 
     def step2(self):
-        for p, (first, i, j, col, width) in enumerate(self.parts):
-            size = self.buf.at[pl.ds(1, 3), self.k, pl.ds(0, 48), pl.ds(col, width // 2)]
-            self.net.landed(size, self.slot + 3 + 3 * p)
-            spot = self.buf.at[pl.ds(1, 3), self.k, ds(i, 32), pl.ds(col, width)]
-            size = self.buf.at[pl.ds(1, 3), self.k, pl.ds(0, 96), pl.ds(col, width)]
-            self.net.send(
-                [(spot, spot, self.peer(first == "x", d)) for d in (2, 1, 3)], size, self.slot + 4 + 3 * p
-            )
+        for n in range(2):
+            self.net.landed(self.size(96), self.slot + 2 + n)
+        spot = self.buf.at[pl.ds(1, 3), self.k]
+        self.net.send([(spot, spot, device(self.c, self.z, 1 - self.k))], spot, self.slot + 5)
 
     def step3(self):
-        for p, (first, i, j, col, width) in enumerate(self.parts):
-            size = self.buf.at[pl.ds(1, 3), self.k, pl.ds(0, 96), pl.ds(col, width)]
-            self.net.landed(size, self.slot + 4 + 3 * p)
-        spot = self.buf.at[pl.ds(1, 3), self.k]
-        self.net.send([(spot, spot, device(self.c, self.z, 1 - self.k))], spot, self.slot + 1)
-
-    def step4(self):
-        self.mine.wait()
-        self.net.landed(self.buf.at[0, 0], self.slot)
-        self.net.landed(self.buf.at[pl.ds(1, 3), 0], self.slot + 1)
+        for copy in self.mine:
+            copy.wait()
+        self.net.landed(self.buf.at[0, 0], self.slot + 4)
+        self.net.landed(self.buf.at[pl.ds(1, 3), 0], self.slot + 5)
 
 
 SHARED = dict(
@@ -363,7 +350,7 @@
     pers=((2, 2, 16, 128), bf16),
     x_all=((4, 128, 1024), bf16),
     cot_all=((4, 128, 1024), bf16),
-    w_own=((4, 128, 768), bf16),
+    w_ffn=((2, 128, 2816), bf16),
     w_all=((4, 2, 128, 768), bf16),
     wo_all=((4, 2, 128, 1024), bf16),
     stage=((4, 128, 1536), bf16),
@@ -371,6 +358,7 @@
     wide=((128, 1024), f32),
     wd_all=((768, 1024), bf16),
     n_all=((4, 128, 1024), bf16),
+    n_t=((8, 128, 512), bf16),
     qkv_s=((3, 512, 256), bf16),
     qkv=((16, 3, 64, 128), bf16),
     probs=((1024, 1024), bf16),
@@ -403,7 +391,7 @@
     out_r=((3, 128, 1024), bf16),
     d_resid=((128, 1024), f32),
     dbr_all=((4, 128, 1024), bf16),
-    dmix=((128, 1024), bf16),
+    dmix=((4, 2, 2, 64, 128), bf16),
     dm=((16, 64, 128), bf16),
     dq_a=((1024, 128), f32),
     dk_a=((1024, 128), f32),
@@ -465,10 +453,10 @@
     for name, ref in zip(names, refs):
         setattr(a, name, ref)
     rest = refs[len(names) :]
-    ssem, rsem, lsem, plane_sem, cube_sem, own_sem = rest[-6:]
+    ssem, rsem, lsem, plane_sem, cube_sem = rest[-5:]
     c, z, k = coords()
     f = 2 * z + k
-    hb, zs, sb = pair_of(c)
+    hb, zs, sb = pair_of(c, z)
     x_at, y_at = lax.div(c, 4), lax.rem(c, 4)
     here, sibling = device(c, z, k), device(c, z, 1 - k)
     same_plane = zs == z
@@ -510,11 +498,7 @@
             pl.semaphore_signal(barrier, inc=1, device_id=peer, device_id_type=MESH)
     pl.semaphore_signal(barrier, inc=1, device_id=sibling, device_id_type=MESH)
 
-    for n, w in enumerate((a.wq, a.wk, a.wv)):
-        for m in range(4):
-            pltpu.make_async_copy(
-                w.at[:, pl.ds(256 * m, 256)], a.w_own.at[m, :, pl.ds(256 * n, 256)], own_sem
-            ).start()
+    into_ffn = [net.local(w, a.w_ffn.at[n]) for n, w in enumerate((a.wg, a.wu))]
 
     lane8 = lax.broadcasted_iota(jnp.int32, (8, 128), 1)
     row8 = lax.broadcasted_iota(jnp.int32, (8, 128), 0)
@@ -550,26 +534,40 @@
 
     r_meta, r_meta_s, r_x = net.slots(), net.slots(), net.slots(3)
     r_plan, r_pers, r_wd, r_cot = net.slots(3), net.slots(), net.slots(), net.slots()
-    w_qkv = Weight(net, a.w_all, lambda zz: a.w_own.at[zz], [("x", 0, 512), ("y", 512, 256)], c, z, k)
-    w_o = Weight(net, a.wo_all, lambda zz: a.wo, [("x", 0, 512), ("y", 512, 512)], c, z, k)
-    w_gu = Weight(net, a.wgu_all, lambda zz: a.stage.at[zz], [("x", 0, 768), ("y", 768, 768)], c, z, k)
-
-    pltpu.make_async_copy(a.w_own, a.w_own, own_sem).wait()
+    def from_qkv(zz):
+        start = pl.multiple_of(zz * 256, 256)
+        middle = pl.multiple_of(zz * 256 + 128, 128)
+        return [
+            (a.wq, start, 0, 256), (a.wk, start, 256, 128), (a.wk, middle, 384, 128), (a.wv, start, 512, 256),
+        ]
+
+    w_qkv = Weight(net, a.w_all, from_qkv, c, z, k)
+    w_o = Weight(net, a.wo_all, lambda zz: [(a.wo, 0, 0, 512), (a.wo, 512, 512, 512)], c, z, k)
+    w_gu = Weight(
+        net, a.wgu_all, lambda zz: [(a.stage.at[zz], 0, 0, 768), (a.stage.at[zz], 768, 768, 768)], c, z, k
+    )
     w_qkv.step0()
+    spot = a.meta.at[z, k]
+    net.send([(spot, spot, z_peer(d)) for d in Z_STEPS], a.meta.at[pl.ds(0, 3), 0], r_meta)
+    spot = a.plan.at[z, x_at, y_at]
+    net.send([(spot, spot, along("x", d)) for d in Z_STEPS], a.plan.at[0, 0, pl.ds(0, 3)], r_plan)
+    w_qkv.step1()
     net.send(
         [(a.x_all.at[z], a.x_all.at[z], z_peer(d), r_x + d - 1) for d in Z_STEPS], a.x_all.at[pl.ds(0, 3)], None
     )
-    spot = a.meta.at[z, k]
-    net.send([(spot, spot, z_peer(d)) for d in Z_STEPS], a.meta.at[pl.ds(0, 3), 0], r_meta)
     w_o.step0()
-    spot = a.plan.at[z, x_at, y_at]
-    net.send([(spot, spot, along("x", d)) for d in Z_STEPS], a.plan.at[0, 0, pl.ds(0, 3)], r_plan)
-    net.send([(a.pers.at[k], a.pers.at[k], sibling)], a.pers.at[0], r_pers)
-    wd_rows = pl.ds(pl.multiple_of(k * 352, 32), 352)
-    own_wd = net.local(a.wd, a.wd_all.at[wd_rows, :])
-    net.send([(a.wd, a.wd_all.at[wd_rows, :], sibling)], a.gd_r, r_wd)
-    a.wd_all[704:768, :] = jnp.zeros((64, 1024), bf16)
-    w_qkv.step1()
+
+    def stage_ffn(blocks):
+        for n in blocks:
+            for m in range(2):
+                block = a.w_ffn[m, :, 704 * n : 704 * n + 704]
+                a.stage[n, :, 768 * m : 768 * m + 768] = jnp.concatenate(
+                    [block, jnp.zeros((128, 64), bf16)], axis=1
+                )
+
+    for copy in into_ffn:
+        copy.wait()
+    stage_ffn((0, 1))
     net.landed(a.meta.at[pl.ds(0, 3), 0], r_meta)
     spot = a.meta.at[:, k]
     net.send([(spot, spot, sibling)], spot, r_meta_s)
@@ -577,16 +575,13 @@
     spot = a.plan.at[z, :, y_at]
     net.send([(spot, spot, along("y", d)) for d in Z_STEPS], a.plan.at[0, pl.ds(0, 3)], r_plan + 1)
     w_qkv.step2()
-    w_o.step1()
-    for n in range(4):
-        for m, w in enumerate((a.wg, a.wu)):
-            block = jnp.concatenate([w[:, 704 * n : 704 * n + 704], jnp.zeros((128, 64), bf16)], axis=1)
-            a.stage[n, :, 768 * m : 768 * m + 768] = block
+    stage_ffn((2, 3))
     w_gu.step0()
-    own_cot = net.local(a.cot, a.cot_all.at[z])
-    net.send([(a.cot, a.cot_all.at[z], z_peer(d)) for d in Z_STEPS], a.cot_all.at[pl.ds(0, 3)], r_cot)
-    early = len(net.due)
-
+    net.send([(a.pers.at[k], a.pers.at[k], sibling)], a.pers.at[0], r_pers)
+    wd_rows = pl.ds(pl.multiple_of(k * 352, 32), 352)
+    own_wd = net.local(a.wd, a.wd_all.at[wd_rows, :])
+    net.send([(a.wd, a.wd_all.at[wd_rows, :], sibling)], a.gd_r, r_wd)
+    a.wd_all[704:768, :] = jnp.zeros((64, 1024), bf16)
     pl.semaphore_wait(plane_sem, 3)
     for d in Z_STEPS:
         pl.semaphore_signal(cube_sem, inc=1, device_id=z_peer(d), device_id_type=MESH)
@@ -598,7 +593,6 @@
         return jnp.concatenate([a.meta[i // 2, i % 2, n : n + 1, :] for i in range(8)], axis=1)
 
     gain_one, gain_two = gain_row(0), gain_row(1)
-    w_qkv.step3()
 
     def ahead(e):
         return ds(z_at(e), 256)
@@ -612,7 +606,7 @@
             net.landed(a.x_all.at[0], r_x + d - 1)
         xf = a.x_all[zz].astype(f32)
         a.n_all[zz] = (xf * scaled(xf) * gain_one).astype(bf16)
-    w_qkv.step4()
+    w_qkv.step3()
     for d in (0, *Z_STEPS):
         zz = z_at(-d)
         rows = sum(nn(a.n_all[zz, :, ahead(e)], whole(a.w_all, e)) for e in range(4)).astype(bf16)
@@ -622,7 +616,7 @@
     r_qkv = net.slots()
 
     def pair_block(ref, cc):
-        hb2, zs2, sb2 = pair_of(cc)
+        hb2, zs2, sb2 = pair_of(cc, z)
         return ref.at[:, ds(zs2 * 2 + sb2, 64), ds(hb2, 128)]
 
     net.own(pair_block(a.qkv_s, c), a.qkv.at[c], r_qkv)
@@ -635,8 +629,12 @@
         r_qkv,
     )
 
-    w_o.step2()
-    w_gu.step1()
+    w_o.step1()
+    own_cot = net.local(a.cot, a.cot_all.at[z])
+    net.send([(a.cot, a.cot_all.at[z], z_peer(d)) for d in Z_STEPS], a.cot_all.at[pl.ds(0, 3)], r_cot)
+    early = len(net.due)
+    for i in range(8):
+        a.n_t[i] = a.n_all[:, :, 128 * i : 128 * i + 128].reshape(512, 128).T
 
     net.landed(a.plan.at[pl.ds(0, 3)], r_plan + 2)
     net.landed(a.pers.at[0], r_pers)
@@ -659,7 +657,6 @@
     early_late = lax.broadcasted_iota(jnp.int32, (256, 256), 0) <= lax.broadcasted_iota(jnp.int32, (256, 256), 1)
 
     net.landed(a.qkv, r_qkv)
-    w_gu.step2()
 
     def rows_of(n):
         return a.qkv[:, n].reshape(1024, 128)
@@ -671,7 +668,7 @@
         got = tn(a.k_l[b], jnp.concatenate([a.k_l[b], a.qkv[b, 2]], axis=1))
         a.qa[b, 64:192] = got[:, :128].astype(bf16)
         a.outer[b] = got[:, 128:]
-    w_o.step3()
+    w_gu.step1()
     pl.semaphore_wait(cube_sem, 3)
     r_home, r_mq = net.slots(), net.slots()
     home_s = net.s
@@ -728,6 +725,9 @@
                     def _():
                         go_home(cc).start()
 
+        if i == 1:
+            w_o.step2()
+
     net.own(a.mixed.at[c], quart_spot, r_mq)
     net.send(
         [
@@ -737,9 +737,9 @@
         a.mixed.at[pl.ds(0, 15)],
         r_mq,
     )
-    w_gu.step3()
-
-    w_o.step4()
+    w_gu.step2()
+
+    w_o.step3()
     net.landed(a.mt, r_home)
     r_nf = net.slots(3)
     xf = a.x[...].astype(f32)
@@ -747,13 +747,13 @@
     a.resid[...] = resid
     a.nf_all[z] = (resid * scaled(resid) * gain_two).astype(bf16)
     net.send(
-        [(a.nf_all.at[z], a.nf_all.at[z], z_peer(d), r_nf + d - 1) for d in Z_STEPS],
+        [(a.nf_all.at[z], a.nf_all.at[z], z_peer(d), r_nf + d - 1) for d in (2, 1, 3)],
         a.nf_all.at[pl.ds(0, 3)],
         None,
     )
     own_wd.wait()
     own_cot.wait()
-    w_gu.step4()
+    w_gu.step3()
     net.landed(a.gd_r, r_wd)
 
     def live_chunk(zz):
@@ -769,7 +769,7 @@
     a.dh[...] = nt(a.od_all[...].reshape(512, 1024), a.wd_all[...]).reshape(4, 128, 768)
     r_nfp, r_out = net.slots(), net.slots()
     nfp_s = net.group(a.nf_s.at[pl.ds(0, 3)])
-    for group in ((0,), (1, 3), (2,)):
+    for group in ((0,), (2,), (1, 3)):
         places = [z_at(-d) for d in group]
         for d in group:
             if d:
@@ -819,6 +819,12 @@
     their_rows = pl.ds(pl.multiple_of((1 - k) * 352, 32), 352)
     net.send([(a.gd.at[their_rows, :], a.gd_r, sibling)], a.gd_r, r_gd_c)
 
+    net.landed(a.gu_r, r_gu_c)
+    for n in range(4):
+        a.gu_1[n] = (gu_tile(n, k) + a.gu_r[n].astype(f32)).astype(bf16)
+    net.landed(a.gd_r, r_gd_c)
+    a.gd_1[...] = (a.gd[my_rows, :].astype(f32) + a.gd_r[...].astype(f32)).astype(bf16)
+
     d_nf = a.nf_own[...]
     net.landed(a.nf_r, r_nfp)
     for d in range(3):
@@ -829,14 +835,16 @@
     a.d_resid[...] = d_resid
     a.dbr_all[z] = d_resid.astype(bf16)
     for e in range(4):
-        a.dmix[:, ahead(e)] = nt(a.dbr_all[z], whole(a.wo_all, e)).astype(bf16)
+        part = nt(a.dbr_all[z], whole(a.wo_all, e)).astype(bf16)
+        for n in range(4):
+            a.dmix[e, n // 2, n % 2] = part[64 * (n % 2) : 64 * (n % 2) + 64, 128 * (n // 2) : 128 * (n // 2) + 128]
     r_dm, r_dbr = net.slots(), net.slots()
     dm_s = net.s
     net.s += 1
     for d in (*Z_STEPS, 0):
         for n in range(4):
-            owner = (n // 2) * 8 + z * 2 + n % 2
-            src = a.dmix.at[ds(n % 2, 64), ds(2 * z_at(d) + n // 2, 128)]
+            owner = (n // 2) * 8 + lax.rem(z + z_at(d), 4) * 2 + n % 2
+            src = a.dmix.at[d, n // 2, n % 2]
             copy = remote(src, a.dm.at[c], ssem.at[dm_s], rsem.at[r_dm], device(owner, z_at(d), k))
             if d:
                 copy.start()
@@ -850,19 +858,11 @@
                 def _():
                     copy.start()
 
-    for d in Z_STEPS:
-        zz = z_at(-d)
-        a.out_s[zz] = nn(a.hid_all[zz], a.wd_all[...]).astype(bf16)
-    net.landed(a.gu_r, r_gu_c)
-    for n in range(4):
-        a.gu_1[n] = (gu_tile(n, k) + a.gu_r[n].astype(f32)).astype(bf16)
-    net.landed(a.gd_r, r_gd_c)
-    a.gd_1[...] = (a.gd[my_rows, :].astype(f32) + a.gd_r[...].astype(f32)).astype(bf16)
-    net.landed(a.dm, r_dm)
     ffn = [shared[n] for n in ("gate", "up", "down_a", "down_b")]
     q_w, k_w, val, w_out = (shared[n] for n in ("q", "k", "v", "out"))
     for one in ffn:
         one.step1()
+    net.landed(a.dm, r_dm)
     net.send([(a.dbr_all.at[z], a.dbr_all.at[z], z_peer(d)) for d in Z_STEPS], a.dbr_all.at[pl.ds(0, 3)], r_dbr)
 
     dm = a.dm[...].reshape(1024, 128)
@@ -926,6 +926,8 @@
         a.dqkv[b, 0] = (a.dq_a[rows, :] + unit_back(qf, unit_rows(qf)[1], d_qu)).astype(bf16)
     for n, b in enumerate(spots):
         send_home(n, b, 0, 1, r_dq, dq_s)
+    for one in ffn:
+        one.step2()
     for b in range(16):
         rows = slice(64 * b, 64 * b + 64)
         total, k_l = a.adj[b], a.k_l[b]
@@ -947,23 +949,22 @@
     r_gq, r_gkv, r_go, r_dn, r_sm = net.slots(), net.slots(), net.slots(), net.slots(), net.slots(4)
 
     def qkv_tile(n, half, first, count):
-        return tn(
-            a.n_all[:, :, ds(2 * n + half, 128)].reshape(512, 128), a.dq_l[:, 256 * first : 256 * (first + count)]
-        )
-
+        return nn(a.n_t[2 * n + half], a.dq_l[:, 256 * first : 256 * (first + count)])
+
+    for one in ffn:
+        one.step3()
+    for d in Z_STEPS:
+        zz = z_at(-d)
+        a.out_s[zz] = nn(a.hid_all[zz], a.wd_all[...]).astype(bf16)
+    net.send(
+        [(a.out_s.at[z_at(-d)], a.out_r.at[d - 1], z_peer(-d)) for d in Z_STEPS], a.out_s.at[pl.ds(0, 3)], r_out
+    )
     net.landed(a.dq_home.at[0], r_dq)
     a.dq_l[:, 0:256] = a.dq_home[0]
     for n in range(4):
         a.gq_s[n, :, 0:256] = qkv_tile(n, 1 - k, 0, 1).astype(bf16)
     spot = pl.ds(0, 256)
     net.send([(a.gq_s.at[:, :, spot], a.gq_r.at[:, :, spot], sibling)], a.gq_s.at[:, :, spot], r_gq)
-    for one in ffn:
-        one.step2()
-    net.landed(a.gq_r.at[:, :, spot], r_gq)
-    for n in range(4):
-        a.gq_1[n, :, 0:256] = (qkv_tile(n, k, 0, 1) + a.gq_r[n, :, 0:256].astype(f32)).astype(bf16)
-
-    q_w.step1()
 
     def out_tile(half):
         return tn(a.mq[:, ds(half, 128)], all_rows(a.dbr_all))
@@ -973,7 +974,11 @@
     a.go_s[...] = out_tile(1 - k).astype(bf16)
     net.send([(a.go_s, a.go_r, sibling)], a.go_s, r_go)
     for one in ffn:
-        one.step3()
+        one.step4()
+    net.landed(a.gq_r.at[:, :, spot], r_gq)
+    for n in range(4):
+        a.gq_1[n, :, 0:256] = (qkv_tile(n, k, 0, 1) + a.gq_r[n, :, 0:256].astype(f32)).astype(bf16)
+    q_w.step1()
 
     net.landed(a.dq_home.at[pl.ds(1, 2)], r_dkv)
     for n in (1, 2):
@@ -982,28 +987,36 @@
         a.gq_s[n, :, 256:768] = qkv_tile(n, 1 - k, 1, 2).astype(bf16)
     spot = pl.ds(256, 512)
     net.send([(a.gq_s.at[:, :, spot], a.gq_r.at[:, :, spot], sibling)], a.gq_s.at[:, :, spot], r_gkv)
-    gain_grad = jnp.zeros((1, 1024), f32)
     dn_s = net.group(a.dn_s.at[pl.ds(0, 3)])
-    for d in (*Z_STEPS, 0):
-        zz = z_at(-d)
+
+    def dn_part(zz):
         for e in range(4):
             a.wide[:, ahead(e)] = nt(a.dq_l[ds(zz, 128), :], whole(a.w_all, e))
         part = a.wide[...]
-        if d:
-            a.dn_s[zz] = part.astype(bf16)
-            net.send([(a.dn_s.at[zz], a.dn_r.at[d - 1], z_peer(-d))], None, r_dn, dn_s)
-        else:
-            a.nf_own[...] = part
         rows_f = a.x_all[zz].astype(f32)
-        gain_grad += jnp.sum(part * (rows_f * scaled(rows_f)), axis=0, keepdims=True)
+        return part, jnp.sum(part * (rows_f * scaled(rows_f)), axis=0, keepdims=True)
+
+    gain_grad = jnp.zeros((1, 1024), f32)
+
+    def dn_send(d):
+        part, gain = dn_part(z_at(-d))
+        a.dn_s[z_at(-d)] = part.astype(bf16)
+        net.send([(a.dn_s.at[z_at(-d)], a.dn_r.at[d - 1], z_peer(-d))], None, r_dn, dn_s)
+        return gain
+
+    gain_grad += dn_send(2)
+    gain_grad += dn_send(1)
     net.landed(a.gq_r.at[:, :, spot], r_gkv)
     for n in range(4):
         a.gq_1[n, :, 256:768] = (qkv_tile(n, k, 1, 2) + a.gq_r[n, :, 256:768].astype(f32)).astype(bf16)
     k_w.step1()
     val.step1()
-    net.send(
-        [(a.out_s.at[z_at(-d)], a.out_r.at[d - 1], z_peer(-d)) for d in Z_STEPS], a.out_s.at[pl.ds(0, 3)], r_out
-    )
+    for one in ffn:
+        one.step5()
+    gain_grad += dn_send(3)
+    part, gain = dn_part(z)
+    a.nf_own[...] = part
+    gain_grad += gain
     for i in range(8):
         columns = slice(128 * i, 128 * i + 128)
         a.gains[i : i + 1, :] = gain_grad[:, columns]
@@ -1028,26 +1041,28 @@
 
     k_w.step2()
     val.step2()
-    for one in ffn:
-        one.step4()
+    out_sum = a.resid[...] + nn(a.hid_all[z], a.wd_all[...])
+    net.landed(a.out_r, r_out)
+    for d in range(3):
+        out_sum += a.out_r[d].astype(f32)
+    a.output[...] = out_sum.astype(bf16)
     net.landed(a.sm_x.at[pl.ds(0, 3)], r_sm + 1)
     a.sm_y[y_at] = a.sm_x[0] + a.sm_x[1] + a.sm_x[2] + a.sm_x[3]
     net.send(
         [(a.sm_y.at[y_at], a.sm_y.at[y_at], along("y", d)) for d in Z_STEPS], a.sm_y.at[pl.ds(0, 3)], r_sm + 2
     )
-    w_out.step2()
     for one in (q_w, k_w, val):
         one.step3()
-    for one in ffn:
-        one.step5()
+    w_out.step2()
     net.landed(a.sm_y.at[pl.ds(0, 3)], r_sm + 2)
     plane = a.sm_y[0] + a.sm_y[1] + a.sm_y[2] + a.sm_y[3]
     a.small[0:32, :] = plane[0:32]
     a.sm_z[z] = plane[32:64]
     net.send([(a.sm_z.at[z], a.sm_z.at[z], z_peer(d)) for d in Z_STEPS], a.sm_z.at[pl.ds(0, 3)], r_sm + 3)
+    for one in (q_w, k_w, val):
+        one.step4()
     w_out.step3()
-    for one in (q_w, k_w, val, w_out):
-        one.step4()
+    w_out.step4()
     d_n = a.nf_own[...]
     net.landed(a.dn_r, r_dn)
     for d in range(3):
@@ -1056,11 +1071,6 @@
     a.input_grad[...] = a.d_resid[...] + back
     for one in (q_w, k_w, val, w_out):
         one.step5()
-    out_sum = a.resid[...] + nn(a.hid_all[z], a.wd_all[...])
-    net.landed(a.out_r, r_out)
-    for d in range(3):
-        out_sum += a.out_r[d].astype(f32)
-    a.output[...] = out_sum.astype(bf16)
     net.landed(a.sm_z.at[pl.ds(0, 3)], r_sm + 3)
     a.small[32:64, :] = a.sm_z[0] + a.sm_z[1] + a.sm_z[2] + a.sm_z[3]
     for one in (*ffn, w_out, q_w, k_w, val):
@@ -1144,7 +1154,7 @@
         pk=persist_key, pv=persist_value, ga=gain_attn.reshape(1, 128), gf=gain_ffn.reshape(1, 128),
         dec=decay_table, mom=momentum_table, lens=lengths, didx=decay_index.reshape(2), midx=momentum_index.reshape(2),
     )
-    far = {"cot", "wq", "wk", "wv", "wo", "wd"}
+    far = {"cot", "wq", "wk", "wv", "wo", "wd", "wg", "wu"}
     scalars = {"lens", "didx", "midx"}
 
     def space(name):
@@ -1155,7 +1165,7 @@
     for zdim, block, piece in SHARED.values():
         scratch += shared_shapes(zdim, block, piece)
     scratch += [pltpu.SemaphoreType.DMA((n,)) for n in SEMS]
-    scratch += [pltpu.SemaphoreType.REGULAR, pltpu.SemaphoreType.REGULAR, pltpu.SemaphoreType.DMA]
+    scratch += [pltpu.SemaphoreType.REGULAR, pltpu.SemaphoreType.REGULAR]
     results = pl.pallas_call(
         layer_kernel,
         out_shape=[jax.ShapeDtypeStruct(s, t) for s, t in OUTPUTS.values()],

time: 178 us -> 157 us (0.88)
  Pallas kernels: 175 us -> 156 us
    pallas_call x1, Pallas kernels: 171 us -> 151 us  [shards(): pl.pallas_call(layer_kernel, out_shape=[jax.ShapeDtypeStruct(s, t) for s,...]
where the time goes in v3:
time: 157 us
  Pallas kernels  156 us (99%)
    pallas_call x1, Pallas kernels, shards(): pl.pallas_call(layer_kernel, out_shape=[jax.ShapeDtypeStruct(s, t) for s,...  151 us
    pallas_call x1, Pallas kernels, shards(): pl.pallas_call(finish_kernel, out_shape=[jax.ShapeDtypeStruct(*OUTPUTS[n]...  4.5 us

profile of v3, /device:TPU:0, one launch (start us, length us, event | category | flops | bytes accessed | tf_op | source)
XLA Modules:
  0.0 156.6 jit_solution(3030593331610981163)
XLA Ops:
  0.7 151.2 %layer.1 = (bf16[128,1024]{1,0:T(8,128)(2,1)}, f32[128,1024]{1,0:T(8,128)}, bf16[4,128,768]{2,1,0:T(8,128)(2,1)}, bf16[4,128,768]{2,1,0:T(8,128)(2,1)}, bf16[4,1...) custom-call(bf16[128,1024]{1,0:T(8,128)(2,1)} %bitcast.10, ...), custom_call_target="tpu_custom_call" | custom-call | tf_op jit(solution)/shard_map/layer/pallas_call | solution.py:1169
  151.9 4.5 %finish.1 = (bf16[128,1024]{1,0:T(8,128)(2,1)}, f32[128,1024]{1,0:T(8,128)}, f32[1,128]{1,0:T(1,128)}, f32[128,1024]{1,0:T(8,128)}, f32[128,1024]{1,0:T(8,128)},...) custom-call(bf16[128,1024]{1,0:T(8,128)(2,1)} %get-tuple-element.40., ...), custom_call_target="tpu_custom_call" | custom-call | tf_op jit(solution)/shard_map/finish/pallas_call | solution.py:1185

commit v4 on v3

--- a/solution.py
+++ b/solution.py
@@ -14,7 +14,7 @@
 RATE = 0.1
 SCALE = 128**-0.5
 VMEM_LIMIT = 63 << 20
-SEMS = (84, 91, 20)
+SEMS = (84, 91, 22)
 
 
 def coords():
@@ -390,6 +390,7 @@
     out_s=((4, 128, 1024), bf16),
     out_r=((3, 128, 1024), bf16),
     d_resid=((128, 1024), f32),
+    out_v=((128, 1024), bf16),
     dbr_all=((4, 128, 1024), bf16),
     dmix=((4, 2, 2, 64, 128), bf16),
     dm=((16, 64, 128), bf16),
@@ -565,9 +566,6 @@
                     [block, jnp.zeros((128, 64), bf16)], axis=1
                 )
 
-    for copy in into_ffn:
-        copy.wait()
-    stage_ffn((0, 1))
     net.landed(a.meta.at[pl.ds(0, 3), 0], r_meta)
     spot = a.meta.at[:, k]
     net.send([(spot, spot, sibling)], spot, r_meta_s)
@@ -575,8 +573,6 @@
     spot = a.plan.at[z, :, y_at]
     net.send([(spot, spot, along("y", d)) for d in Z_STEPS], a.plan.at[0, pl.ds(0, 3)], r_plan + 1)
     w_qkv.step2()
-    stage_ffn((2, 3))
-    w_gu.step0()
     net.send([(a.pers.at[k], a.pers.at[k], sibling)], a.pers.at[0], r_pers)
     wd_rows = pl.ds(pl.multiple_of(k * 352, 32), 352)
     own_wd = net.local(a.wd, a.wd_all.at[wd_rows, :])
@@ -630,6 +626,10 @@
     )
 
     w_o.step1()
+    for copy in into_ffn:
+        copy.wait()
+    stage_ffn(range(4))
+    w_gu.step0()
     own_cot = net.local(a.cot, a.cot_all.at[z])
     net.send([(a.cot, a.cot_all.at[z], z_peer(d)) for d in Z_STEPS], a.cot_all.at[pl.ds(0, 3)], r_cot)
     early = len(net.due)
@@ -728,17 +728,6 @@
         if i == 1:
             w_o.step2()
 
-    net.own(a.mixed.at[c], quart_spot, r_mq)
-    net.send(
-        [
-            (a.mixed.at[at_ctx(c, dx, dy)], quart_spot, device(at_ctx(c, dx, dy), z, k))
-            for dx, dy in CTX_STEPS
-        ],
-        a.mixed.at[pl.ds(0, 15)],
-        r_mq,
-    )
-    w_gu.step2()
-
     w_o.step3()
     net.landed(a.mt, r_home)
     r_nf = net.slots(3)
@@ -751,6 +740,16 @@
         a.nf_all.at[pl.ds(0, 3)],
         None,
     )
+    net.own(a.mixed.at[c], quart_spot, r_mq)
+    net.send(
+        [
+            (a.mixed.at[at_ctx(c, dx, dy)], quart_spot, device(at_ctx(c, dx, dy), z, k))
+            for dx, dy in CTX_STEPS
+        ],
+        a.mixed.at[pl.ds(0, 15)],
+        r_mq,
+    )
+    w_gu.step2()
     own_wd.wait()
     own_cot.wait()
     w_gu.step3()
@@ -860,9 +859,11 @@
 
     ffn = [shared[n] for n in ("gate", "up", "down_a", "down_b")]
     q_w, k_w, val, w_out = (shared[n] for n in ("q", "k", "v", "out"))
-    for one in ffn:
+    for one in ffn[:2]:
         one.step1()
     net.landed(a.dm, r_dm)
+    for one in ffn[2:]:
+        one.step1()
     net.send([(a.dbr_all.at[z], a.dbr_all.at[z], z_peer(d)) for d in Z_STEPS], a.dbr_all.at[pl.ds(0, 3)], r_dbr)
 
     dm = a.dm[...].reshape(1024, 128)
@@ -931,11 +932,10 @@
     for b in range(16):
         rows = slice(64 * b, 64 * b + 64)
         total, k_l = a.adj[b], a.k_l[b]
-        d_outer = -RATE * nt(total, a.m0[b])
+        d_outer = (-RATE * nt(total, a.m0[b])).astype(bf16)
         kf = a.qkv[b, 1].astype(f32)
-        sym = (d_outer + d_outer.T).astype(bf16)
-        got = nn(k_l, jnp.concatenate([sym, total], axis=1))
-        d_kl = got[:, :128] + RATE * nt(a.qkv[b, 2], total)
+        got = nn(k_l, jnp.concatenate([d_outer, total], axis=1))
+        d_kl = got[:, :128] + nt(k_l, d_outer) + RATE * nt(a.qkv[b, 2], total)
         a.dqkv[b, 1] = (a.dk_a[rows, :] + unit_back(kf, unit_rows(kf)[1], d_kl * live[rows])).astype(bf16)
         a.dqkv[b, 2] = (a.dv_a[rows, :] + RATE * got[:, 128:]).astype(bf16)
     for n, b in enumerate(spots):
@@ -987,6 +987,8 @@
         a.gq_s[n, :, 256:768] = qkv_tile(n, 1 - k, 1, 2).astype(bf16)
     spot = pl.ds(256, 512)
     net.send([(a.gq_s.at[:, :, spot], a.gq_r.at[:, :, spot], sibling)], a.gq_s.at[:, :, spot], r_gkv)
+    for one in ffn:
+        one.step5()
     dn_s = net.group(a.dn_s.at[pl.ds(0, 3)])
 
     def dn_part(zz):
@@ -1011,8 +1013,6 @@
         a.gq_1[n, :, 256:768] = (qkv_tile(n, k, 1, 2) + a.gq_r[n, :, 256:768].astype(f32)).astype(bf16)
     k_w.step1()
     val.step1()
-    for one in ffn:
-        one.step5()
     gain_grad += dn_send(3)
     part, gain = dn_part(z)
     a.nf_own[...] = part
@@ -1045,7 +1045,8 @@
     net.landed(a.out_r, r_out)
     for d in range(3):
         out_sum += a.out_r[d].astype(f32)
-    a.output[...] = out_sum.astype(bf16)
+    a.out_v[...] = out_sum.astype(bf16)
+    done = [net.local(a.out_v, a.output)]
     net.landed(a.sm_x.at[pl.ds(0, 3)], r_sm + 1)
     a.sm_y[y_at] = a.sm_x[0] + a.sm_x[1] + a.sm_x[2] + a.sm_x[3]
     net.send(
@@ -1068,13 +1069,16 @@
     for d in range(3):
         d_n += a.dn_r[d].astype(f32)
     back, _ = norm_back(a.x[...].astype(f32), gain_one, d_n)
-    a.input_grad[...] = a.d_resid[...] + back
+    a.d_resid[...] = a.d_resid[...] + back
+    done.append(net.local(a.d_resid, a.input_grad))
     for one in (q_w, k_w, val, w_out):
         one.step5()
     net.landed(a.sm_z.at[pl.ds(0, 3)], r_sm + 3)
     a.small[32:64, :] = a.sm_z[0] + a.sm_z[1] + a.sm_z[2] + a.sm_z[3]
     for one in (*ffn, w_out, q_w, k_w, val):
         one.step6()
+    for copy in done:
+        copy.wait()
     net.drain()
     assert (net.s, net.r, net.l) == SEMS, (net.s, net.r, net.l)
 
@@ -1160,7 +1164,7 @@
     def space(name):
         return pl.ANY if name in far else pltpu.SMEM if name in scalars else pltpu.VMEM
 
-    near = {"output", "input_grad", "small"}
+    near = {"small"}
     scratch = [pltpu.VMEM(shape, dtype) for shape, dtype in SCRATCH.values()]
     for zdim, block, piece in SHARED.values():
         scratch += shared_shapes(zdim, block, piece)

time: 157 us -> 155 us (0.987)
  Pallas kernels: 156 us -> 154 us
    pallas_call x1, Pallas kernels: 151 us -> 149 us  [shards(): pl.pallas_call(layer_kernel, out_shape=[jax.ShapeDtypeStruct(s, t) for s,...]
where the time goes in v4:
time: 155 us
  Pallas kernels  154 us (99%)
    pallas_call x1, Pallas kernels, shards(): pl.pallas_call(layer_kernel, out_shape=[jax.ShapeDtypeStruct(s, t) for s,...  149 us
    pallas_call x1, Pallas kernels, shards(): pl.pallas_call(finish_kernel, out_shape=[jax.ShapeDtypeStruct(*OUTPUTS[n]...  4.5 us

profile of v4, /device:TPU:0, one launch (start us, length us, event | category | flops | bytes accessed | tf_op | source)
XLA Modules:
  0.0 154.8 jit_solution(12650019056628833277)
XLA Ops:
  0.7 149.5 %layer.1 = (bf16[128,1024]{1,0:T(8,128)(2,1)}, f32[128,1024]{1,0:T(8,128)}, bf16[4,128,768]{2,1,0:T(8,128)(2,1)}, bf16[4,128,768]{2,1,0:T(8,128)(2,1)}, bf16[4,1...) custom-call(bf16[128,1024]{1,0:T(8,128)(2,1)} %bitcast.10, ...), custom_call_target="tpu_custom_call" | custom-call | tf_op jit(solution)/shard_map/layer/pallas_call | solution.py:1173
  150.1 4.5 %finish.1 = (bf16[128,1024]{1,0:T(8,128)(2,1)}, f32[128,1024]{1,0:T(8,128)}, f32[1,128]{1,0:T(1,128)}, f32[128,1024]{1,0:T(8,128)}, f32[128,1024]{1,0:T(8,128)},...) custom-call(bf16[128,1024]{1,0:T(8,128)(2,1)} %get-tuple-element.40., ...), custom_call_target="tpu_custom_call" | custom-call | tf_op jit(solution)/shard_map/finish/pallas_call | solution.py:1189

commit v5 on v4

--- a/solution.py
+++ b/solution.py
@@ -596,15 +596,17 @@
     def whole(ref, e):
         return ref[e].reshape(256, ref.shape[-1])
 
+    def norm_chunk(zz):
+        xf = a.x_all[zz].astype(f32)
+        a.n_all[zz] = (xf * scaled(xf) * gain_one).astype(bf16)
+
+    norm_chunk(z)
+    w_qkv.step3()
     for d in (0, *Z_STEPS):
         zz = z_at(-d)
         if d:
             net.landed(a.x_all.at[0], r_x + d - 1)
-        xf = a.x_all[zz].astype(f32)
-        a.n_all[zz] = (xf * scaled(xf) * gain_one).astype(bf16)
-    w_qkv.step3()
-    for d in (0, *Z_STEPS):
-        zz = z_at(-d)
+            norm_chunk(zz)
         rows = sum(nn(a.n_all[zz, :, ahead(e)], whole(a.w_all, e)) for e in range(4)).astype(bf16)
         for n in range(3):
             a.qkv_s[n, ds(zz, 128), :] = rows[:, 256 * n : 256 * n + 256]

time: 155 us -> 155 us (level)
  no operation moved by 1% of the time
where the time goes in v5:
time: 155 us
  Pallas kernels  154 us (99%)
    pallas_call x1, Pallas kernels, shards(): pl.pallas_call(layer_kernel, out_shape=[jax.ShapeDtypeStruct(s, t) for s,...  149 us
    pallas_call x1, Pallas kernels, shards(): pl.pallas_call(finish_kernel, out_shape=[jax.ShapeDtypeStruct(*OUTPUTS[n]...  4.5 us

profile of v5, /device:TPU:0, one launch (start us, length us, event | category | flops | bytes accessed | tf_op | source)
XLA Modules:
  0.0 154.7 jit_solution(10535116643934020078)
XLA Ops:
  0.7 149.3 %layer.1 = (bf16[128,1024]{1,0:T(8,128)(2,1)}, f32[128,1024]{1,0:T(8,128)}, bf16[4,128,768]{2,1,0:T(8,128)(2,1)}, bf16[4,128,768]{2,1,0:T(8,128)(2,1)}, bf16[4,1...) custom-call(bf16[128,1024]{1,0:T(8,128)(2,1)} %bitcast.10, ...), custom_call_target="tpu_custom_call" | custom-call | tf_op jit(solution)/shard_map/layer/pallas_call | solution.py:1175
  150.0 4.5 %finish.1 = (bf16[128,1024]{1,0:T(8,128)(2,1)}, f32[128,1024]{1,0:T(8,128)}, f32[1,128]{1,0:T(1,128)}, f32[128,1024]{1,0:T(8,128)}, f32[128,1024]{1,0:T(8,128)},...) custom-call(bf16[128,1024]{1,0:T(8,128)(2,1)} %get-tuple-element.40., ...), custom_call_target="tpu_custom_call" | custom-call | tf_op jit(solution)/shard_map/finish/pallas_call | solution.py:1191
